TPU v7x, 512 devices: a whole 4x4x16 slice. The times are simulated.
512 devices in a mesh: section: 32 (over y, z_lo), dp: 16 (over z_hi, x, core).
Axes of the slice: x: 4, y: 4, z: 16 (z_hi: 2, z_lo: 8; z = z_hi * 8 + z_lo), core: 2. Of those that a mesh axis runs over, the one named last changes fastest.
Arguments:
- acts: bfloat16 [32, 2, 1024, 6144], P('section', None, 'dp'), may hold values from -6 to 6
- grads_sent: bfloat16 [32, 2, 1024, 6144], P('section', None, 'dp'), may hold values from -48 to 48
- replicas: bfloat16 [32, 2, 2, 16, 6144], P('section'), may hold values from -4 to 4
- master: float32 [32, 2, 16, 6144], P('section', None, None, 'dp'), may hold values from -1 to 1
- moment: float32 [32, 2, 16, 6144], P('section', None, None, 'dp'), may hold values from -3 to 3
- second: float32 [32, 2, 16, 6144], P('section', None, None, 'dp'), may hold values from 0.05 to 4
Outputs:
- new_master: float32 [32, 2, 16, 6144], P('section', None, None, 'dp')
- new_moment: float32 [32, 2, 16, 6144], P('section', None, None, 'dp')
- new_second: float32 [32, 2, 16, 6144], P('section', None, None, 'dp')
- new_replicas: bfloat16 [32, 2, 2, 16, 6144], P('section')
All inputs are finite; a program needn't handle non-finite values.
Results may differ from a plain program's by a relative error of at most 0.006.
Values may be sent and summed in bfloat16 or wider, within the bound.
No kernel may reach another device: no remote copies, remote signals or barrier semaphores. Data moves between devices by JAX's collectives and lax.ppermute only.
A program may use at most 64 MiB of HBM per device.

v0:
```python
import jax
import jax.numpy as jnp
from jax import lax
from jax.sharding import PartitionSpec as P

D = 6144
FF = 24576


beta_one = 0.9
beta_two = 0.95
adam_eps = 1e-08
learn_rate = 0.05
decay_rate = 0.01
adam_steps = 10.0


def partner(value, axis, distance):
    mask = 2**distance
    pairs = [(source, source ^ mask) for source in range(lax.axis_size(axis))]
    return lax.ppermute(value, axis, pairs)


def sent_to_all(value, axis):
    devices = lax.axis_size(axis)
    return lax.all_to_all(
        jnp.broadcast_to(value[None], (devices, *value.shape)), axis, 0, 0, tiled=True
    )


def laid_out(tiles, dim):
    shape = list(tiles.shape[1:])
    shape[dim] *= tiles.shape[0]
    return jnp.moveaxis(tiles, 0, dim).reshape(shape)


def gathered_copies(value, axis, dim):
    tiles = sent_to_all(value, axis)
    return laid_out(tiles, dim)


def shifted(block, axis, distance):
    devices = range(lax.axis_size(axis))
    route = [((i - distance) % len(devices), i) for i in devices]
    return lax.ppermute(block, axis, route)


def in_blocks(value, dim, devices):
    shape = value.shape
    tiles = value.reshape(*shape[:dim], devices, shape[dim] // devices, *shape[dim + 1 :])
    return jnp.moveaxis(tiles, dim, 0)


def sent_and_summed(value, axis, dim):
    tiles = in_blocks(value, dim, lax.axis_size(axis))
    arrived = lax.all_to_all(tiles, axis, split_axis=0, concat_axis=0, tiled=True)
    return arrived.astype(jnp.float32).sum(axis=0)


def gelu_exact(values):
    return 0.5 * values * (1.0 + lax.erf(values * 0.7071067811865476))


def gelu_slope(values):
    return (
        0.5 * (1.0 + lax.erf(values * 0.7071067811865476))
        + values * jnp.exp(-0.5 * values * values) * 0.3989422804014327
    )


def forward_part(inputs, w_in):
    inv_width = 1.0 / D**0.5
    pre_act = (
        lax.dot_general(inputs, w_in, (((1,), (1,)), ((), ())), preferred_element_type=jnp.float32)
        * inv_width
    )
    activation = gelu_exact(pre_act).astype(jnp.bfloat16)
    return (pre_act, activation)


def upstream_part(upstream, w_out, activation):
    inv_hidden = 1.0 / FF**0.5
    act_grad = (
        lax.dot_general(
            upstream, w_out, (((1,), (1,)), ((), ())), preferred_element_type=jnp.float32
        )
        * inv_hidden
    )
    term_out = (
        lax.dot_general(
            activation, upstream, (((0,), (0,)), ((), ())), preferred_element_type=jnp.float32
        )
        * inv_hidden
    )
    return (act_grad, term_out)


def finish_part(inputs, pre_act, act_grad):
    inv_width = 1.0 / D**0.5
    pre_grad = (act_grad * gelu_slope(pre_act)).astype(jnp.bfloat16)
    return (
        lax.dot_general(
            pre_grad, inputs, (((0,), (0,)), ((), ())), preferred_element_type=jnp.float32
        )
        * inv_width
    )


def mirror_grads_move(payload):
    for bit_place in range(lax.axis_size("section").bit_length() - 1):
        payload = partner(payload.astype(jnp.bfloat16), "section", bit_place).astype(payload.dtype)
    return payload


def mirror_params_move(payload):
    for bit_place in range(lax.axis_size("section").bit_length() - 1):
        payload = partner(payload, "section", bit_place)
    return payload


def collect_columns(payload):
    return gathered_copies(payload, "dp", 3)


def body(acts, grads_sent, replicas, master, moment, second):
    sections = lax.axis_size("section")
    worker = lax.axis_index("section")
    upper_half = worker >= sections // 2
    pre_down, act_down = forward_part(acts[0, 0], replicas[0, 0, 0])
    pre_up, act_up = forward_part(acts[0, 1], replicas[0, 1, 0])
    from_after = shifted(grads_sent[:, 0], "section", -1)
    from_before = shifted(grads_sent[:, 1], "section", 1)
    down_grad, down_out = upstream_part(from_after[0], replicas[0, 0, 1], act_down)
    up_grad, up_out = upstream_part(from_before[0], replicas[0, 1, 1], act_up)
    down_terms = jnp.stack([finish_part(acts[0, 0], pre_down, down_grad), down_out])
    up_terms = jnp.stack([finish_part(acts[0, 1], pre_up, up_grad), up_out])
    partials = jnp.stack([down_terms, up_terms])
    own_part = jnp.where(upper_half, partials[:, 1], partials[:, 0])
    other_part = jnp.where(upper_half, partials[:, 0], partials[:, 1])
    arrived = mirror_grads_move(other_part)
    paired = own_part + arrived[::-1]
    summed_grads = sent_and_summed(paired.astype(jnp.bfloat16), "dp", 2)
    moment_now = beta_one * moment[0] + (1.0 - beta_one) * summed_grads
    second_now = beta_two * second[0] + (1.0 - beta_two) * summed_grads * summed_grads
    corrected = (
        moment_now
        / (1.0 - beta_one**adam_steps)
        / (jnp.sqrt(second_now / (1.0 - beta_two**adam_steps)) + adam_eps)
    )
    master_now = master[0] - learn_rate * (corrected + decay_rate * master[0])
    rounded = master_now.astype(jnp.bfloat16)
    complete = collect_columns(rounded[None])[0]
    from_mirror = mirror_params_move(complete)
    other_full = from_mirror[::-1]
    proj_in = jnp.where(upper_half, other_full, complete)
    proj_out = jnp.where(upper_half, complete, other_full)
    new_replicas = jnp.stack([proj_in, proj_out], axis=1)[None]
    return (master_now[None], moment_now[None], second_now[None], new_replicas)


def solution(mesh):
    in_specs = (
        P("section", None, "dp", None),
        P("section", None, "dp", None),
        P("section", None, None, None, None),
        P("section", None, None, "dp"),
        P("section", None, None, "dp"),
        P("section", None, None, "dp"),
    )
    out_specs = (
        P("section", None, None, "dp"),
        P("section", None, None, "dp"),
        P("section", None, None, "dp"),
        P("section", None, None, None, None),
    )
    return jax.shard_map(body, mesh=mesh, in_specs=in_specs, out_specs=out_specs, check_vma=False)
```

profile of v0, /device:TPU:2, one launch (start us, length us, event | category | flops | bytes accessed | tf_op | source)
XLA Modules:
  0.0 314.7 jit_solution(15465242633165227888)
XLA Ops:
  0.6 2.8 slice_bitcast_fusion.1
  3.4 15.6 %collective-permute-start = (bf16[1,64,6144]{2,1,0:T(8,128)(2,1)}, bf16[1,64,6144]{2,1,0:T(8,128)(2,1)S(1)}, u32[]{:S(2)}, u32[]{:S(2)}) collective-permute-start(bf16[1,64,6144]{2,1,0:T(8,128)(2,1)} %get-tuple-element.11), channel_id=1, source_target_pairs={{16,0},{32,16},{48,32},{64,48},{80,64},{96,80},{112,96},{128,112},... | collective-permute-start | bytes 2359304 | tf_op jit(solution)/shard_map/ppermute | solution.py:45
  19.0 1.9 collective-permute-start.1
  21.0 1.2 fusion.13
  22.2 1.2 fusion.19
  23.5 13.8 %collective-permute-done = bf16[1,64,6144]{2,1,0:T(8,128)(2,1)S(1)} collective-permute-done((bf16[1,64,6144]{2,1,0:T(8,128)(2,1)}, bf16[1,64,6144]{2,1,0:T(8,128)(2,1)S(1)}, u32[]{:S(2)}, u32[]{:S(2)}) %collective-permute-start) | collective-permute-done | bytes 786464 | tf_op jit(solution)/shard_map/ppermute | solution.py:45
  37.3 1.7 fusion.3
  38.9 0.2 fusion.2
  39.2 0.1 maximum_bitcast_fusion
  39.3 14.4 %collective-permute-done.1 = bf16[1,64,6144]{2,1,0:T(8,128)(2,1)S(1)} collective-permute-done((bf16[1,64,6144]{2,1,0:T(8,128)(2,1)}, bf16[1,64,6144]{2,1,0:T(8,128)(2,1)S(1)}, u32[]{:S(2)}, u32[]{:S(2)}) %collective-permute-start.1) | collective-permute-done | bytes 786464 | tf_op jit(solution)/shard_map/ppermute | solution.py:45
  53.6 0.2 fusion
  53.9 2.4 fusion.1
  56.3 1.0 maximum_bitcast_fusion.1
  57.3 0.1 fusion.28
  57.4 3.7 %collective-permute-start.2 = (bf16[2,16,6144]{2,1,0:T(8,128)(2,1)S(1)}, bf16[2,16,6144]{2,1,0:T(8,128)(2,1)S(1)}, u32[]{:S(2)}, u32[]{:S(2)}) collective-permute-start(bf16[2,16,6144]{2,1,0:T(8,128)(2,1)S(1)} %fusion.28), channel_id=1, source_target_pairs={{0,16},{16,0},{32,48},{48,32},{64,80},{80,64},{96,112},{112,96},{1... | collective-permute-start | bytes 1179656 | tf_op jit(solution)/shard_map/ppermute | solution.py:21
  61.1 8.4 %collective-permute-done.2 = bf16[2,16,6144]{2,1,0:T(8,128)(2,1)S(1)} collective-permute-done((bf16[2,16,6144]{2,1,0:T(8,128)(2,1)S(1)}, bf16[2,16,6144]{2,1,0:T(8,128)(2,1)S(1)}, u32[]{:S(2)}, u32[]{:S(2)}) %collective-permute-start.2) | collective-permute-done | bytes 393248 | tf_op jit(solution)/shard_map/ppermute | solution.py:21
  69.5 1.9 collective-permute-start.3
  71.4 18.6 %collective-permute-done.3 = bf16[2,16,6144]{2,1,0:T(8,128)(2,1)S(1)} collective-permute-done((bf16[2,16,6144]{2,1,0:T(8,128)(2,1)S(1)}, bf16[2,16,6144]{2,1,0:T(8,128)(2,1)S(1)}, u32[]{:S(2)}, u32[]{:S(2)}) %collective-permute-start.3) | collective-permute-done | bytes 393248 | tf_op jit(solution)/shard_map/ppermute | solution.py:21
  90.0 1.9 collective-permute-start.4
  91.9 38.0 %collective-permute-done.4 = bf16[2,16,6144]{2,1,0:T(8,128)(2,1)S(1)} collective-permute-done((bf16[2,16,6144]{2,1,0:T(8,128)(2,1)S(1)}, bf16[2,16,6144]{2,1,0:T(8,128)(2,1)S(1)}, u32[]{:S(2)}, u32[]{:S(2)}) %collective-permute-start.4) | collective-permute-done | bytes 393248 | tf_op jit(solution)/shard_map/ppermute | solution.py:21
  129.9 1.9 collective-permute-start.5
  131.8 11.0 %collective-permute-done.5 = bf16[2,16,6144]{2,1,0:T(8,128)(2,1)S(1)} collective-permute-done((bf16[2,16,6144]{2,1,0:T(8,128)(2,1)S(1)}, bf16[2,16,6144]{2,1,0:T(8,128)(2,1)S(1)}, u32[]{:S(2)}, u32[]{:S(2)}) %collective-permute-start.5) | collective-permute-done | bytes 393248 | tf_op jit(solution)/shard_map/ppermute | solution.py:21
  142.8 2.5 collective-permute-start.6
  145.3 11.0 %collective-permute-done.6 = bf16[2,16,6144]{2,1,0:T(8,128)(2,1)S(1)} collective-permute-done((bf16[2,16,6144]{2,1,0:T(8,128)(2,1)S(1)}, bf16[2,16,6144]{2,1,0:T(8,128)(2,1)S(1)}, u32[]{:S(2)}, u32[]{:S(2)}) %collective-permute-start.6) | collective-permute-done | bytes 393248 | tf_op jit(solution)/shard_map/ppermute | solution.py:21
  156.4 0.1 convert_element_type.48
  156.4 0.1 fusion.11
  156.5 0.0 copy-start.2
  156.6 0.0 copy-start.3
  156.6 25.2 %all_to_all.10 = bf16[16,2,16,384]{3,2,1,0:T(8,128)(2,1)S(1)} all-to-all(bf16[16,2,16,384]{3,2,1,0:T(8,128)(2,1)S(1)} %bitcast.120), channel_id=1, replica_groups=mesh['section'=32,'dp'=16] {'dp'}, dimensions={0} | all-to-all | bytes 786432 | tf_op jit(solution)/shard_map/all_to_all | solution.py:56
  181.9 0.1 convert_reduce_fusion
  182.0 0.1 fusion.49
  182.1 30.4 %all_to_all.11 = bf16[16,1,2,16,384]{4,3,2,1,0:T(8,128)(2,1)S(1)} all-to-all(bf16[16,1,2,16,384]{4,3,2,1,0:T(8,128)(2,1)S(1)} %broadcast_in_dim.4), channel_id=1, replica_groups=mesh['section'=32,'dp'=16] {'dp'}, dimensions={0} | all-to-all | bytes 786432 | tf_op jit(solution)/shard_map/all_to_all | solution.py:26
  212.5 0.1 copy.26
  212.6 0.2 squeeze_reshape.3
  212.8 1.9 collective-permute-start.7
  214.8 11.8 %collective-permute-done.7 = bf16[2,16,6144]{2,1,0:T(8,128)(2,1)S(1)} collective-permute-done((bf16[2,16,6144]{2,1,0:T(8,128)(2,1)S(1)}, bf16[2,16,6144]{2,1,0:T(8,128)(2,1)S(1)}, u32[]{:S(2)}, u32[]{:S(2)}) %collective-permute-start.7) | collective-permute-done | bytes 393248 | tf_op jit(solution)/shard_map/ppermute | solution.py:21
  226.5 1.9 collective-permute-start.8
  228.4 20.0 %collective-permute-done.8 = bf16[2,16,6144]{2,1,0:T(8,128)(2,1)S(1)} collective-permute-done((bf16[2,16,6144]{2,1,0:T(8,128)(2,1)S(1)}, bf16[2,16,6144]{2,1,0:T(8,128)(2,1)S(1)}, u32[]{:S(2)}, u32[]{:S(2)}) %collective-permute-start.8) | collective-permute-done | bytes 393248 | tf_op jit(solution)/shard_map/ppermute | solution.py:21
  248.4 2.7 collective-permute-start.9
  251.1 35.9 %collective-permute-done.9 = bf16[2,16,6144]{2,1,0:T(8,128)(2,1)S(1)} collective-permute-done((bf16[2,16,6144]{2,1,0:T(8,128)(2,1)S(1)}, bf16[2,16,6144]{2,1,0:T(8,128)(2,1)S(1)}, u32[]{:S(2)}, u32[]{:S(2)}) %collective-permute-start.9) | collective-permute-done | bytes 393248 | tf_op jit(solution)/shard_map/ppermute | solution.py:21
  287.0 3.3 %collective-permute-start.10 = (bf16[2,16,6144]{2,1,0:T(8,128)(2,1)S(1)}, bf16[2,16,6144]{2,1,0:T(8,128)(2,1)S(1)}, u32[]{:S(2)}, u32[]{:S(2)}) collective-permute-start(bf16[2,16,6144]{2,1,0:T(8,128)(2,1)S(1)} %collective-permute-done.9), channel_id=1, source_target_pairs={{0,128},{16,144},{32,160},{48,176},{64,192},{80,208},{96,224},{112... | collective-permute-start | bytes 1179656 | tf_op jit(solution)/shard_map/ppermute | solution.py:21
  290.3 9.6 %collective-permute-done.10 = bf16[2,16,6144]{2,1,0:T(8,128)(2,1)S(1)} collective-permute-done((bf16[2,16,6144]{2,1,0:T(8,128)(2,1)S(1)}, bf16[2,16,6144]{2,1,0:T(8,128)(2,1)S(1)}, u32[]{:S(2)}, u32[]{:S(2)}) %collective-permute-start.10) | collective-permute-done | bytes 393248 | tf_op jit(solution)/shard_map/ppermute | solution.py:21
  300.0 4.9 %collective-permute-start.11 = (bf16[2,16,6144]{2,1,0:T(8,128)(2,1)S(1)}, bf16[2,16,6144]{2,1,0:T(8,128)(2,1)S(1)}, u32[]{:S(2)}, u32[]{:S(2)}) collective-permute-start(bf16[2,16,6144]{2,1,0:T(8,128)(2,1)S(1)} %collective-permute-done.10), channel_id=1, source_target_pairs={{0,256},{16,272},{32,288},{48,304},{64,320},{80,336},{96,352},{112... | collective-permute-start | bytes 1179656 | tf_op jit(solution)/shard_map/ppermute | solution.py:21
  304.9 0.7 multiply_subtract_fusion
  305.6 8.0 %collective-permute-done.11 = bf16[2,16,6144]{2,1,0:T(8,128)(2,1)S(1)} collective-permute-done((bf16[2,16,6144]{2,1,0:T(8,128)(2,1)S(1)}, bf16[2,16,6144]{2,1,0:T(8,128)(2,1)S(1)}, u32[]{:S(2)}, u32[]{:S(2)}) %collective-permute-start.11) | collective-permute-done | bytes 393248 | tf_op jit(solution)/shard_map/ppermute | solution.py:21
  313.5 0.1 select_bitcast_fusion.1
  313.7 0.1 maximum_bitcast_fusion.2
  313.8 0.9 copy.27
  (8 shorter events, 0.1 us)
Async XLA Ops:
  0.6 20.3 %copy-start = (bf16[1,2,64,6144]{3,2,1,0:T(8,128)(2,1)S(1)}, bf16[1,2,64,6144]{3,2,1,0:T(8,128)(2,1)}, u32[]{:S(2)}) copy-start(bf16[1,2,64,6144]{3,2,1,0:T(8,128)(2,1)} %param.6) | copy-start | bytes 4718596
  3.4 33.8 %collective-permute-start = (bf16[1,64,6144]{2,1,0:T(8,128)(2,1)}, bf16[1,64,6144]{2,1,0:T(8,128)(2,1)S(1)}, u32[]{:S(2)}, u32[]{:S(2)}) collective-permute-start(bf16[1,64,6144]{2,1,0:T(8,128)(2,1)} %get-tuple-element.11), channel_id=1, source_target_pairs={{16,0},{32,16},{48,32},{64,48},{80,64},{96,80},{112,96},{128,112},... | collective-permute-start | bytes 2359304 | tf_op jit(solution)/shard_map/ppermute | solution.py:45
  19.0 34.6 %collective-permute-start.1 = (bf16[1,64,6144]{2,1,0:T(8,128)(2,1)}, bf16[1,64,6144]{2,1,0:T(8,128)(2,1)S(1)}, u32[]{:S(2)}, u32[]{:S(2)}) collective-permute-start(bf16[1,64,6144]{2,1,0:T(8,128)(2,1)} %get-tuple-element.12), channel_id=1, source_target_pairs={{496,0},{0,16},{16,32},{32,48},{48,64},{64,80},{80,96},{96,112},{1... | collective-permute-start | bytes 2359304 | tf_op jit(solution)/shard_map/ppermute | solution.py:45
  57.4 12.1 %collective-permute-start.2 = (bf16[2,16,6144]{2,1,0:T(8,128)(2,1)S(1)}, bf16[2,16,6144]{2,1,0:T(8,128)(2,1)S(1)}, u32[]{:S(2)}, u32[]{:S(2)}) collective-permute-start(bf16[2,16,6144]{2,1,0:T(8,128)(2,1)S(1)} %fusion.28), channel_id=1, source_target_pairs={{0,16},{16,0},{32,48},{48,32},{64,80},{80,64},{96,112},{112,96},{1... | collective-permute-start | bytes 1179656 | tf_op jit(solution)/shard_map/ppermute | solution.py:21
  69.5 20.5 %collective-permute-start.3 = (bf16[2,16,6144]{2,1,0:T(8,128)(2,1)S(1)}, bf16[2,16,6144]{2,1,0:T(8,128)(2,1)S(1)}, u32[]{:S(2)}, u32[]{:S(2)}) collective-permute-start(bf16[2,16,6144]{2,1,0:T(8,128)(2,1)S(1)} %collective-permute-done.2), channel_id=1, source_target_pairs={{0,32},{16,48},{32,0},{48,16},{64,96},{80,112},{96,64},{112,80},{1... | collective-permute-start | bytes 1179656 | tf_op jit(solution)/shard_map/ppermute | solution.py:21
  90.0 39.9 %collective-permute-start.4 = (bf16[2,16,6144]{2,1,0:T(8,128)(2,1)S(1)}, bf16[2,16,6144]{2,1,0:T(8,128)(2,1)S(1)}, u32[]{:S(2)}, u32[]{:S(2)}) collective-permute-start(bf16[2,16,6144]{2,1,0:T(8,128)(2,1)S(1)} %collective-permute-done.3), channel_id=1, source_target_pairs={{0,64},{16,80},{32,96},{48,112},{64,0},{80,16},{96,32},{112,48},{1... | collective-permute-start | bytes 1179656 | tf_op jit(solution)/shard_map/ppermute | solution.py:21
  129.9 12.9 %collective-permute-start.5 = (bf16[2,16,6144]{2,1,0:T(8,128)(2,1)S(1)}, bf16[2,16,6144]{2,1,0:T(8,128)(2,1)S(1)}, u32[]{:S(2)}, u32[]{:S(2)}) collective-permute-start(bf16[2,16,6144]{2,1,0:T(8,128)(2,1)S(1)} %collective-permute-done.4), channel_id=1, source_target_pairs={{0,128},{16,144},{32,160},{48,176},{64,192},{80,208},{96,224},{112... | collective-permute-start | bytes 1179656 | tf_op jit(solution)/shard_map/ppermute | solution.py:21
  142.8 13.6 %collective-permute-start.6 = (bf16[2,16,6144]{2,1,0:T(8,128)(2,1)S(1)}, bf16[2,16,6144]{2,1,0:T(8,128)(2,1)S(1)}, u32[]{:S(2)}, u32[]{:S(2)}) collective-permute-start(bf16[2,16,6144]{2,1,0:T(8,128)(2,1)S(1)} %collective-permute-done.5), channel_id=1, source_target_pairs={{0,256},{16,272},{32,288},{48,304},{64,320},{80,336},{96,352},{112... | collective-permute-start | bytes 1179656 | tf_op jit(solution)/shard_map/ppermute | solution.py:21
  156.5 25.4 %copy-start.1 = (f32[1,2,16,384]{3,2,1,0:T(8,128)S(1)}, f32[1,2,16,384]{3,2,1,0:T(8,128)}, u32[]{:S(2)}) copy-start(f32[1,2,16,384]{3,2,1,0:T(8,128)} %param.9) | copy-start | bytes 147460
  156.5 25.4 %copy-start.2 = (f32[1,2,16,384]{3,2,1,0:T(8,128)S(1)}, f32[1,2,16,384]{3,2,1,0:T(8,128)}, u32[]{:S(2)}) copy-start(f32[1,2,16,384]{3,2,1,0:T(8,128)} %param.10) | copy-start | bytes 147460
  156.6 25.4 %copy-start.3 = (f32[1,2,16,384]{3,2,1,0:T(8,128)S(1)}, f32[1,2,16,384]{3,2,1,0:T(8,128)}, u32[]{:S(2)}) copy-start(f32[1,2,16,384]{3,2,1,0:T(8,128)} %param.11) | copy-start | bytes 147460
  212.8 13.7 %collective-permute-start.7 = (bf16[2,16,6144]{2,1,0:T(8,128)(2,1)S(1)}, bf16[2,16,6144]{2,1,0:T(8,128)(2,1)S(1)}, u32[]{:S(2)}, u32[]{:S(2)}) collective-permute-start(bf16[2,16,6144]{2,1,0:T(8,128)(2,1)S(1)} %squeeze_reshape.3), channel_id=1, source_target_pairs={{0,16},{16,0},{32,48},{48,32},{64,80},{80,64},{96,112},{112,96},{1... | collective-permute-start | bytes 1179656 | tf_op jit(solution)/shard_map/ppermute | solution.py:21
  226.5 21.9 %collective-permute-start.8 = (bf16[2,16,6144]{2,1,0:T(8,128)(2,1)S(1)}, bf16[2,16,6144]{2,1,0:T(8,128)(2,1)S(1)}, u32[]{:S(2)}, u32[]{:S(2)}) collective-permute-start(bf16[2,16,6144]{2,1,0:T(8,128)(2,1)S(1)} %collective-permute-done.7), channel_id=1, source_target_pairs={{0,32},{16,48},{32,0},{48,16},{64,96},{80,112},{96,64},{112,80},{1... | collective-permute-start | bytes 1179656 | tf_op jit(solution)/shard_map/ppermute | solution.py:21
  248.4 38.6 %collective-permute-start.9 = (bf16[2,16,6144]{2,1,0:T(8,128)(2,1)S(1)}, bf16[2,16,6144]{2,1,0:T(8,128)(2,1)S(1)}, u32[]{:S(2)}, u32[]{:S(2)}) collective-permute-start(bf16[2,16,6144]{2,1,0:T(8,128)(2,1)S(1)} %collective-permute-done.8), channel_id=1, source_target_pairs={{0,64},{16,80},{32,96},{48,112},{64,0},{80,16},{96,32},{112,48},{1... | collective-permute-start | bytes 1179656 | tf_op jit(solution)/shard_map/ppermute | solution.py:21
  287.0 12.9 %collective-permute-start.10 = (bf16[2,16,6144]{2,1,0:T(8,128)(2,1)S(1)}, bf16[2,16,6144]{2,1,0:T(8,128)(2,1)S(1)}, u32[]{:S(2)}, u32[]{:S(2)}) collective-permute-start(bf16[2,16,6144]{2,1,0:T(8,128)(2,1)S(1)} %collective-permute-done.9), channel_id=1, source_target_pairs={{0,128},{16,144},{32,160},{48,176},{64,192},{80,208},{96,224},{112... | collective-permute-start | bytes 1179656 | tf_op jit(solution)/shard_map/ppermute | solution.py:21
  300.0 13.6 %collective-permute-start.11 = (bf16[2,16,6144]{2,1,0:T(8,128)(2,1)S(1)}, bf16[2,16,6144]{2,1,0:T(8,128)(2,1)S(1)}, u32[]{:S(2)}, u32[]{:S(2)}) collective-permute-start(bf16[2,16,6144]{2,1,0:T(8,128)(2,1)S(1)} %collective-permute-done.10), channel_id=1, source_target_pairs={{0,256},{16,272},{32,288},{48,304},{64,320},{80,336},{96,352},{112... | collective-permute-start | bytes 1179656 | tf_op jit(solution)/shard_map/ppermute | solution.py:21
where the time goes:
time: 315 us
  waiting for transfers between devices  200 us (63%)
  blocking collectives  55.7 us (18%)
  starting transfers between devices  44.2 us (14%)
  matrix products  7.01 us (2%)
  local copies, waits for them, and re-layouts  4.13 us (1%)
    ppermute x10, waiting for transfers between devices, partner(): return lax.ppermute(value, axis, pairs)  172 us
    all_to_all x1, blocking collectives, sent_to_all(): lax.all_to_all(jnp.broadcast_to(value[None], (devices, *value.shape)), ax...  30.4 us
    ppermute x2, waiting for transfers between devices, shifted(): return lax.ppermute(block, axis, route)  28.2 us
    ppermute x10, starting transfers between devices, partner(): return lax.ppermute(value, axis, pairs)  26.7 us
    all_to_all x1, blocking collectives, sent_and_summed(): lax.all_to_all(tiles, axis, split_axis=0, concat_axis=0, tiled=True)  25.2 us
    ppermute x2, starting transfers between devices, shifted(): return lax.ppermute(block, axis, route)  17.5 us
  transfers between devices with their start and end apart: 12, of which 12 were waited for; matrix products, arithmetic and copies ran while one was open for 2% of the time, Pallas kernels for 0%

commit v1 on v0

v1 whole, which is shorter than its diff:
```python
import jax
import jax.numpy as jnp
from jax import lax
from jax.sharding import Mesh, PartitionSpec as P

D = 6144
FF = 24576

beta_one = 0.9
beta_two = 0.95
adam_eps = 1e-08
learn_rate = 0.05
decay_rate = 0.01
adam_steps = 10.0

SECTION = ("y", "zl")
DP = ("zh", "x", "c")
NEAR = ("x", "c")
FAR = ("y", "zl", "zh")


def far_groups():
    groups = []
    for low in range(16):
        groups.append([w * 2 + zh for w in (low, 31 - low) for zh in range(2)])
    return groups


def shifted(block, distance):
    route = [((i - distance) % 32, i) for i in range(32)]
    return lax.ppermute(block, SECTION, route)


def gelu_exact(values):
    return 0.5 * values * (1.0 + lax.erf(values * 0.7071067811865476))


def gelu_slope(values):
    return (
        0.5 * (1.0 + lax.erf(values * 0.7071067811865476))
        + values * jnp.exp(-0.5 * values * values) * 0.3989422804014327
    )


def dot(a, b, ca, cb):
    return lax.dot_general(a, b, (((ca,), (cb,)), ((), ())), preferred_element_type=jnp.float32)


def terms_of(inputs, upstream, w_in, w_out):
    inv_width = 1.0 / D**0.5
    inv_hidden = 1.0 / FF**0.5
    pre_act = dot(w_in, inputs, 1, 1) * inv_width
    activation = gelu_exact(pre_act).astype(jnp.bfloat16)
    act_grad = dot(w_out, upstream, 1, 1) * inv_hidden
    pre_grad = (act_grad * gelu_slope(pre_act)).astype(jnp.bfloat16)
    term_in = dot(pre_grad, inputs, 1, 0) * inv_width
    term_out = dot(activation, upstream, 1, 0) * inv_hidden
    return jnp.stack([term_in, term_out])


def body(acts, grads_sent, replicas, master, moment, second):
    upper = lax.axis_index("y") >= 2
    from_after = shifted(grads_sent[0, 0], -1)
    from_before = shifted(grads_sent[0, 1], 1)
    down = terms_of(acts[0, 0], from_after, replicas[0, 0, 0], replicas[0, 0, 1])
    up = terms_of(acts[0, 1], from_before, replicas[0, 1, 0], replicas[0, 1, 1])
    pair = jnp.stack(
        [jnp.where(upper, up, down), jnp.where(upper, down, up)], axis=1
    ).astype(jnp.bfloat16)
    tiles = pair.reshape(2, 2, 16, 2, 8, 384).transpose(4, 0, 3, 1, 2, 5)
    near = lax.all_to_all(tiles, NEAR, 0, 0, tiled=True)
    near = near.astype(jnp.float32).sum(axis=0).astype(jnp.bfloat16)
    far = lax.all_to_all(
        near.reshape(4, 2, 16, 384), FAR, 0, 0, axis_index_groups=far_groups(), tiled=True
    )
    summed = far.astype(jnp.float32).sum(axis=0)
    grads = jnp.where(upper, summed[::-1], summed)
    moment_now = beta_one * moment[0] + (1.0 - beta_one) * grads
    second_now = beta_two * second[0] + (1.0 - beta_two) * grads * grads
    corrected = (
        moment_now
        / (1.0 - beta_one**adam_steps)
        / (jnp.sqrt(second_now / (1.0 - beta_two**adam_steps)) + adam_eps)
    )
    master_now = master[0] - learn_rate * (corrected + decay_rate * master[0])
    rounded = master_now.astype(jnp.bfloat16)
    rounded = jnp.where(upper, rounded[::-1], rounded)
    shared = lax.all_to_all(
        jnp.broadcast_to(rounded[None], (4, 2, 16, 384)),
        FAR, 0, 0, axis_index_groups=far_groups(), tiled=True,
    )
    full = lax.all_gather(shared, NEAR, axis=0, tiled=False)
    full = full.reshape(8, 2, 2, 2, 16, 384).transpose(3, 1, 4, 2, 0, 5).reshape(2, 2, 16, D)
    new_replicas = jnp.where(upper, full[::-1], full)
    return (master_now[None], moment_now[None], second_now[None], new_replicas[None])


def solution(mesh):
    fine = Mesh(mesh.devices.reshape(4, 8, 2, 4, 2), ("y", "zl", "zh", "x", "c"))
    in_specs = (
        P(SECTION, None, DP, None),
        P(SECTION, None, DP, None),
        P(SECTION, None, None, None, None),
        P(SECTION, None, None, DP),
        P(SECTION, None, None, DP),
        P(SECTION, None, None, DP),
    )
    out_specs = (
        P(SECTION, None, None, DP),
        P(SECTION, None, None, DP),
        P(SECTION, None, None, DP),
        P(SECTION, None, None, None, None),
    )
    return jax.shard_map(body, mesh=fine, in_specs=in_specs, out_specs=out_specs, check_vma=False)
```

time: 315 us -> 134 us (0.43)
  the two profiles are of different devices: /device:TPU:2 before, /device:TPU:1 now
where the time goes in v1:
time: 134 us
  blocking collectives  72.5 us (54%)
  waiting for transfers between devices  29.5 us (22%)
  starting transfers between devices  18.1 us (14%)
  local copies, waits for them, and re-layouts  4.5 us (3%)
  matrix products  4.42 us (3%)
  other arithmetic  3.69 us (3%)
    ppermute x2, waiting for transfers between devices, shifted(): return lax.ppermute(block, SECTION, route)  29.5 us
    all_to_all x1, blocking collectives, body(): lax.all_to_all(near.reshape(4, 2, 16, 384), FAR, 0, 0, axis_index_groups=...  19.7 us
    all_gather x1, blocking collectives, body(): full = lax.all_gather(shared, NEAR, axis=0, tiled=False)  19 us
    ppermute x2, starting transfers between devices, shifted(): return lax.ppermute(block, SECTION, route)  18.1 us
    all_to_all x1, blocking collectives, body(): near = lax.all_to_all(tiles, NEAR, 0, 0, tiled=True)  17.8 us
    all_to_all x1, blocking collectives, body(): lax.all_to_all(jnp.broadcast_to(rounded[None], (4, 2, 16, 384)), FAR, 0,...  16.1 us
    dot_general x6, matrix products, dot(): lax.dot_general(a, b, (((ca,), (cb,)), ((), ())), preferred_element_type=...  4.42 us
    squeeze x1, local copies, waits for them, and re-layouts, body(): from_before = shifted(grads_sent[0, 1], 1)  2.82 us
  transfers between devices with their start and end apart: 2, of which 2 were waited for; matrix products, arithmetic and copies ran while one was open for 2% of the time, Pallas kernels for 0%

profile of v1, /device:TPU:1, one launch (start us, length us, event | category | flops | bytes accessed | tf_op | source)
XLA Modules:
  0.0 133.5 jit_solution(4938281191987726043)
XLA Ops:
  0.6 0.0 copy-start
  0.6 0.0 copy-start.1
  0.7 2.8 %slice_bitcast_fusion.1 = (bf16[64,6144]{1,0:T(8,128)(2,1)}, bf16[64,6144]{1,0:T(8,128)(2,1)}) fusion(bf16[1,2,64,6144]{3,2,1,0:T(8,128)(2,1)} %param.7), kind=kLoop, calls=%fused_computation.22 | loop fusion | bytes 3145728 | tf_op jit(solution)/shard_map/squeeze | solution.py:64
  3.5 16.1 %collective-permute-start.1 = (bf16[64,6144]{1,0:T(8,128)(2,1)}, bf16[64,6144]{1,0:T(8,128)(2,1)S(1)}, u32[]{:S(2)}, u32[]{:S(2)}) collective-permute-start(bf16[64,6144]{1,0:T(8,128)(2,1)} %get-tuple-element.7), channel_id=1, source_target_pairs={{16,0},{32,16},{48,32},{64,48},{80,64},{96,80},{112,96},{128,112},... | collective-permute-start | bytes 2359304 | tf_op jit(solution)/shard_map/ppermute | solution.py:31
  19.6 1.9 %collective-permute-start = (bf16[64,6144]{1,0:T(8,128)(2,1)}, bf16[64,6144]{1,0:T(8,128)(2,1)S(1)}, u32[]{:S(2)}, u32[]{:S(2)}) collective-permute-start(bf16[64,6144]{1,0:T(8,128)(2,1)} %get-tuple-element.6), channel_id=1, source_target_pairs={{496,0},{0,16},{16,32},{32,48},{48,64},{64,80},{80,96},{96,112},{1... | collective-permute-start | bytes 2359304 | tf_op jit(solution)/shard_map/ppermute | solution.py:31
  21.6 0.0 copy-done
  21.6 0.0 copy-done.1
  21.6 0.3 fusion.6
  21.9 0.3 fusion.9
  22.2 14.0 %collective-permute-done.1 = bf16[64,6144]{1,0:T(8,128)(2,1)S(1)} collective-permute-done((bf16[64,6144]{1,0:T(8,128)(2,1)}, bf16[64,6144]{1,0:T(8,128)(2,1)S(1)}, u32[]{:S(2)}, u32[]{:S(2)}) %collective-permute-start.1) | collective-permute-done | bytes 786464 | tf_op jit(solution)/shard_map/ppermute | solution.py:31
  36.2 1.7 %convolution_multiply_fusion.1 = bf16[16,6144]{1,0:T(8,128)(2,1)S(1)} fusion(bf16[64,6144]{1,0:T(8,128)(2,1)S(1)} %collective-permute-done.1, bf16[1,2,64,6144]{3,2,1,0:T(8,128)(2,1)S(1)} %copy-done, bf16[1,2,2,16,6144]{4,3,2,1,0:T(8,128)(2,1)} %param.8, f32[16,64]{1,0:T(8,128)S(1)} %fusion.6), kind=kOutput, calls=%fused_computation.1 | convolution fusion | flops 25374720 | bytes 1974272 | tf_op jit(solution)/shard_map/dot_general | solution.py:46
  37.9 0.2 convolution_multiply_fusion
  38.2 0.2 copy_dynamic-update-slice_fusion.1
  38.3 15.5 %collective-permute-done = bf16[64,6144]{1,0:T(8,128)(2,1)S(1)} collective-permute-done((bf16[64,6144]{1,0:T(8,128)(2,1)}, bf16[64,6144]{1,0:T(8,128)(2,1)S(1)}, u32[]{:S(2)}, u32[]{:S(2)}) %collective-permute-start) | collective-permute-done | bytes 786464 | tf_op jit(solution)/shard_map/ppermute | solution.py:31
  53.8 1.7 %convolution_multiply_fusion.3 = bf16[16,6144]{1,0:T(8,128)(2,1)S(1)} fusion(bf16[64,6144]{1,0:T(8,128)(2,1)S(1)} %collective-permute-done, bf16[1,2,64,6144]{3,2,1,0:T(8,128)(2,1)S(1)} %copy-done, bf16[1,2,2,16,6144]{4,3,2,1,0:T(8,128)(2,1)} %param.8, f32[16,64]{1,0:T(8,128)S(1)} %fusion.9), kind=kOutput, calls=%fused_computation.3 | convolution fusion | flops 25374720 | bytes 1974272 | tf_op jit(solution)/shard_map/dot_general | solution.py:46
  55.5 0.2 copy_dynamic-update-slice_fusion.3
  55.7 0.2 convolution_multiply_fusion.2
  55.9 0.4 copy_dynamic-update-slice_fusion
  56.3 0.1 select_convert_fusion.1
  56.4 1.0 maximum_bitcast_fusion
  57.5 0.0 copy-start.2
  57.5 0.0 copy-start.3
  57.5 0.0 copy-start.4
  57.5 17.8 %all_to_all.15 = bf16[8,2,2,2,16,384]{5,2,4,3,1,0:T(2,128)(2,1)S(1)} all-to-all(bf16[8,2,2,2,16,384]{5,2,4,3,1,0:T(2,128)(2,1)S(1)} %maximum_bitcast_fusion), channel_id=1, replica_groups=mesh['y'=4,'zl'=8,'zh'=2,'x'=4,'c'=2] {'x','c'}, dimensions={0} | all-to-all | bytes 1572864 | tf_op jit(solution)/shard_map/all_to_all | solution.py:71
  75.3 0.9 reduce_sum.21
  76.2 19.7 %all_to_all.16 = bf16[4,2,16,384]{3,2,1,0:T(8,128)(2,1)S(1)} all-to-all(bf16[4,2,16,384]{3,2,1,0:T(8,128)(2,1)S(1)} %bitcast.100), channel_id=1, replica_groups={{0,8,496,504},{16,24,480,488},{32,40,464,472},{48,56,448,456},{64,72,43..., dimensions={0} | all-to-all | bytes 196608 | tf_op jit(solution)/shard_map/all_to_all | solution.py:73
  95.9 0.0 copy-done.2
  95.9 0.0 copy-done.3
  95.9 0.0 copy-done.4
  95.9 0.7 fusion.72
  96.6 16.1 %all_to_all.17 = bf16[4,2,16,384]{3,2,1,0:T(8,128)(2,1)S(1)} all-to-all(bf16[4,2,16,384]{3,2,1,0:T(8,128)(2,1)S(1)} %broadcast_in_dim.21), channel_id=1, replica_groups={{0,8,496,504},{16,24,480,488},{32,40,464,472},{48,56,448,456},{64,72,43..., dimensions={0} | all-to-all | bytes 196608 | tf_op jit(solution)/shard_map/all_to_all | solution.py:88
  112.7 19.0 %all-gather = bf16[32,2,16,384]{3,2,1,0:T(8,128)(2,1)S(1)} all-gather(bf16[4,2,16,384]{3,2,1,0:T(8,128)(2,1)S(1)} %all_to_all.17), channel_id=2, replica_groups=mesh['y'=4,'zl'=8,'zh'=2,'x'=4,'c'=2] {'x','c'}, dimensions={0}, use_global_device_ids=true | all-gather | bytes 884736 | tf_op jit(solution)/shard_map/all_gather | solution.py:92
  131.7 0.5 copy.23
  132.1 0.4 reshape.161
  132.5 1.0 fusion.4
  (8 shorter events, 0.2 us)
Async XLA Ops:
  0.6 20.9 %copy-start = (bf16[1,2,64,6144]{3,2,1,0:T(8,128)(2,1)S(1)}, bf16[1,2,64,6144]{3,2,1,0:T(8,128)(2,1)}, u32[]{:S(2)}) copy-start(bf16[1,2,64,6144]{3,2,1,0:T(8,128)(2,1)} %param.6) | copy-start | bytes 4718596
  0.6 20.9 %copy-start.1 = (bf16[1,2,2,16,6144]{4,3,2,1,0:T(8,128)(2,1)S(1)}, bf16[1,2,2,16,6144]{4,3,2,1,0:T(8,128)(2,1)}, u32[]{:S(2)}) copy-start(bf16[1,2,2,16,6144]{4,3,2,1,0:T(8,128)(2,1)} %param.8) | copy-start | bytes 2359300
  3.5 32.7 %collective-permute-start.1 = (bf16[64,6144]{1,0:T(8,128)(2,1)}, bf16[64,6144]{1,0:T(8,128)(2,1)S(1)}, u32[]{:S(2)}, u32[]{:S(2)}) collective-permute-start(bf16[64,6144]{1,0:T(8,128)(2,1)} %get-tuple-element.7), channel_id=1, source_target_pairs={{16,0},{32,16},{48,32},{64,48},{80,64},{96,80},{112,96},{128,112},... | collective-permute-start | bytes 2359304 | tf_op jit(solution)/shard_map/ppermute | solution.py:31
  19.6 34.2 %collective-permute-start = (bf16[64,6144]{1,0:T(8,128)(2,1)}, bf16[64,6144]{1,0:T(8,128)(2,1)S(1)}, u32[]{:S(2)}, u32[]{:S(2)}) collective-permute-start(bf16[64,6144]{1,0:T(8,128)(2,1)} %get-tuple-element.6), channel_id=1, source_target_pairs={{496,0},{0,16},{16,32},{32,48},{48,64},{64,80},{80,96},{96,112},{1... | collective-permute-start | bytes 2359304 | tf_op jit(solution)/shard_map/ppermute | solution.py:31
  57.5 38.4 %copy-start.2 = (f32[1,2,16,384]{3,2,1,0:T(8,128)S(1)}, f32[1,2,16,384]{3,2,1,0:T(8,128)}, u32[]{:S(2)}) copy-start(f32[1,2,16,384]{3,2,1,0:T(8,128)} %param.11) | copy-start | bytes 147460
  57.5 38.4 %copy-start.3 = (f32[1,2,16,384]{3,2,1,0:T(8,128)S(1)}, f32[1,2,16,384]{3,2,1,0:T(8,128)}, u32[]{:S(2)}) copy-start(f32[1,2,16,384]{3,2,1,0:T(8,128)} %param.10) | copy-start | bytes 147460
  57.5 38.4 %copy-start.4 = (f32[1,2,16,384]{3,2,1,0:T(8,128)S(1)}, f32[1,2,16,384]{3,2,1,0:T(8,128)}, u32[]{:S(2)}) copy-start(f32[1,2,16,384]{3,2,1,0:T(8,128)} %param.9) | copy-start | bytes 147460

commit v2 on v1

--- a/solution.py
+++ b/solution.py
@@ -1,6 +1,10 @@
+import functools
+
 import jax
 import jax.numpy as jnp
 from jax import lax
+from jax.experimental import pallas as pl
+from jax.experimental.pallas import tpu as pltpu
 from jax.sharding import Mesh, PartitionSpec as P
 
 D = 6144
@@ -26,9 +30,40 @@
     return groups
 
 
+def far_index(w, zh):
+    return (w % 32) * 2 + zh
+
+
+def wrap_route(flip):
+    route = []
+    for w in range(7, 32, 8):
+        for zh in range(2):
+            left, right = far_index(w, zh), far_index(w + 1, zh ^ flip)
+            route += [(left, right), (right, left)]
+    return route
+
+
 def shifted(block, distance):
-    route = [((i - distance) % 32, i) for i in range(32)]
+    skipped = 7 if distance < 0 else 0
+    route = [((i - distance) % 32, i) for i in range(32) if i % 8 != skipped]
     return lax.ppermute(block, SECTION, route)
+
+
+def take_kernel(c, src, dst, sem):
+    copy = pltpu.make_async_copy(src.at[0, c], dst, sem)
+    copy.start()
+    copy.wait()
+
+
+def take(array, c):
+    shape = array.shape[2:]
+    return pl.pallas_call(
+        functools.partial(take_kernel, c),
+        out_shape=jax.ShapeDtypeStruct(shape, array.dtype),
+        in_specs=[pl.BlockSpec(memory_space=pl.ANY)],
+        out_specs=pl.BlockSpec(memory_space=pl.ANY),
+        scratch_shapes=[pltpu.SemaphoreType.DMA],
+    )(array)
 
 
 def gelu_exact(values):
@@ -46,30 +81,38 @@
     return lax.dot_general(a, b, (((ca,), (cb,)), ((), ())), preferred_element_type=jnp.float32)
 
 
-def terms_of(inputs, upstream, w_in, w_out):
+def body(acts, grads_sent, replicas, master, moment, second):
     inv_width = 1.0 / D**0.5
     inv_hidden = 1.0 / FF**0.5
-    pre_act = dot(w_in, inputs, 1, 1) * inv_width
-    activation = gelu_exact(pre_act).astype(jnp.bfloat16)
-    act_grad = dot(w_out, upstream, 1, 1) * inv_hidden
-    pre_grad = (act_grad * gelu_slope(pre_act)).astype(jnp.bfloat16)
-    term_in = dot(pre_grad, inputs, 1, 0) * inv_width
-    term_out = dot(activation, upstream, 1, 0) * inv_hidden
-    return jnp.stack([term_in, term_out])
-
-
-def body(acts, grads_sent, replicas, master, moment, second):
     upper = lax.axis_index("y") >= 2
-    from_after = shifted(grads_sent[0, 0], -1)
-    from_before = shifted(grads_sent[0, 1], 1)
-    down = terms_of(acts[0, 0], from_after, replicas[0, 0, 0], replicas[0, 0, 1])
-    up = terms_of(acts[0, 1], from_before, replicas[0, 1, 0], replicas[0, 1, 1])
-    pair = jnp.stack(
-        [jnp.where(upper, up, down), jnp.where(upper, down, up)], axis=1
-    ).astype(jnp.bfloat16)
-    tiles = pair.reshape(2, 2, 16, 2, 8, 384).transpose(4, 0, 3, 1, 2, 5)
+    zl = lax.axis_index("zl")
+    left, right = zl == 7, zl == 0
+    w_outs = lax.ppermute(
+        jnp.where(left, replicas[0, 0, 1], replicas[0, 1, 1]), FAR, wrap_route(1)
+    )
+    upstream = [shifted(take(grads_sent, 0), -1), shifted(take(grads_sent, 1), 1)]
+    pre_act = [dot(replicas[0, c, 0], acts[0, c], 1, 1) * inv_width for c in range(2)]
+    held = jnp.where(left, grads_sent[0, 1], grads_sent[0, 0])
+    wrap_grad = dot(w_outs, held, 1, 1) * inv_hidden
+    sent = jnp.concatenate([jnp.where(left, pre_act[0], pre_act[1]), wrap_grad], axis=0)
+    wrapped = lax.ppermute(sent, FAR, wrap_route(0))
+    terms = []
+    for c, wrap in enumerate((left, right)):
+        act_grad = dot(replicas[0, c, 1], upstream[c], 1, 1) * inv_hidden
+        act_grad = jnp.where(wrap, wrapped[16:], act_grad)
+        pre_grad = (act_grad * gelu_slope(pre_act[c])).astype(jnp.bfloat16)
+        activation = gelu_exact(jnp.where(wrap, wrapped[:16], pre_act[c])).astype(jnp.bfloat16)
+        term_in = dot(pre_grad, acts[0, c], 1, 0) * inv_width
+        term_out = dot(activation, jnp.where(wrap, held, upstream[c]), 1, 0) * inv_hidden
+        terms.append(jnp.stack([term_in, term_out]).astype(jnp.bfloat16))
+    tiles = jnp.stack(terms).reshape(2, 2, 16, 2, 8, 384).transpose(4, 0, 1, 3, 2, 5)
     near = lax.all_to_all(tiles, NEAR, 0, 0, tiled=True)
     near = near.astype(jnp.float32).sum(axis=0).astype(jnp.bfloat16)
+    down, up = near[0], near[1]
+    other = lax.ppermute(jnp.where(left, down[1], up[1]), FAR, wrap_route(1))
+    down = jnp.stack([down[0], jnp.where(left, other, down[1])])
+    up = jnp.stack([up[0], jnp.where(right, other, up[1])])
+    near = jnp.stack([jnp.where(upper, up, down), jnp.where(upper, down, up)], axis=2)
     far = lax.all_to_all(
         near.reshape(4, 2, 16, 384), FAR, 0, 0, axis_index_groups=far_groups(), tiled=True
     )

time: 134 us -> 182 us (1.36)
  Pallas kernels: 0 us -> 49.9 us
  blocking collectives: 72.5 us -> 50.2 us
  starting transfers between devices: 18.1 us -> 34.4 us
  matrix products: 4.42 us -> 8.74 us
  local copies, waits for them, and re-layouts: 4.5 us -> 1.69 us
    pallas_call x0 -> x2, Pallas kernels: none -> 49.9 us  [take(): pl.pallas_call(functools.partial(take_kernel, c), out_shape=jax.ShapeDtyp...]
    ppermute x2, waiting for transfers between devices: 29.5 us -> 0.01 us  [shifted(): return lax.ppermute(block, SECTION, route)]
    ppermute x0 -> x3, starting transfers between devices: none -> 21.8 us  [the longest x1 11.3 us: body(): lax.ppermute(jnp.where(left, replicas[0, 0, 1], replicas[0, 1, 1]), FAR,...]
    ppermute x0 -> x3, waiting for transfers between devices: none -> 17.9 us  [the longest x1 10.9 us: body(): wrapped = lax.ppermute(sent, FAR, wrap_route(0))]
    all_to_all x1 -> x0, blocking collectives: 17.8 us -> none  [body(): near = lax.all_to_all(tiles, NEAR, 0, 0, tiled=True)]
    all_to_all x0 -> x1, waiting for transfers between devices: none -> 12.3 us  [body(): near = lax.all_to_all(tiles, NEAR, 0, 0, tiled=True)]
    ppermute x2, starting transfers between devices: 18.1 us -> 5.98 us  [shifted(): return lax.ppermute(block, SECTION, route)]
    all_to_all x0 -> x1, starting transfers between devices: none -> 6.59 us  [body(): near = lax.all_to_all(tiles, NEAR, 0, 0, tiled=True)]
  transfers between devices with their start and end apart: 2 -> 6, of which waited for: 2 -> 3; matrix products, arithmetic and copies ran while one was open for 2% -> 3% of each run, Pallas kernels for 0% -> 14%
where the time goes in v2:
time: 182 us; the launch traced here: 181 us
  blocking collectives  50.2 us (28%)
  Pallas kernels  49.9 us (27%)
  starting transfers between devices  34.4 us (19%)
  waiting for transfers between devices  30.2 us (17%)
  matrix products  8.74 us (5%)
  other arithmetic  5.03 us (3%)
    pallas_call x2, Pallas kernels, take(): pl.pallas_call(functools.partial(take_kernel, c), out_shape=jax.ShapeDtyp...  49.9 us
    all_gather x1, blocking collectives, body(): full = lax.all_gather(shared, NEAR, axis=0, tiled=False)  17.4 us
    all_to_all x1, blocking collectives, body(): lax.all_to_all(near.reshape(4, 2, 16, 384), FAR, 0, 0, axis_index_groups=...  16.6 us
    all_to_all x1, blocking collectives, body(): lax.all_to_all(jnp.broadcast_to(rounded[None], (4, 2, 16, 384)), FAR, 0,...  16.1 us
    all_to_all x1, waiting for transfers between devices, body(): near = lax.all_to_all(tiles, NEAR, 0, 0, tiled=True)  12.3 us
    ppermute x1, starting transfers between devices, body(): lax.ppermute(jnp.where(left, replicas[0, 0, 1], replicas[0, 1, 1]), FAR,...  11.3 us
    ppermute x1, waiting for transfers between devices, body(): wrapped = lax.ppermute(sent, FAR, wrap_route(0))  10.9 us
    dot_general x7, matrix products, dot(): lax.dot_general(a, b, (((ca,), (cb,)), ((), ())), preferred_element_type=...  8.74 us
  transfers between devices with their start and end apart: 6, of which 3 were waited for; matrix products, arithmetic and copies ran while one was open for 3% of the time, Pallas kernels for 14%

profile of v2, /device:TPU:1, one launch (start us, length us, event | category | flops | bytes accessed | tf_op | source)
XLA Modules:
  0.0 181.0 jit_solution(1100644566781093903)
XLA Ops:
  0.6 0.0 copy-start.3
  0.6 24.9 %shard_map.94 = bf16[64,6144]{1,0:T(8,128)(2,1)} custom-call(bf16[1,2,64,6144]{3,2,1,0:T(8,128)(2,1)} %src.3), custom_call_target="tpu_custom_call" | custom-call | tf_op jit(solution)/shard_map/pallas_call | solution.py:60
  25.6 0.0 copy-start
  25.6 4.6 %collective-permute-start.3 = (bf16[64,6144]{1,0:T(8,128)(2,1)}, bf16[64,6144]{1,0:T(8,128)(2,1)S(1)}, u32[]{:S(2)}, u32[]{:S(2)}) collective-permute-start(bf16[64,6144]{1,0:T(8,128)(2,1)} %shard_map.94), channel_id=1, source_target_pairs={{0,16},{16,32},{32,48},{48,64},{64,80},{80,96},{96,112},{128,144},... | collective-permute-start | bytes 2359304 | tf_op jit(solution)/shard_map/ppermute | solution.py:49
  30.2 0.0 copy-done.3
  30.2 11.3 %collective-permute-start = (bf16[16,6144]{1,0:T(8,128)(2,1)S(1)}, bf16[16,6144]{1,0:T(8,128)(2,1)S(1)}, u32[]{:S(2)}, u32[]{:S(2)}) collective-permute-start(bf16[16,6144]{1,0:T(8,128)(2,1)S(1)} %bitcast_select_fusion.4), channel_id=1, source_target_pairs={{112,136},{136,112},{120,128},{128,120},{240,264},{264,240},{248,2... | collective-permute-start | bytes 589832 | tf_op jit(solution)/shard_map/ppermute | solution.py:90
  41.5 24.9 %shard_map.93 = bf16[64,6144]{1,0:T(8,128)(2,1)} custom-call(bf16[1,2,64,6144]{3,2,1,0:T(8,128)(2,1)} %src.3), custom_call_target="tpu_custom_call" | custom-call | tf_op jit(solution)/shard_map/pallas_call | solution.py:60
  66.4 0.0 copy-start.1
  66.4 0.0 copy-start.4
  66.5 1.4 collective-permute-start.2
  67.9 0.0 copy-done
  67.9 0.1 slice_select_fusion
  68.0 0.0 copy-done.1
  68.0 0.0 copy-done.4
  68.0 0.9 fusion.16
  69.0 1.6 multiply_select_fusion
  70.6 0.0 collective-permute-done
  70.6 0.3 convolution_multiply_fusion.6
  70.9 8.6 %collective-permute-start.1 = (f32[32,64]{1,0:T(8,128)S(1)}, f32[32,64]{1,0:T(8,128)S(1)}, u32[]{:S(2)}, u32[]{:S(2)}) collective-permute-start(f32[32,64]{1,0:T(8,128)S(1)} %pad_maximum_fusion.3), channel_id=1, source_target_pairs={{112,128},{128,112},{120,136},{136,120},{240,256},{256,240},{248,2... | collective-permute-start | bytes 24584 | tf_op jit(solution)/shard_map/ppermute | solution.py:98
  79.5 10.9 %collective-permute-done.1 = f32[32,64]{1,0:T(8,128)S(1)} collective-permute-done((f32[32,64]{1,0:T(8,128)S(1)}, f32[32,64]{1,0:T(8,128)S(1)}, u32[]{:S(2)}, u32[]{:S(2)}) %collective-permute-start.1) | collective-permute-done | bytes 8224 | tf_op jit(solution)/shard_map/ppermute | solution.py:98
  90.4 0.0 collective-permute-done.3
  90.4 0.9 fusion.3
  91.4 0.2 copy.29
  91.6 0.0 copy-done.2
  91.6 1.7 fusion.2
  93.3 0.2 copy.28
  93.4 0.0 collective-permute-done.2
  93.4 1.4 fusion.1
  94.9 0.2 copy.27
  95.0 1.9 %fusion = bf16[16,6144]{1,0:T(8,128)(2,1)S(1)} fusion(bf16[64,6144]{1,0:T(8,128)(2,1)} %collective-permute-done.2, bf16[1,2,64,6144]{3,2,1,0:T(8,128)(2,1)S(1)} %copy-done.2, bf16[1,2,2,16,6144]{4,3,2,1,0:T(8,128)(2,1)} %param.8, f32[16,64]{1,0:T(8,128)} %fusion.16, f32[32,64]{1,0:T(8,128)S(1)} %collective-permute-done.1, pred[]{:T(512)S(6)} %eq.6), kind=kOutput, calls=%fused_computation.4 | convolution fusion | flops 25375744 | bytes 1982465 | tf_op jit(solution)/shard_map/dot_general | solution.py:81
  97.0 0.2 copy.26
  97.1 2.1 %maximum_bitcast_fusion = bf16[8,2,2,2,16,384]{5,3,4,2,1,0:T(2,128)(2,1)} fusion(bf16[1,1,16,2,8,384]{5,3,2,1,0,4:T(2,128)(2,1)S(1)} %copy.29, bf16[1,1,16,2,8,384]{5,3,2,1,0,4:T(2,128)(2,1)S(1)} %copy.28, bf16[1,1,16,2,8,384]{5,3,2,1,0,4:T(2,128)(2,1)S(1)} %copy.27, bf16[1,1,16,2,8,384]{5,3,2,1,0,4:T(2,128)(2,1)S(1)} %copy.26), kind=kLoop, calls=%fused_computation.19 | loop fusion | flops 1179648 | bytes 1572864 | tf_op jit(solution)/shard_map/transpose | solution.py:108
  99.2 6.6 %all-to-all-start = ((bf16[8,2,2,2,16,384]{5,3,4,2,1,0:T(2,128)(2,1)}), bf16[8,2,2,2,16,384]{5,3,4,2,1,0:T(2,128)(2,1)S(1)}, u32[]{:S(2)}, u32[]{:S(2)}) async-start(bf16[8,2,2,2,16,384]{5,3,4,2,1,0:T(2,128)(2,1)} %maximum_bitcast_fusion), calls=%async_computation | async-start | bytes 1572864 | tf_op jit(solution)/shard_map/all_to_all | solution.py:109
  105.8 12.3 %all-to-all-done = bf16[8,2,2,2,16,384]{5,3,4,2,1,0:T(2,128)(2,1)S(1)} async-done(((bf16[8,2,2,2,16,384]{5,3,4,2,1,0:T(2,128)(2,1)}), bf16[8,2,2,2,16,384]{5,3,4,2,1,0:T(2,128)(2,1)S(1)}, u32[]{:S(2)}, u32[]{:S(2)}) %all-to-all-start) | async-done | bytes 786464 | tf_op jit(solution)/shard_map/all_to_all | solution.py:109
  118.1 0.9 reduce_sum.21
  119.0 1.9 %collective-permute-start.4 = (bf16[2,16,384]{2,0,1:T(2,128)(2,1)S(1)}, bf16[2,16,384]{2,0,1:T(2,128)(2,1)S(1)}, u32[]{:S(2)}, u32[]{:S(2)}) collective-permute-start(bf16[2,16,384]{2,0,1:T(2,128)(2,1)S(1)} %broadcast_select_fusion.3), channel_id=1, source_target_pairs={{112,136},{136,112},{120,128},{128,120},{240,264},{264,240},{248,2... | collective-permute-start | bytes 73736 | tf_op jit(solution)/shard_map/ppermute | solution.py:112
  121.0 6.9 %collective-permute-done.4 = bf16[2,16,384]{2,0,1:T(2,128)(2,1)S(1)} collective-permute-done((bf16[2,16,384]{2,0,1:T(2,128)(2,1)S(1)}, bf16[2,16,384]{2,0,1:T(2,128)(2,1)S(1)}, u32[]{:S(2)}, u32[]{:S(2)}) %collective-permute-start.4) | collective-permute-done | bytes 24608 | tf_op jit(solution)/shard_map/ppermute | solution.py:112
  128.0 0.2 broadcast_select_fusion.1
  128.2 16.6 %all_to_all.15 = bf16[4,2,16,384]{3,2,1,0:T(8,128)(2,1)S(1)} all-to-all(bf16[4,2,16,384]{3,2,1,0:T(8,128)(2,1)S(1)} %copy.33), channel_id=1, replica_groups={{0,8,496,504},{16,24,480,488},{32,40,464,472},{48,56,448,456},{64,72,43..., dimensions={0} | all-to-all | bytes 196608 | tf_op jit(solution)/shard_map/all_to_all | solution.py:116
  144.9 0.0 copy-done.5
  144.9 0.0 copy-done.6
  144.9 0.0 copy-done.7
  144.9 0.7 fusion.115
  145.6 16.1 %all_to_all.16 = bf16[4,2,16,384]{3,2,1,0:T(8,128)(2,1)S(1)} all-to-all(bf16[4,2,16,384]{3,2,1,0:T(8,128)(2,1)S(1)} %broadcast_in_dim.21), channel_id=1, replica_groups={{0,8,496,504},{16,24,480,488},{32,40,464,472},{48,56,448,456},{64,72,43..., dimensions={0} | all-to-all | bytes 196608 | tf_op jit(solution)/shard_map/all_to_all | solution.py:131
  161.7 17.4 %all-gather = bf16[32,2,16,384]{3,2,1,0:T(8,128)(2,1)S(1)} all-gather(bf16[4,2,16,384]{3,2,1,0:T(8,128)(2,1)S(1)} %all_to_all.16), channel_id=2, replica_groups=mesh['y'=4,'zl'=8,'zh'=2,'x'=4,'c'=2] {'x','c'}, dimensions={0}, use_global_device_ids=true | all-gather | bytes 884736 | tf_op jit(solution)/shard_map/all_gather | solution.py:135
  179.2 0.5 copy.34
  179.6 0.4 reshape.162
  180.0 1.0 fusion.10
  (20 shorter events, 0.3 us)
Async XLA Ops:
  0.6 29.5 %copy-start.3 = (bf16[1,2,2,16,6144]{4,3,2,1,0:T(8,128)(2,1)S(1)}, bf16[1,2,2,16,6144]{4,3,2,1,0:T(8,128)(2,1)}, u32[]{:S(2)}) copy-start(bf16[1,2,2,16,6144]{4,3,2,1,0:T(8,128)(2,1)} %param.8) | copy-start | bytes 2359300
  25.6 42.3 %copy-start = (bf16[1,2,64,6144]{3,2,1,0:T(8,128)(2,1)S(1)}, bf16[1,2,64,6144]{3,2,1,0:T(8,128)(2,1)}, u32[]{:S(2)}) copy-start(bf16[1,2,64,6144]{3,2,1,0:T(8,128)(2,1)} %src.3) | copy-start | bytes 4718596
  25.6 64.8 %collective-permute-start.3 = (bf16[64,6144]{1,0:T(8,128)(2,1)}, bf16[64,6144]{1,0:T(8,128)(2,1)S(1)}, u32[]{:S(2)}, u32[]{:S(2)}) collective-permute-start(bf16[64,6144]{1,0:T(8,128)(2,1)} %shard_map.94), channel_id=1, source_target_pairs={{0,16},{16,32},{32,48},{48,64},{64,80},{80,96},{96,112},{128,144},... | collective-permute-start | bytes 2359304 | tf_op jit(solution)/shard_map/ppermute | solution.py:49
  30.2 40.4 %collective-permute-start = (bf16[16,6144]{1,0:T(8,128)(2,1)S(1)}, bf16[16,6144]{1,0:T(8,128)(2,1)S(1)}, u32[]{:S(2)}, u32[]{:S(2)}) collective-permute-start(bf16[16,6144]{1,0:T(8,128)(2,1)S(1)} %bitcast_select_fusion.4), channel_id=1, source_target_pairs={{112,136},{136,112},{120,128},{128,120},{240,264},{264,240},{248,2... | collective-permute-start | bytes 589832 | tf_op jit(solution)/shard_map/ppermute | solution.py:90
  66.4 1.6 copy-start.1
  66.4 1.6 copy-start.4
  66.5 27.0 %collective-permute-start.2 = (bf16[64,6144]{1,0:T(8,128)(2,1)}, bf16[64,6144]{1,0:T(8,128)(2,1)}, u32[]{:S(2)}, u32[]{:S(2)}) collective-permute-start(bf16[64,6144]{1,0:T(8,128)(2,1)} %shard_map.93), channel_id=1, source_target_pairs={{16,0},{32,16},{48,32},{64,48},{80,64},{96,80},{112,96},{144,128},... | collective-permute-start | bytes 2359304 | tf_op jit(solution)/shard_map/ppermute | solution.py:49
  70.6 21.0 %copy-start.2 = (bf16[1,2,64,6144]{3,2,1,0:T(8,128)(2,1)S(1)}, bf16[1,2,64,6144]{3,2,1,0:T(8,128)(2,1)}, u32[]{:S(2)}) copy-start(bf16[1,2,64,6144]{3,2,1,0:T(8,128)(2,1)} %param.6) | copy-start | bytes 4718596
  70.9 19.5 %collective-permute-start.1 = (f32[32,64]{1,0:T(8,128)S(1)}, f32[32,64]{1,0:T(8,128)S(1)}, u32[]{:S(2)}, u32[]{:S(2)}) collective-permute-start(f32[32,64]{1,0:T(8,128)S(1)} %pad_maximum_fusion.3), channel_id=1, source_target_pairs={{112,128},{128,112},{120,136},{136,120},{240,256},{256,240},{248,2... | collective-permute-start | bytes 24584 | tf_op jit(solution)/shard_map/ppermute | solution.py:98
  99.2 45.7 %copy-start.5 = (f32[1,2,16,384]{3,2,1,0:T(8,128)S(1)}, f32[1,2,16,384]{3,2,1,0:T(8,128)}, u32[]{:S(2)}) copy-start(f32[1,2,16,384]{3,2,1,0:T(8,128)} %param.11) | copy-start | bytes 147460
  99.2 45.7 %copy-start.6 = (f32[1,2,16,384]{3,2,1,0:T(8,128)S(1)}, f32[1,2,16,384]{3,2,1,0:T(8,128)}, u32[]{:S(2)}) copy-start(f32[1,2,16,384]{3,2,1,0:T(8,128)} %param.10) | copy-start | bytes 147460
  99.2 45.7 %copy-start.7 = (f32[1,2,16,384]{3,2,1,0:T(8,128)S(1)}, f32[1,2,16,384]{3,2,1,0:T(8,128)}, u32[]{:S(2)}) copy-start(f32[1,2,16,384]{3,2,1,0:T(8,128)} %param.9) | copy-start | bytes 147460
  99.2 18.9 %all-to-all-start = ((bf16[8,2,2,2,16,384]{5,3,4,2,1,0:T(2,128)(2,1)}), bf16[8,2,2,2,16,384]{5,3,4,2,1,0:T(2,128)(2,1)S(1)}, u32[]{:S(2)}, u32[]{:S(2)}) async-start(bf16[8,2,2,2,16,384]{5,3,4,2,1,0:T(2,128)(2,1)} %maximum_bitcast_fusion), calls=%async_computation | async-start | bytes 1572864 | tf_op jit(solution)/shard_map/all_to_all | solution.py:109
  119.0 8.9 %collective-permute-start.4 = (bf16[2,16,384]{2,0,1:T(2,128)(2,1)S(1)}, bf16[2,16,384]{2,0,1:T(2,128)(2,1)S(1)}, u32[]{:S(2)}, u32[]{:S(2)}) collective-permute-start(bf16[2,16,384]{2,0,1:T(2,128)(2,1)S(1)} %broadcast_select_fusion.3), channel_id=1, source_target_pairs={{112,136},{136,112},{120,128},{128,120},{240,264},{264,240},{248,2... | collective-permute-start | bytes 73736 | tf_op jit(solution)/shard_map/ppermute | solution.py:112

commit v3 on v1

v3 whole, which is shorter than its diff:
```python
import functools

import jax
import jax.numpy as jnp
from jax import lax
from jax.experimental import pallas as pl
from jax.experimental.pallas import tpu as pltpu
from jax.sharding import Mesh, PartitionSpec as P

D = 6144
FF = 24576
UNITS = 16
INV_WIDTH = 1.0 / D**0.5
INV_HIDDEN = 1.0 / FF**0.5

beta_one = 0.9
beta_two = 0.95
adam_eps = 1e-08
learn_rate = 0.05
decay_rate = 0.01
adam_steps = 10.0

SECTION = ("y", "zl")
DP = ("zh", "x", "c")
NEAR = ("x", "c")
FAR = ("y", "zl", "zh")

ANY = pl.BlockSpec(memory_space=pl.ANY)
VMEM = pl.BlockSpec(memory_space=pltpu.VMEM)
BF16 = jnp.bfloat16
F32 = jnp.float32


def far_groups():
    groups = []
    for low in range(16):
        groups.append([w * 2 + zh for w in (low, 31 - low) for zh in range(2)])
    return groups


def wrap_route():
    route = []
    for left in range(7, 32, 8):
        right = (left + 1) % 32
        route += [(left, right), (right, left)]
    return route


def swap_route():
    return [(7, 23), (23, 7), (8, 24), (24, 8)]


def weights_route():
    route = []
    for w, v in wrap_route():
        for zh in range(2):
            route.append((w * 2 + zh, v * 2 + 1 - zh))
    return route


def shifted(block, distance):
    skipped = 7 if distance < 0 else 0
    route = [((i - distance) % 32, i) for i in range(32) if i % 8 != skipped]
    return lax.ppermute(block, SECTION, route)


def swap_cores(block):
    return lax.ppermute(block, "c", [(0, 1), (1, 0)])


def here(array):
    return pltpu.with_memory_space_constraint(array, pltpu.VMEM)


def call(kernel, outs, *args, specs=None, scratch=(), flops=0, moved=0):
    return pl.pallas_call(
        kernel,
        out_shape=[pltpu.VMEM(*out) if isinstance(out, tuple) else out for out in outs],
        in_specs=specs or [VMEM] * len(args),
        out_specs=[VMEM if isinstance(out, tuple) else ANY for out in outs],
        scratch_shapes=list(scratch),
        cost_estimate=pl.CostEstimate(flops=flops, bytes_accessed=moved, transcendentals=0),
        compiler_params=pltpu.CompilerParams(vmem_limit_bytes=32 * 2**20),
    )(*args)


def gelu_exact(values):
    return 0.5 * values * (1.0 + lax.erf(values * 0.7071067811865476))


def gelu_slope(values):
    return (
        0.5 * (1.0 + lax.erf(values * 0.7071067811865476))
        + values * jnp.exp(-0.5 * values * values) * 0.3989422804014327
    )


def dot(a, b, ca, cb):
    return lax.dot_general(a, b, (((ca,), (cb,)), ((), ())), preferred_element_type=F32)


def take_kernel(grads, weights, w_out, down, up, sems):
    side = jnp.where(lax.axis_index("zl") == 7, 0, 1)
    copies = [
        pltpu.make_async_copy(weights.at[0, side, 1], w_out, sems.at[0]),
        pltpu.make_async_copy(grads.at[0, 0], down, sems.at[1]),
        pltpu.make_async_copy(grads.at[0, 1], up, sems.at[2]),
    ]
    for copy in copies:
        copy.start()
    for copy in copies:
        copy.wait()


def forward_kernel(acts, weights, pre_act):
    for c in range(2):
        pre_act[c] = dot(weights[0, c, 0], acts[0, c], 1, 1) * INV_WIDTH


def wrap_kernel(w_out, down, up, pre_act, sent):
    left = lax.axis_index("zl") == 7

    @pl.when(left)
    def _():
        sent[:UNITS] = pre_act[0]
        sent[UNITS:] = dot(w_out[...], up[...], 1, 1) * INV_HIDDEN

    @pl.when(jnp.logical_not(left))
    def _():
        sent[:UNITS] = pre_act[1]
        sent[UNITS:] = dot(w_out[...], down[...], 1, 1) * INV_HIDDEN


def terms_kernel(
    from_after, from_before, wrapped, acts, weights, pre_act, down, up, keep, send, grad, factor
):
    zl = lax.axis_index("zl")
    first = lax.axis_index("c") == 0

    def product(lhs, rhs, scale, row):
        for block in range(8):
            x, zh = block % 4, block // 4
            even = dot(lhs, rhs(block * 768), 1, 0) * scale
            odd = dot(lhs, rhs(block * 768 + 384), 1, 0) * scale
            spot = (x, pl.ds(row, UNITS), pl.ds(zh * 384, 384))
            keep[spot] = jnp.where(first, even, odd)
            send[spot] = jnp.where(first, odd, even).astype(BF16)

    for c in range(2):
        wrap = zl == (7 if c == 0 else 0)
        upstream = from_after if c == 0 else from_before
        own = up if c == 0 else down

        @pl.when(wrap)
        def _():
            grad[...] = wrapped[UNITS:]
            factor[...] = wrapped[:UNITS]

        @pl.when(jnp.logical_not(wrap))
        def _():
            grad[...] = dot(weights[0, c, 1], upstream[...], 1, 1) * INV_HIDDEN
            factor[...] = pre_act[c]

        pre_grad = (grad[...] * gelu_slope(pre_act[c])).astype(BF16)
        activation = gelu_exact(factor[...]).astype(BF16)
        row = c * 2 * UNITS
        product(pre_grad, lambda at: acts[0, c, :, at : at + 384], INV_WIDTH, row)

        @pl.when(wrap)
        def _():
            product(activation, lambda at: own[:, at : at + 384], INV_HIDDEN, row + UNITS)

        @pl.when(jnp.logical_not(wrap))
        def _():
            product(activation, lambda at: upstream[:, at : at + 384], INV_HIDDEN, row + UNITS)


def merge_kernel(keep, arrived, out):
    out[...] = (keep[...] + arrived[...].astype(F32)).astype(BF16)


def near_kernel(arrived, total, swap):
    for row in range(4):
        rows = pl.ds(row * UNITS, UNITS)
        part = arrived[0, rows].astype(F32)
        for x in range(1, 4):
            part += arrived[x, rows].astype(F32)
        total[rows] = part.astype(BF16)
    side = jnp.where(lax.axis_index("zl") == 7, UNITS, 3 * UNITS)
    swap[...] = total[pl.ds(pl.multiple_of(side, UNITS), UNITS)]


def spread_kernel(total, swap, out):
    y, zl = lax.axis_index("y"), lax.axis_index("zl")
    upper = y >= 2
    for zh in range(2):
        columns = slice(zh * 384, zh * 384 + 384)
        for p in range(2):
            parts = []
            for c in range(2):
                part = total[(2 * c + p) * UNITS : (2 * c + p + 1) * UNITS, columns]
                if p == 1:
                    moved = (zl == (7 if c == 0 else 0)) & (y % 2 == c)
                    part = jnp.where(moved, swap[:, columns], part)
                parts.append(part)
            out[2 * p + zh, 0] = jnp.where(upper, parts[1], parts[0])
            out[2 * p + zh, 1] = jnp.where(upper, parts[0], parts[1])


def adam_kernel(arrived, master, moment, second, new_master, new_moment, new_second, shared):
    upper = lax.axis_index("y") >= 2
    sums = []
    for sec in range(2):
        part = arrived[0, sec].astype(F32)
        for i in range(1, 4):
            part += arrived[i, sec].astype(F32)
        sums.append(part)
    rounded = []
    for j in range(2):
        grad = jnp.where(upper, sums[1 - j], sums[j])
        moment_now = beta_one * moment[0, j] + (1.0 - beta_one) * grad
        second_now = beta_two * second[0, j] + (1.0 - beta_two) * grad * grad
        corrected = (
            moment_now
            / (1.0 - beta_one**adam_steps)
            / (jnp.sqrt(second_now / (1.0 - beta_two**adam_steps)) + adam_eps)
        )
        old = master[0, j]
        master_now = old - learn_rate * (corrected + decay_rate * old)
        new_master[0, j] = master_now
        new_moment[0, j] = moment_now
        new_second[0, j] = second_now
        rounded.append(master_now.astype(BF16))
    for sec in range(2):
        part = jnp.where(upper, rounded[1 - sec], rounded[sec])
        for i in range(4):
            shared[i, sec] = part


def finish_kernel(full, out, sem):
    upper = jnp.where(lax.axis_index("y") >= 2, 1, 0)
    copies = []
    for near in range(8):
        for zh in range(2):
            for sec in range(2):
                c = sec + upper - 2 * sec * upper
                at = (zh * 8 + near) * 384
                for p in range(2):
                    copies.append(
                        pltpu.make_async_copy(
                            full.at[near, 2 * p + zh, sec], out.at[0, c, p, :, pl.ds(at, 384)], sem
                        )
                    )
    for copy in copies:
        copy.start()
    for copy in copies:
        copy.wait()


def body(acts, grads_sent, replicas, master, moment, second):
    acts, weights = here(acts), here(replicas)
    w_out, down, up = call(
        take_kernel,
        [((UNITS, D), BF16), ((64, D), BF16), ((64, D), BF16)],
        grads_sent, replicas, specs=[ANY, ANY], scratch=[pltpu.SemaphoreType.DMA((3,))],
    )
    w_out = lax.ppermute(w_out, FAR, weights_route())
    from_after, from_before = shifted(down, -1), shifted(up, 1)
    (pre_act,) = call(forward_kernel, [((2, UNITS, 64), F32)], acts, weights)
    (sent,) = call(wrap_kernel, [((2 * UNITS, 64), F32)], here(w_out), down, up, pre_act)
    wrapped = lax.ppermute(sent, SECTION, wrap_route())
    keep, send = call(
        terms_kernel,
        [((4, 64, 768), F32), ((4, 64, 768), BF16)],
        here(from_after), here(from_before), here(wrapped), acts, weights, pre_act, down, up,
        scratch=[pltpu.VMEM((UNITS, 64), F32), pltpu.VMEM((UNITS, 64), F32)],
    )
    arrived = swap_cores(send)
    (tiles,) = call(merge_kernel, [((4, 64, 768), BF16)], keep, here(arrived))
    near = lax.all_to_all(tiles, "x", 0, 0, tiled=True)
    total, swap = call(near_kernel, [((64, 768), BF16), ((UNITS, 768), BF16)], here(near))
    swap = lax.ppermute(swap, SECTION, swap_route())
    (spread,) = call(spread_kernel, [((4, 2, UNITS, 384), BF16)], total, here(swap))
    far = lax.all_to_all(spread, FAR, 0, 0, axis_index_groups=far_groups(), tiled=True)
    shard = ((1, 2, UNITS, 384), F32)
    new_master, new_moment, new_second, shared = call(
        adam_kernel,
        [shard, shard, shard, ((4, 2, UNITS, 384), BF16)],
        here(far), here(master), here(moment), here(second),
    )
    shared = lax.all_to_all(shared, FAR, 0, 0, axis_index_groups=far_groups(), tiled=True)
    full = lax.all_gather(shared, NEAR, axis=0, tiled=False)
    (new_replicas,) = call(
        finish_kernel,
        [jax.ShapeDtypeStruct((1, 2, 2, UNITS, D), BF16)],
        here(full), scratch=[pltpu.SemaphoreType.DMA],
    )
    return (new_master, new_moment, new_second, new_replicas)


def solution(mesh):
    fine = Mesh(mesh.devices.reshape(4, 8, 2, 4, 2), ("y", "zl", "zh", "x", "c"))
    in_specs = (
        P(SECTION, None, DP, None),
        P(SECTION, None, DP, None),
        P(SECTION, None, None, None, None),
        P(SECTION, None, None, DP),
        P(SECTION, None, None, DP),
        P(SECTION, None, None, DP),
    )
    out_specs = (
        P(SECTION, None, None, DP),
        P(SECTION, None, None, DP),
        P(SECTION, None, None, DP),
        P(SECTION, None, None, None, None),
    )
    return jax.shard_map(body, mesh=fine, in_specs=in_specs, out_specs=out_specs, check_vma=False)
```

time: 134 us -> 118 us (0.88)
  the two profiles are of different devices: /device:TPU:1 before, /device:TPU:9 now
where the time goes in v3:
time: 118 us; the launch traced here: 117 us
  blocking collectives  51.9 us (44%)
  starting transfers between devices  35.8 us (30%)
  waiting for transfers between devices  20.1 us (17%)
  local copies, waits for them, and re-layouts  4.41 us (4%)
  Pallas kernels  4.26 us (4%)
    all_to_all x1, blocking collectives, body(): lax.all_to_all(spread, FAR, 0, 0, axis_index_groups=far_groups(), tiled=T...  22 us
    all_gather x1, blocking collectives, body(): full = lax.all_gather(shared, NEAR, axis=0, tiled=False)  18.8 us
    all_to_all x1, blocking collectives, body(): near = lax.all_to_all(tiles, 'x', 0, 0, tiled=True)  11 us
    all_to_all x1, waiting for transfers between devices, body(): lax.all_to_all(shared, FAR, 0, 0, axis_index_groups=far_groups(), tiled=T...  9.7 us
    ppermute x1, starting transfers between devices, body(): w_out = lax.ppermute(w_out, FAR, weights_route())  9.47 us
    ppermute x1, starting transfers between devices, body(): wrapped = lax.ppermute(sent, SECTION, wrap_route())  8.57 us
    ppermute x2, starting transfers between devices, shifted(): return lax.ppermute(block, SECTION, route)  5.64 us
    ppermute x1, starting transfers between devices, swap_cores(): return lax.ppermute(block, 'c', [(0, 1), (1, 0)])  4.6 us
  transfers between devices with their start and end apart: 7, of which 5 were waited for; matrix products, arithmetic and copies ran while one was open for 2% of the time, Pallas kernels for 1%

profile of v3, /device:TPU:9, one launch (start us, length us, event | category | flops | bytes accessed | tf_op | source)
XLA Modules:
  0.0 117.2 jit_solution(5747268322723512879)
XLA Ops:
  0.6 0.0 copy-start
  0.6 1.1 copy-done
  1.8 0.0 copy-start.3
  1.8 1.4 %copy-done.3 = bf16[1,2,64,6144]{3,2,1,0:T(8,128)(2,1)S(1)} copy-done((bf16[1,2,64,6144]{3,2,1,0:T(8,128)(2,1)S(1)}, bf16[1,2,64,6144]{3,2,1,0:T(8,128)(2,1)}, u32[]{:S(2)}) %copy-start.3) | copy-done | bytes 1572888
  3.2 0.0 copy-start.1
  3.2 0.0 copy-start.2
  3.2 0.4 shard_map.93
  3.6 1.4 %collective-permute-start = (bf16[64,6144]{1,0:T(8,128)(2,1)S(1)}, bf16[64,6144]{1,0:T(8,128)(2,1)S(1)}, u32[]{:S(2)}, u32[]{:S(2)}) collective-permute-start(bf16[64,6144]{1,0:T(8,128)(2,1)S(1)} %get-tuple-element.15.down), channel_id=1, source_target_pairs={{16,0},{32,16},{48,32},{64,48},{80,64},{96,80},{112,96},{144,128},... | collective-permute-start | bytes 2359304 | tf_op jit(solution)/shard_map/ppermute | solution.py:64
  5.0 4.2 %collective-permute-start.1 = (bf16[64,6144]{1,0:T(8,128)(2,1)S(1)}, bf16[64,6144]{1,0:T(8,128)(2,1)S(1)}, u32[]{:S(2)}, u32[]{:S(2)}) collective-permute-start(bf16[64,6144]{1,0:T(8,128)(2,1)S(1)} %get-tuple-element.16.up), channel_id=1, source_target_pairs={{0,16},{16,32},{32,48},{48,64},{64,80},{80,96},{96,112},{128,144},... | collective-permute-start | bytes 2359304 | tf_op jit(solution)/shard_map/ppermute | solution.py:64
  9.2 9.5 %collective-permute-start.2 = (bf16[16,6144]{1,0:T(8,128)(2,1)S(1)}, bf16[16,6144]{1,0:T(8,128)(2,1)S(1)}, u32[]{:S(2)}, u32[]{:S(2)}) collective-permute-start(bf16[16,6144]{1,0:T(8,128)(2,1)S(1)} %get-tuple-element.17), channel_id=1, source_target_pairs={{112,136},{120,128},{128,120},{136,112},{240,264},{248,256},{256,2... | collective-permute-start | bytes 589832 | tf_op jit(solution)/shard_map/ppermute | solution.py:267
  18.7 0.0 copy-done.1
  18.7 0.0 copy-done.2
  18.7 0.5 shard_map.94.pre_act
  19.2 3.8 %collective-permute-done.2.w_out = bf16[16,6144]{1,0:T(8,128)(2,1)S(1)} collective-permute-done((bf16[16,6144]{1,0:T(8,128)(2,1)S(1)}, bf16[16,6144]{1,0:T(8,128)(2,1)S(1)}, u32[]{:S(2)}, u32[]{:S(2)}) %collective-permute-start.2) | collective-permute-done | bytes 196640 | tf_op jit(solution)/shard_map/ppermute | solution.py:267
  23.0 0.3 shard_map.95
  23.3 8.6 %collective-permute-start.3 = (f32[32,64]{1,0:T(8,128)S(1)}, f32[32,64]{1,0:T(8,128)S(1)}, u32[]{:S(2)}, u32[]{:S(2)}) collective-permute-start(f32[32,64]{1,0:T(8,128)S(1)} %shard_map.95), channel_id=1, source_target_pairs={{112,128},{128,112},{240,256},{256,240},{368,384},{384,368},{496,0... | collective-permute-start | bytes 24584 | tf_op jit(solution)/shard_map/ppermute | solution.py:271
  31.9 3.4 %collective-permute-done.3.wrapped = f32[32,64]{1,0:T(8,128)S(1)} collective-permute-done((f32[32,64]{1,0:T(8,128)S(1)}, f32[32,64]{1,0:T(8,128)S(1)}, u32[]{:S(2)}, u32[]{:S(2)}) %collective-permute-start.3) | collective-permute-done | bytes 8224 | tf_op jit(solution)/shard_map/ppermute | solution.py:271
  35.3 0.0 collective-permute-done.from_after
  35.3 0.0 collective-permute-done.1.from_before
  35.3 1.4 %shard_map.96 = (f32[4,64,768]{2,1,0:T(8,128)S(1)}, bf16[4,64,768]{2,1,0:T(8,128)(2,1)S(1)}) custom-call(bf16[64,6144]{1,0:T(8,128)(2,1)S(1)} %collective-permute-done.from_after, bf16[64,6144]{1,0:T(8,128)(2,1)S(1)} %collective-permute-done.1.from_before, f32[32,64]{1,0:T(8,128)S(1)} %collective-permute-done.3.wrapped, ...), custom_call_target="tpu_custom_call" | custom-call | tf_op jit(solution)/shard_map/pallas_call | solution.py:76
  36.7 4.6 %collective-permute-start.4 = (bf16[4,64,768]{2,1,0:T(8,128)(2,1)S(1)}, bf16[4,64,768]{2,1,0:T(8,128)(2,1)S(1)}, u32[]{:S(2)}, u32[]{:S(2)}) collective-permute-start(bf16[4,64,768]{2,1,0:T(8,128)(2,1)S(1)} %get-tuple-element.19), channel_id=1, source_target_pairs={{0,1},{1,0},{2,3},{3,2},{4,5},{5,4},{6,7},{7,6},{8,9},{9,8},{10,11... | collective-permute-start | bytes 1179656 | tf_op jit(solution)/shard_map/ppermute | solution.py:68
  41.3 1.3 %collective-permute-done.4.arrived = bf16[4,64,768]{2,1,0:T(8,128)(2,1)S(1)} collective-permute-done((bf16[4,64,768]{2,1,0:T(8,128)(2,1)S(1)}, bf16[4,64,768]{2,1,0:T(8,128)(2,1)S(1)}, u32[]{:S(2)}, u32[]{:S(2)}) %collective-permute-start.4) | collective-permute-done | bytes 393248 | tf_op jit(solution)/shard_map/ppermute | solution.py:68
  42.6 0.0 copy-start.4
  42.6 0.0 copy-start.5
  42.6 0.0 copy-start.6
  42.6 0.1 shard_map.97
  42.7 11.0 %all_to_all.15.arrived = bf16[4,64,768]{2,1,0:T(8,128)(2,1)S(1)} all-to-all(bf16[4,64,768]{2,1,0:T(8,128)(2,1)S(1)} %shard_map.97), channel_id=1, replica_groups=mesh['y'=4,'zl'=8,'zh'=2,'x'=4,'c'=2] {'x'}, dimensions={0} | all-to-all | bytes 786432 | tf_op jit(solution)/shard_map/all_to_all | solution.py:280
  53.7 0.1 shard_map.98
  53.8 4.2 %collective-permute-start.5 = (bf16[16,768]{1,0:T(8,128)(2,1)S(1)}, bf16[16,768]{1,0:T(8,128)(2,1)S(1)}, u32[]{:S(2)}, u32[]{:S(2)}) collective-permute-start(bf16[16,768]{1,0:T(8,128)(2,1)S(1)} %get-tuple-element.21), channel_id=1, source_target_pairs={{112,368},{368,112},{128,384},{384,128},{113,369},{369,113},{129,3... | collective-permute-start | bytes 73736 | tf_op jit(solution)/shard_map/ppermute | solution.py:282
  58.0 1.9 %collective-permute-done.5.swap = bf16[16,768]{1,0:T(8,128)(2,1)S(1)} collective-permute-done((bf16[16,768]{1,0:T(8,128)(2,1)S(1)}, bf16[16,768]{1,0:T(8,128)(2,1)S(1)}, u32[]{:S(2)}, u32[]{:S(2)}) %collective-permute-start.5) | collective-permute-done | bytes 24608 | tf_op jit(solution)/shard_map/ppermute | solution.py:282
  59.9 22.0 %all_to_all.16.arrived = bf16[4,2,16,384]{3,2,1,0:T(8,128)(2,1)S(1)} all-to-all(bf16[4,2,16,384]{3,2,1,0:T(8,128)(2,1)S(1)} %shard_map.99), channel_id=1, replica_groups={{0,8,496,504},{16,24,480,488},{32,40,464,472},{48,56,448,456},{64,72,43..., dimensions={0} | all-to-all | bytes 196608 | tf_op jit(solution)/shard_map/all_to_all | solution.py:284
  81.9 0.0 copy-done.4
  81.9 0.0 copy-done.5
  81.9 0.0 copy-done.6
  81.9 0.7 shard_map.100
  82.6 3.3 %all-to-all-start.2 = ((bf16[4,2,16,384]{3,2,1,0:T(8,128)(2,1)}), bf16[4,2,16,384]{3,2,1,0:T(8,128)(2,1)S(1)}, u32[]{:S(2)}, u32[]{:S(2)}) async-start(bf16[4,2,16,384]{3,2,1,0:T(8,128)(2,1)} %get-tuple-element.25), calls=%async_computation.2 | async-start | bytes 196608 | tf_op jit(solution)/shard_map/all_to_all | solution.py:291
  85.9 0.6 copy.10
  86.6 0.6 copy.11
  87.2 0.6 copy.12
  87.8 9.7 %all-to-all-done.2 = bf16[4,2,16,384]{3,2,1,0:T(8,128)(2,1)S(1)} async-done(((bf16[4,2,16,384]{3,2,1,0:T(8,128)(2,1)}), bf16[4,2,16,384]{3,2,1,0:T(8,128)(2,1)S(1)}, u32[]{:S(2)}, u32[]{:S(2)}) %all-to-all-start.2) | async-done | bytes 98336 | tf_op jit(solution)/shard_map/all_to_all | solution.py:291
  97.5 18.8 %all-gather = bf16[32,2,16,384]{3,2,1,0:T(8,128)(2,1)S(1)} all-gather(bf16[4,2,16,384]{3,2,1,0:T(8,128)(2,1)S(1)} %all-to-all-done.2), channel_id=2, replica_groups=mesh['y'=4,'zl'=8,'zh'=2,'x'=4,'c'=2] {'x','c'}, dimensions={0}, use_global_device_ids=true | all-gather | bytes 884736 | tf_op jit(solution)/shard_map/all_gather | solution.py:292
  116.3 0.8 shard_map.101
  (1 shorter events, 0.0 us)
Async XLA Ops:
  0.6 1.1 copy-start
  1.8 1.4 %copy-start.3 = (bf16[1,2,64,6144]{3,2,1,0:T(8,128)(2,1)S(1)}, bf16[1,2,64,6144]{3,2,1,0:T(8,128)(2,1)}, u32[]{:S(2)}) copy-start(bf16[1,2,64,6144]{3,2,1,0:T(8,128)(2,1)} %grads.1) | copy-start | bytes 4718596
  3.2 15.5 %copy-start.1 = (bf16[1,2,2,16,6144]{4,3,2,1,0:T(8,128)(2,1)S(1)}, bf16[1,2,2,16,6144]{4,3,2,1,0:T(8,128)(2,1)}, u32[]{:S(2)}) copy-start(bf16[1,2,2,16,6144]{4,3,2,1,0:T(8,128)(2,1)} %weights.5) | copy-start | bytes 2359300
  3.2 15.5 %copy-start.2 = (bf16[1,2,64,6144]{3,2,1,0:T(8,128)(2,1)S(1)}, bf16[1,2,64,6144]{3,2,1,0:T(8,128)(2,1)}, u32[]{:S(2)}) copy-start(bf16[1,2,64,6144]{3,2,1,0:T(8,128)(2,1)} %acts.3) | copy-start | bytes 4718596
  3.6 31.7 %collective-permute-start = (bf16[64,6144]{1,0:T(8,128)(2,1)S(1)}, bf16[64,6144]{1,0:T(8,128)(2,1)S(1)}, u32[]{:S(2)}, u32[]{:S(2)}) collective-permute-start(bf16[64,6144]{1,0:T(8,128)(2,1)S(1)} %get-tuple-element.15.down), channel_id=1, source_target_pairs={{16,0},{32,16},{48,32},{64,48},{80,64},{96,80},{112,96},{144,128},... | collective-permute-start | bytes 2359304 | tf_op jit(solution)/shard_map/ppermute | solution.py:64
  5.0 30.3 %collective-permute-start.1 = (bf16[64,6144]{1,0:T(8,128)(2,1)S(1)}, bf16[64,6144]{1,0:T(8,128)(2,1)S(1)}, u32[]{:S(2)}, u32[]{:S(2)}) collective-permute-start(bf16[64,6144]{1,0:T(8,128)(2,1)S(1)} %get-tuple-element.16.up), channel_id=1, source_target_pairs={{0,16},{16,32},{32,48},{48,64},{64,80},{80,96},{96,112},{128,144},... | collective-permute-start | bytes 2359304 | tf_op jit(solution)/shard_map/ppermute | solution.py:64
  9.2 13.8 %collective-permute-start.2 = (bf16[16,6144]{1,0:T(8,128)(2,1)S(1)}, bf16[16,6144]{1,0:T(8,128)(2,1)S(1)}, u32[]{:S(2)}, u32[]{:S(2)}) collective-permute-start(bf16[16,6144]{1,0:T(8,128)(2,1)S(1)} %get-tuple-element.17), channel_id=1, source_target_pairs={{112,136},{120,128},{128,120},{136,112},{240,264},{248,256},{256,2... | collective-permute-start | bytes 589832 | tf_op jit(solution)/shard_map/ppermute | solution.py:267
  23.3 12.0 %collective-permute-start.3 = (f32[32,64]{1,0:T(8,128)S(1)}, f32[32,64]{1,0:T(8,128)S(1)}, u32[]{:S(2)}, u32[]{:S(2)}) collective-permute-start(f32[32,64]{1,0:T(8,128)S(1)} %shard_map.95), channel_id=1, source_target_pairs={{112,128},{128,112},{240,256},{256,240},{368,384},{384,368},{496,0... | collective-permute-start | bytes 24584 | tf_op jit(solution)/shard_map/ppermute | solution.py:271
  36.7 5.9 %collective-permute-start.4 = (bf16[4,64,768]{2,1,0:T(8,128)(2,1)S(1)}, bf16[4,64,768]{2,1,0:T(8,128)(2,1)S(1)}, u32[]{:S(2)}, u32[]{:S(2)}) collective-permute-start(bf16[4,64,768]{2,1,0:T(8,128)(2,1)S(1)} %get-tuple-element.19), channel_id=1, source_target_pairs={{0,1},{1,0},{2,3},{3,2},{4,5},{5,4},{6,7},{7,6},{8,9},{9,8},{10,11... | collective-permute-start | bytes 1179656 | tf_op jit(solution)/shard_map/ppermute | solution.py:68
  42.6 39.3 %copy-start.4 = (f32[1,2,16,384]{3,2,1,0:T(8,128)S(1)}, f32[1,2,16,384]{3,2,1,0:T(8,128)}, u32[]{:S(2)}) copy-start(f32[1,2,16,384]{3,2,1,0:T(8,128)} %master.1) | copy-start | bytes 147460
  42.6 39.3 %copy-start.5 = (f32[1,2,16,384]{3,2,1,0:T(8,128)S(1)}, f32[1,2,16,384]{3,2,1,0:T(8,128)}, u32[]{:S(2)}) copy-start(f32[1,2,16,384]{3,2,1,0:T(8,128)} %moment.1) | copy-start | bytes 147460
  42.6 39.3 %copy-start.6 = (f32[1,2,16,384]{3,2,1,0:T(8,128)S(1)}, f32[1,2,16,384]{3,2,1,0:T(8,128)}, u32[]{:S(2)}) copy-start(f32[1,2,16,384]{3,2,1,0:T(8,128)} %second.1) | copy-start | bytes 147460
  53.8 6.1 %collective-permute-start.5 = (bf16[16,768]{1,0:T(8,128)(2,1)S(1)}, bf16[16,768]{1,0:T(8,128)(2,1)S(1)}, u32[]{:S(2)}, u32[]{:S(2)}) collective-permute-start(bf16[16,768]{1,0:T(8,128)(2,1)S(1)} %get-tuple-element.21), channel_id=1, source_target_pairs={{112,368},{368,112},{128,384},{384,128},{113,369},{369,113},{129,3... | collective-permute-start | bytes 73736 | tf_op jit(solution)/shard_map/ppermute | solution.py:282
  82.6 14.9 %all-to-all-start.2 = ((bf16[4,2,16,384]{3,2,1,0:T(8,128)(2,1)}), bf16[4,2,16,384]{3,2,1,0:T(8,128)(2,1)S(1)}, u32[]{:S(2)}, u32[]{:S(2)}) async-start(bf16[4,2,16,384]{3,2,1,0:T(8,128)(2,1)} %get-tuple-element.25), calls=%async_computation.2 | async-start | bytes 196608 | tf_op jit(solution)/shard_map/all_to_all | solution.py:291

commit v4 on v3

--- a/solution.py
+++ b/solution.py
@@ -26,6 +26,7 @@
 FAR = ("y", "zl", "zh")
 
 ANY = pl.BlockSpec(memory_space=pl.ANY)
+HBM = pl.BlockSpec(memory_space=pltpu.HBM)
 VMEM = pl.BlockSpec(memory_space=pltpu.VMEM)
 BF16 = jnp.bfloat16
 F32 = jnp.float32
@@ -72,7 +73,7 @@
     return pltpu.with_memory_space_constraint(array, pltpu.VMEM)
 
 
-def call(kernel, outs, *args, specs=None, scratch=(), flops=0, moved=0):
+def call(kernel, outs, *args, specs=None, scratch=(), flops=0, moved=0, vmem=32):
     return pl.pallas_call(
         kernel,
         out_shape=[pltpu.VMEM(*out) if isinstance(out, tuple) else out for out in outs],
@@ -80,7 +81,7 @@
         out_specs=[VMEM if isinstance(out, tuple) else ANY for out in outs],
         scratch_shapes=list(scratch),
         cost_estimate=pl.CostEstimate(flops=flops, bytes_accessed=moved, transcendentals=0),
-        compiler_params=pltpu.CompilerParams(vmem_limit_bytes=32 * 2**20),
+        compiler_params=pltpu.CompilerParams(vmem_limit_bytes=vmem * 2**20),
     )(*args)
 
 
@@ -99,12 +100,15 @@
     return lax.dot_general(a, b, (((ca,), (cb,)), ((), ())), preferred_element_type=F32)
 
 
-def take_kernel(grads, weights, w_out, down, up, sems):
+def take_weights_kernel(weights, w_out, sem):
     side = jnp.where(lax.axis_index("zl") == 7, 0, 1)
+    pltpu.async_copy(weights.at[0, side, 1], w_out, sem).wait()
+
+
+def take_grads_kernel(grads, down, up, sems):
     copies = [
-        pltpu.make_async_copy(weights.at[0, side, 1], w_out, sems.at[0]),
-        pltpu.make_async_copy(grads.at[0, 0], down, sems.at[1]),
-        pltpu.make_async_copy(grads.at[0, 1], up, sems.at[2]),
+        pltpu.make_async_copy(grads.at[0, 0], down, sems.at[0]),
+        pltpu.make_async_copy(grads.at[0, 1], up, sems.at[1]),
     ]
     for copy in copies:
         copy.start()
@@ -258,16 +262,21 @@
 
 
 def body(acts, grads_sent, replicas, master, moment, second):
+    (w_out,) = call(
+        take_weights_kernel,
+        [((UNITS, D), BF16)],
+        replicas, specs=[HBM], scratch=[pltpu.SemaphoreType.DMA], vmem=63,
+    )
+    w_out_moved = lax.ppermute(w_out, FAR, weights_route())
+    down, up = call(
+        take_grads_kernel,
+        [((64, D), BF16), ((64, D), BF16)],
+        grads_sent, specs=[HBM], scratch=[pltpu.SemaphoreType.DMA((2,))], vmem=60, flops=10**10,
+    )
+    from_after, from_before = shifted(down, -1), shifted(up, 1)
     acts, weights = here(acts), here(replicas)
-    w_out, down, up = call(
-        take_kernel,
-        [((UNITS, D), BF16), ((64, D), BF16), ((64, D), BF16)],
-        grads_sent, replicas, specs=[ANY, ANY], scratch=[pltpu.SemaphoreType.DMA((3,))],
-    )
-    w_out = lax.ppermute(w_out, FAR, weights_route())
-    from_after, from_before = shifted(down, -1), shifted(up, 1)
-    (pre_act,) = call(forward_kernel, [((2, UNITS, 64), F32)], acts, weights)
-    (sent,) = call(wrap_kernel, [((2 * UNITS, 64), F32)], here(w_out), down, up, pre_act)
+    (pre_act,) = call(forward_kernel, [((2, UNITS, 64), F32)], acts, weights, flops=10**10)
+    (sent,) = call(wrap_kernel, [((2 * UNITS, 64), F32)], here(w_out_moved), down, up, pre_act)
     wrapped = lax.ppermute(sent, SECTION, wrap_route())
     keep, send = call(
         terms_kernel,

time: 118 us -> 119 us (level)
  waiting for transfers between devices: 20.1 us -> 25.8 us
  starting transfers between devices: 35.8 us -> 32.5 us
  Pallas kernels: 4.26 us -> 6.92 us
  local copies, waits for them, and re-layouts: 4.41 us -> 1.89 us
    ppermute x1, waiting for transfers between devices: 3.42 us -> 12.6 us  [body(): wrapped = lax.ppermute(sent, SECTION, wrap_route())]
    ppermute x1, waiting for transfers between devices: 3.76 us -> 0.01 us  [body(): w_out_moved = lax.ppermute(w_out, FAR, weights_route())]
    ppermute x1, starting transfers between devices: 8.57 us -> 5.06 us  [body(): wrapped = lax.ppermute(sent, SECTION, wrap_route())]
    pallas_call x9 -> x10, Pallas kernels: 4.26 us -> 6.92 us  [call(): pl.pallas_call(kernel, out_shape=[pltpu.VMEM(*out) if isinstance(out, tup...]
    unnamed x17 -> x13, local copies, waits for them, and re-layouts: 4.41 us -> 1.89 us
    ppermute x1, starting transfers between devices: 9.47 us -> 11.1 us  [body(): w_out_moved = lax.ppermute(w_out, FAR, weights_route())]
  transfers between devices with their start and end apart: 7 -> 7, of which waited for: 5 -> 4; matrix products, arithmetic and copies ran while one was open for 2% -> 2% of each run, Pallas kernels for 1% -> 2%
where the time goes in v4:
time: 119 us
  blocking collectives  51.1 us (43%)
  starting transfers between devices  32.5 us (27%)
  waiting for transfers between devices  25.8 us (22%)
  Pallas kernels  6.92 us (6%)
  local copies, waits for them, and re-layouts  1.89 us (2%)
    all_to_all x1, blocking collectives, body(): lax.all_to_all(spread, FAR, 0, 0, axis_index_groups=far_groups(), tiled=T...  21.1 us
    all_gather x1, blocking collectives, body(): full = lax.all_gather(shared, NEAR, axis=0, tiled=False)  18.9 us
    ppermute x1, waiting for transfers between devices, body(): wrapped = lax.ppermute(sent, SECTION, wrap_route())  12.6 us
    ppermute x1, starting transfers between devices, body(): w_out_moved = lax.ppermute(w_out, FAR, weights_route())  11.1 us
    all_to_all x1, blocking collectives, body(): near = lax.all_to_all(tiles, 'x', 0, 0, tiled=True)  11 us
    all_to_all x1, waiting for transfers between devices, body(): lax.all_to_all(shared, FAR, 0, 0, axis_index_groups=far_groups(), tiled=T...  9.7 us
    pallas_call x10, Pallas kernels, call(): pl.pallas_call(kernel, out_shape=[pltpu.VMEM(*out) if isinstance(out, tup...  6.92 us
    ppermute x2, starting transfers between devices, shifted(): return lax.ppermute(block, SECTION, route)  5.33 us
  transfers between devices with their start and end apart: 7, of which 4 were waited for; matrix products, arithmetic and copies ran while one was open for 2% of the time, Pallas kernels for 2%

profile of v4, /device:TPU:9, one launch (start us, length us, event | category | flops | bytes accessed | tf_op | source)
XLA Modules:
  0.0 119.0 jit_solution(1028611177318643359)
XLA Ops:
  0.6 1.6 %shard_map.94 = bf16[16,6144]{1,0:T(8,128)(2,1)} custom-call(bf16[1,2,2,16,6144]{4,3,2,1,0:T(8,128)(2,1)} %weights.5), custom_call_target="tpu_custom_call" | custom-call | tf_op jit(solution)/shard_map/pallas_call | solution.py:77
  2.3 0.0 copy-start
  2.3 0.0 copy-start.1
  2.3 11.1 %collective-permute-start.2 = (bf16[16,6144]{1,0:T(8,128)(2,1)}, bf16[16,6144]{1,0:T(8,128)(2,1)S(1)}, u32[]{:S(2)}, u32[]{:S(2)}) collective-permute-start(bf16[16,6144]{1,0:T(8,128)(2,1)} %shard_map.94), channel_id=1, source_target_pairs={{112,136},{120,128},{128,120},{136,112},{240,264},{248,256},{256,2... | collective-permute-start | bytes 589832 | tf_op jit(solution)/shard_map/ppermute | solution.py:270
  13.4 1.4 %shard_map.93 = (bf16[64,6144]{1,0:T(8,128)(2,1)S(1)}, bf16[64,6144]{1,0:T(8,128)(2,1)S(1)}) custom-call(bf16[1,2,64,6144]{3,2,1,0:T(8,128)(2,1)} %grads.1), custom_call_target="tpu_custom_call" | custom-call | flops 10000000000 | tf_op jit(solution)/shard_map/pallas_call | solution.py:77
  14.8 1.3 %collective-permute-start = (bf16[64,6144]{1,0:T(8,128)(2,1)S(1)}, bf16[64,6144]{1,0:T(8,128)(2,1)S(1)}, u32[]{:S(2)}, u32[]{:S(2)}) collective-permute-start(bf16[64,6144]{1,0:T(8,128)(2,1)S(1)} %get-tuple-element.14.down), channel_id=1, source_target_pairs={{16,0},{32,16},{48,32},{64,48},{80,64},{96,80},{112,96},{144,128},... | collective-permute-start | bytes 2359304 | tf_op jit(solution)/shard_map/ppermute | solution.py:65
  16.1 4.0 %collective-permute-start.1 = (bf16[64,6144]{1,0:T(8,128)(2,1)S(1)}, bf16[64,6144]{1,0:T(8,128)(2,1)S(1)}, u32[]{:S(2)}, u32[]{:S(2)}) collective-permute-start(bf16[64,6144]{1,0:T(8,128)(2,1)S(1)} %get-tuple-element.15.up), channel_id=1, source_target_pairs={{0,16},{16,32},{32,48},{48,64},{64,80},{80,96},{96,112},{128,144},... | collective-permute-start | bytes 2359304 | tf_op jit(solution)/shard_map/ppermute | solution.py:65
  20.2 0.0 copy-done
  20.2 0.0 copy-done.1
  20.2 0.5 shard_map.95.pre_act
  20.7 0.0 collective-permute-done.2.w_out
  20.7 0.3 shard_map.96
  21.0 5.1 %collective-permute-start.3 = (f32[32,64]{1,0:T(8,128)S(1)}, f32[32,64]{1,0:T(8,128)S(1)}, u32[]{:S(2)}, u32[]{:S(2)}) collective-permute-start(f32[32,64]{1,0:T(8,128)S(1)} %shard_map.96), channel_id=1, source_target_pairs={{112,128},{128,112},{240,256},{256,240},{368,384},{384,368},{496,0... | collective-permute-start | bytes 24584 | tf_op jit(solution)/shard_map/ppermute | solution.py:280
  26.1 12.6 %collective-permute-done.3.wrapped = f32[32,64]{1,0:T(8,128)S(1)} collective-permute-done((f32[32,64]{1,0:T(8,128)S(1)}, f32[32,64]{1,0:T(8,128)S(1)}, u32[]{:S(2)}, u32[]{:S(2)}) %collective-permute-start.3) | collective-permute-done | bytes 8224 | tf_op jit(solution)/shard_map/ppermute | solution.py:280
  38.7 0.0 collective-permute-done.from_after
  38.7 0.0 collective-permute-done.1.from_before
  38.7 1.4 %shard_map.97 = (f32[4,64,768]{2,1,0:T(8,128)S(1)}, bf16[4,64,768]{2,1,0:T(8,128)(2,1)S(1)}) custom-call(bf16[64,6144]{1,0:T(8,128)(2,1)S(1)} %collective-permute-done.from_after, bf16[64,6144]{1,0:T(8,128)(2,1)S(1)} %collective-permute-done.1.from_before, f32[32,64]{1,0:T(8,128)S(1)} %collective-permute-done.3.wrapped, ...), custom_call_target="tpu_custom_call" | custom-call | tf_op jit(solution)/shard_map/pallas_call | solution.py:77
  40.1 3.7 %collective-permute-start.4 = (bf16[4,64,768]{2,1,0:T(8,128)(2,1)S(1)}, bf16[4,64,768]{2,1,0:T(8,128)(2,1)S(1)}, u32[]{:S(2)}, u32[]{:S(2)}) collective-permute-start(bf16[4,64,768]{2,1,0:T(8,128)(2,1)S(1)} %get-tuple-element.17), channel_id=1, source_target_pairs={{0,1},{1,0},{2,3},{3,2},{4,5},{5,4},{6,7},{7,6},{8,9},{9,8},{10,11... | collective-permute-start | bytes 1179656 | tf_op jit(solution)/shard_map/ppermute | solution.py:69
  43.9 1.3 %collective-permute-done.4.arrived = bf16[4,64,768]{2,1,0:T(8,128)(2,1)S(1)} collective-permute-done((bf16[4,64,768]{2,1,0:T(8,128)(2,1)S(1)}, bf16[4,64,768]{2,1,0:T(8,128)(2,1)S(1)}, u32[]{:S(2)}, u32[]{:S(2)}) %collective-permute-start.4) | collective-permute-done | bytes 393248 | tf_op jit(solution)/shard_map/ppermute | solution.py:69
  45.2 0.0 copy-start.2
  45.2 0.0 copy-start.3
  45.2 0.0 copy-start.4
  45.2 0.1 shard_map.98
  45.3 11.0 %all_to_all.15.arrived = bf16[4,64,768]{2,1,0:T(8,128)(2,1)S(1)} all-to-all(bf16[4,64,768]{2,1,0:T(8,128)(2,1)S(1)} %shard_map.98), channel_id=1, replica_groups=mesh['y'=4,'zl'=8,'zh'=2,'x'=4,'c'=2] {'x'}, dimensions={0} | all-to-all | bytes 786432 | tf_op jit(solution)/shard_map/all_to_all | solution.py:289
  56.3 0.1 shard_map.99
  56.4 3.9 %collective-permute-start.5 = (bf16[16,768]{1,0:T(8,128)(2,1)S(1)}, bf16[16,768]{1,0:T(8,128)(2,1)S(1)}, u32[]{:S(2)}, u32[]{:S(2)}) collective-permute-start(bf16[16,768]{1,0:T(8,128)(2,1)S(1)} %get-tuple-element.19), channel_id=1, source_target_pairs={{112,368},{368,112},{128,384},{384,128},{113,369},{369,113},{129,3... | collective-permute-start | bytes 73736 | tf_op jit(solution)/shard_map/ppermute | solution.py:291
  60.3 2.1 %collective-permute-done.5.swap = bf16[16,768]{1,0:T(8,128)(2,1)S(1)} collective-permute-done((bf16[16,768]{1,0:T(8,128)(2,1)S(1)}, bf16[16,768]{1,0:T(8,128)(2,1)S(1)}, u32[]{:S(2)}, u32[]{:S(2)}) %collective-permute-start.5) | collective-permute-done | bytes 24608 | tf_op jit(solution)/shard_map/ppermute | solution.py:291
  62.5 21.1 %all_to_all.16.arrived = bf16[4,2,16,384]{3,2,1,0:T(8,128)(2,1)S(1)} all-to-all(bf16[4,2,16,384]{3,2,1,0:T(8,128)(2,1)S(1)} %shard_map.100), channel_id=1, replica_groups={{0,8,496,504},{16,24,480,488},{32,40,464,472},{48,56,448,456},{64,72,43..., dimensions={0} | all-to-all | bytes 196608 | tf_op jit(solution)/shard_map/all_to_all | solution.py:293
  83.6 0.0 copy-done.2
  83.6 0.0 copy-done.3
  83.6 0.0 copy-done.4
  83.6 0.7 shard_map.101
  84.3 3.3 %all-to-all-start.2 = ((bf16[4,2,16,384]{3,2,1,0:T(8,128)(2,1)}), bf16[4,2,16,384]{3,2,1,0:T(8,128)(2,1)S(1)}, u32[]{:S(2)}, u32[]{:S(2)}) async-start(bf16[4,2,16,384]{3,2,1,0:T(8,128)(2,1)} %get-tuple-element.23), calls=%async_computation.2 | async-start | bytes 196608 | tf_op jit(solution)/shard_map/all_to_all | solution.py:300
  87.6 0.6 copy.10
  88.3 0.6 copy.11
  88.9 0.6 copy.12
  89.5 9.7 %all-to-all-done.2 = bf16[4,2,16,384]{3,2,1,0:T(8,128)(2,1)S(1)} async-done(((bf16[4,2,16,384]{3,2,1,0:T(8,128)(2,1)}), bf16[4,2,16,384]{3,2,1,0:T(8,128)(2,1)S(1)}, u32[]{:S(2)}, u32[]{:S(2)}) %all-to-all-start.2) | async-done | bytes 98336 | tf_op jit(solution)/shard_map/all_to_all | solution.py:300
  99.2 18.9 %all-gather = bf16[32,2,16,384]{3,2,1,0:T(8,128)(2,1)S(1)} all-gather(bf16[4,2,16,384]{3,2,1,0:T(8,128)(2,1)S(1)} %all-to-all-done.2), channel_id=2, replica_groups=mesh['y'=4,'zl'=8,'zh'=2,'x'=4,'c'=2] {'x','c'}, dimensions={0}, use_global_device_ids=true | all-gather | bytes 884736 | tf_op jit(solution)/shard_map/all_gather | solution.py:301
  118.1 0.8 shard_map.102
  (1 shorter events, 0.0 us)
Async XLA Ops:
  2.3 17.9 %copy-start = (bf16[1,2,2,16,6144]{4,3,2,1,0:T(8,128)(2,1)S(1)}, bf16[1,2,2,16,6144]{4,3,2,1,0:T(8,128)(2,1)}, u32[]{:S(2)}) copy-start(bf16[1,2,2,16,6144]{4,3,2,1,0:T(8,128)(2,1)} %weights.5) | copy-start | bytes 2359300
  2.3 17.9 %copy-start.1 = (bf16[1,2,64,6144]{3,2,1,0:T(8,128)(2,1)S(1)}, bf16[1,2,64,6144]{3,2,1,0:T(8,128)(2,1)}, u32[]{:S(2)}) copy-start(bf16[1,2,64,6144]{3,2,1,0:T(8,128)(2,1)} %acts.3) | copy-start | bytes 4718596
  2.3 18.4 %collective-permute-start.2 = (bf16[16,6144]{1,0:T(8,128)(2,1)}, bf16[16,6144]{1,0:T(8,128)(2,1)S(1)}, u32[]{:S(2)}, u32[]{:S(2)}) collective-permute-start(bf16[16,6144]{1,0:T(8,128)(2,1)} %shard_map.94), channel_id=1, source_target_pairs={{112,136},{120,128},{128,120},{136,112},{240,264},{248,256},{256,2... | collective-permute-start | bytes 589832 | tf_op jit(solution)/shard_map/ppermute | solution.py:270
  14.8 23.9 %collective-permute-start = (bf16[64,6144]{1,0:T(8,128)(2,1)S(1)}, bf16[64,6144]{1,0:T(8,128)(2,1)S(1)}, u32[]{:S(2)}, u32[]{:S(2)}) collective-permute-start(bf16[64,6144]{1,0:T(8,128)(2,1)S(1)} %get-tuple-element.14.down), channel_id=1, source_target_pairs={{16,0},{32,16},{48,32},{64,48},{80,64},{96,80},{112,96},{144,128},... | collective-permute-start | bytes 2359304 | tf_op jit(solution)/shard_map/ppermute | solution.py:65
  16.1 22.6 %collective-permute-start.1 = (bf16[64,6144]{1,0:T(8,128)(2,1)S(1)}, bf16[64,6144]{1,0:T(8,128)(2,1)S(1)}, u32[]{:S(2)}, u32[]{:S(2)}) collective-permute-start(bf16[64,6144]{1,0:T(8,128)(2,1)S(1)} %get-tuple-element.15.up), channel_id=1, source_target_pairs={{0,16},{16,32},{32,48},{48,64},{64,80},{80,96},{96,112},{128,144},... | collective-permute-start | bytes 2359304 | tf_op jit(solution)/shard_map/ppermute | solution.py:65
  21.0 17.7 %collective-permute-start.3 = (f32[32,64]{1,0:T(8,128)S(1)}, f32[32,64]{1,0:T(8,128)S(1)}, u32[]{:S(2)}, u32[]{:S(2)}) collective-permute-start(f32[32,64]{1,0:T(8,128)S(1)} %shard_map.96), channel_id=1, source_target_pairs={{112,128},{128,112},{240,256},{256,240},{368,384},{384,368},{496,0... | collective-permute-start | bytes 24584 | tf_op jit(solution)/shard_map/ppermute | solution.py:280
  40.1 5.1 %collective-permute-start.4 = (bf16[4,64,768]{2,1,0:T(8,128)(2,1)S(1)}, bf16[4,64,768]{2,1,0:T(8,128)(2,1)S(1)}, u32[]{:S(2)}, u32[]{:S(2)}) collective-permute-start(bf16[4,64,768]{2,1,0:T(8,128)(2,1)S(1)} %get-tuple-element.17), channel_id=1, source_target_pairs={{0,1},{1,0},{2,3},{3,2},{4,5},{5,4},{6,7},{7,6},{8,9},{9,8},{10,11... | collective-permute-start | bytes 1179656 | tf_op jit(solution)/shard_map/ppermute | solution.py:69
  45.2 38.4 %copy-start.2 = (f32[1,2,16,384]{3,2,1,0:T(8,128)S(1)}, f32[1,2,16,384]{3,2,1,0:T(8,128)}, u32[]{:S(2)}) copy-start(f32[1,2,16,384]{3,2,1,0:T(8,128)} %master.1) | copy-start | bytes 147460
  45.2 38.4 %copy-start.3 = (f32[1,2,16,384]{3,2,1,0:T(8,128)S(1)}, f32[1,2,16,384]{3,2,1,0:T(8,128)}, u32[]{:S(2)}) copy-start(f32[1,2,16,384]{3,2,1,0:T(8,128)} %moment.1) | copy-start | bytes 147460
  45.2 38.4 %copy-start.4 = (f32[1,2,16,384]{3,2,1,0:T(8,128)S(1)}, f32[1,2,16,384]{3,2,1,0:T(8,128)}, u32[]{:S(2)}) copy-start(f32[1,2,16,384]{3,2,1,0:T(8,128)} %second.1) | copy-start | bytes 147460
  56.4 6.1 %collective-permute-start.5 = (bf16[16,768]{1,0:T(8,128)(2,1)S(1)}, bf16[16,768]{1,0:T(8,128)(2,1)S(1)}, u32[]{:S(2)}, u32[]{:S(2)}) collective-permute-start(bf16[16,768]{1,0:T(8,128)(2,1)S(1)} %get-tuple-element.19), channel_id=1, source_target_pairs={{112,368},{368,112},{128,384},{384,128},{113,369},{369,113},{129,3... | collective-permute-start | bytes 73736 | tf_op jit(solution)/shard_map/ppermute | solution.py:291
  84.3 14.9 %all-to-all-start.2 = ((bf16[4,2,16,384]{3,2,1,0:T(8,128)(2,1)}), bf16[4,2,16,384]{3,2,1,0:T(8,128)(2,1)S(1)}, u32[]{:S(2)}, u32[]{:S(2)}) async-start(bf16[4,2,16,384]{3,2,1,0:T(8,128)(2,1)} %get-tuple-element.23), calls=%async_computation.2 | async-start | bytes 196608 | tf_op jit(solution)/shard_map/all_to_all | solution.py:300

commit v5 on v3

--- a/solution.py
+++ b/solution.py
@@ -26,6 +26,7 @@
 FAR = ("y", "zl", "zh")
 
 ANY = pl.BlockSpec(memory_space=pl.ANY)
+HBM = pl.BlockSpec(memory_space=pltpu.HBM)
 VMEM = pl.BlockSpec(memory_space=pltpu.VMEM)
 BF16 = jnp.bfloat16
 F32 = jnp.float32
@@ -72,7 +73,7 @@
     return pltpu.with_memory_space_constraint(array, pltpu.VMEM)
 
 
-def call(kernel, outs, *args, specs=None, scratch=(), flops=0, moved=0):
+def call(kernel, outs, *args, specs=None, scratch=(), flops=0, moved=0, vmem=32):
     return pl.pallas_call(
         kernel,
         out_shape=[pltpu.VMEM(*out) if isinstance(out, tuple) else out for out in outs],
@@ -80,7 +81,7 @@
         out_specs=[VMEM if isinstance(out, tuple) else ANY for out in outs],
         scratch_shapes=list(scratch),
         cost_estimate=pl.CostEstimate(flops=flops, bytes_accessed=moved, transcendentals=0),
-        compiler_params=pltpu.CompilerParams(vmem_limit_bytes=32 * 2**20),
+        compiler_params=pltpu.CompilerParams(vmem_limit_bytes=vmem * 2**20),
     )(*args)
 
 
@@ -258,16 +259,17 @@
 
 
 def body(acts, grads_sent, replicas, master, moment, second):
-    acts, weights = here(acts), here(replicas)
     w_out, down, up = call(
         take_kernel,
         [((UNITS, D), BF16), ((64, D), BF16), ((64, D), BF16)],
-        grads_sent, replicas, specs=[ANY, ANY], scratch=[pltpu.SemaphoreType.DMA((3,))],
-    )
-    w_out = lax.ppermute(w_out, FAR, weights_route())
+        grads_sent, replicas, specs=[HBM, HBM],
+        scratch=[pltpu.SemaphoreType.DMA((3,))], vmem=60,
+    )
+    w_out_moved = lax.ppermute(w_out, FAR, weights_route())
     from_after, from_before = shifted(down, -1), shifted(up, 1)
-    (pre_act,) = call(forward_kernel, [((2, UNITS, 64), F32)], acts, weights)
-    (sent,) = call(wrap_kernel, [((2 * UNITS, 64), F32)], here(w_out), down, up, pre_act)
+    acts, weights = here(acts), here(replicas)
+    (pre_act,) = call(forward_kernel, [((2, UNITS, 64), F32)], acts, weights, flops=10**10)
+    (sent,) = call(wrap_kernel, [((2 * UNITS, 64), F32)], here(w_out_moved), down, up, pre_act)
     wrapped = lax.ppermute(sent, SECTION, wrap_route())
     keep, send = call(
         terms_kernel,

time: 118 us -> 118 us (level)
  waiting for transfers between devices: 20.1 us -> 24.6 us
  local copies, waits for them, and re-layouts: 4.41 us -> 1.88 us
  starting transfers between devices: 35.8 us -> 33.6 us
  Pallas kernels: 4.26 us -> 5.56 us
    ppermute x1, waiting for transfers between devices: 3.42 us -> 11.4 us  [body(): wrapped = lax.ppermute(sent, SECTION, wrap_route())]
    ppermute x1, waiting for transfers between devices: 3.76 us -> 0.01 us  [body(): w_out_moved = lax.ppermute(w_out, FAR, weights_route())]
    unnamed x17 -> x13, local copies, waits for them, and re-layouts: 4.41 us -> 1.88 us
    ppermute x1, starting transfers between devices: 8.57 us -> 6.25 us  [body(): wrapped = lax.ppermute(sent, SECTION, wrap_route())]
    ppermute x1, starting transfers between devices: 9.47 us -> 11 us  [body(): w_out_moved = lax.ppermute(w_out, FAR, weights_route())]
    pallas_call x9, Pallas kernels: 4.26 us -> 5.56 us  [call(): pl.pallas_call(kernel, out_shape=[pltpu.VMEM(*out) if isinstance(out, tup...]
  transfers between devices with their start and end apart: 7 -> 7, of which waited for: 5 -> 4; matrix products, arithmetic and copies ran while one was open for 2% -> 2% of each run, Pallas kernels for 1% -> 1%
where the time goes in v5:
time: 118 us; the launch traced here: 117 us
  blocking collectives  51.1 us (43%)
  starting transfers between devices  33.6 us (28%)
  waiting for transfers between devices  24.6 us (21%)
  Pallas kernels  5.56 us (5%)
  local copies, waits for them, and re-layouts  1.88 us (2%)
    all_to_all x1, blocking collectives, body(): lax.all_to_all(spread, FAR, 0, 0, axis_index_groups=far_groups(), tiled=T...  21.1 us
    all_gather x1, blocking collectives, body(): full = lax.all_gather(shared, NEAR, axis=0, tiled=False)  18.9 us
    ppermute x1, waiting for transfers between devices, body(): wrapped = lax.ppermute(sent, SECTION, wrap_route())  11.4 us
    all_to_all x1, blocking collectives, body(): near = lax.all_to_all(tiles, 'x', 0, 0, tiled=True)  11 us
    ppermute x1, starting transfers between devices, body(): w_out_moved = lax.ppermute(w_out, FAR, weights_route())  11 us
    all_to_all x1, waiting for transfers between devices, body(): lax.all_to_all(shared, FAR, 0, 0, axis_index_groups=far_groups(), tiled=T...  9.7 us
    ppermute x1, starting transfers between devices, body(): wrapped = lax.ppermute(sent, SECTION, wrap_route())  6.25 us
    pallas_call x9, Pallas kernels, call(): pl.pallas_call(kernel, out_shape=[pltpu.VMEM(*out) if isinstance(out, tup...  5.56 us
  transfers between devices with their start and end apart: 7, of which 4 were waited for; matrix products, arithmetic and copies ran while one was open for 2% of the time, Pallas kernels for 1%

profile of v5, /device:TPU:9, one launch (start us, length us, event | category | flops | bytes accessed | tf_op | source)
XLA Modules:
  0.0 117.5 jit_solution(1254626865201036926)
XLA Ops:
  0.6 0.0 copy-start
  0.6 0.0 copy-start.1
  0.7 1.7 %shard_map.93 = (bf16[16,6144]{1,0:T(8,128)(2,1)S(1)}, bf16[64,6144]{1,0:T(8,128)(2,1)S(1)}, bf16[64,6144]{1,0:T(8,128)(2,1)S(1)}) custom-call(bf16[1,2,64,6144]{3,2,1,0:T(8,128)(2,1)} %grads.1, bf16[1,2,2,16,6144]{4,3,2,1,0:T(8,128)(2,1)} %weights.5), custom_call_target="tpu_custom_call" | custom-call | tf_op jit(solution)/shard_map/pallas_call | solution.py:77
  2.3 11.0 %collective-permute-start.2 = (bf16[16,6144]{1,0:T(8,128)(2,1)S(1)}, bf16[16,6144]{1,0:T(8,128)(2,1)S(1)}, u32[]{:S(2)}, u32[]{:S(2)}) collective-permute-start(bf16[16,6144]{1,0:T(8,128)(2,1)S(1)} %get-tuple-element.17), channel_id=1, source_target_pairs={{112,136},{120,128},{128,120},{136,112},{240,264},{248,256},{256,2... | collective-permute-start | bytes 589832 | tf_op jit(solution)/shard_map/ppermute | solution.py:268
  13.3 1.3 %collective-permute-start = (bf16[64,6144]{1,0:T(8,128)(2,1)S(1)}, bf16[64,6144]{1,0:T(8,128)(2,1)S(1)}, u32[]{:S(2)}, u32[]{:S(2)}) collective-permute-start(bf16[64,6144]{1,0:T(8,128)(2,1)S(1)} %get-tuple-element.15.down), channel_id=1, source_target_pairs={{16,0},{32,16},{48,32},{64,48},{80,64},{96,80},{112,96},{144,128},... | collective-permute-start | bytes 2359304 | tf_op jit(solution)/shard_map/ppermute | solution.py:65
  14.6 4.0 %collective-permute-start.1 = (bf16[64,6144]{1,0:T(8,128)(2,1)S(1)}, bf16[64,6144]{1,0:T(8,128)(2,1)S(1)}, u32[]{:S(2)}, u32[]{:S(2)}) collective-permute-start(bf16[64,6144]{1,0:T(8,128)(2,1)S(1)} %get-tuple-element.16.up), channel_id=1, source_target_pairs={{0,16},{16,32},{32,48},{48,64},{64,80},{80,96},{96,112},{128,144},... | collective-permute-start | bytes 2359304 | tf_op jit(solution)/shard_map/ppermute | solution.py:65
  18.7 0.0 copy-done
  18.7 0.0 copy-done.1
  18.7 0.5 shard_map.94.pre_act
  19.2 0.0 collective-permute-done.2.w_out
  19.2 0.3 shard_map.95
  19.5 6.2 %collective-permute-start.3 = (f32[32,64]{1,0:T(8,128)S(1)}, f32[32,64]{1,0:T(8,128)S(1)}, u32[]{:S(2)}, u32[]{:S(2)}) collective-permute-start(f32[32,64]{1,0:T(8,128)S(1)} %shard_map.95), channel_id=1, source_target_pairs={{112,128},{128,112},{240,256},{256,240},{368,384},{384,368},{496,0... | collective-permute-start | bytes 24584 | tf_op jit(solution)/shard_map/ppermute | solution.py:273
  25.8 11.4 %collective-permute-done.3.wrapped = f32[32,64]{1,0:T(8,128)S(1)} collective-permute-done((f32[32,64]{1,0:T(8,128)S(1)}, f32[32,64]{1,0:T(8,128)S(1)}, u32[]{:S(2)}, u32[]{:S(2)}) %collective-permute-start.3) | collective-permute-done | bytes 8224 | tf_op jit(solution)/shard_map/ppermute | solution.py:273
  37.2 0.0 collective-permute-done.from_after
  37.2 0.0 collective-permute-done.1.from_before
  37.2 1.4 %shard_map.96 = (f32[4,64,768]{2,1,0:T(8,128)S(1)}, bf16[4,64,768]{2,1,0:T(8,128)(2,1)S(1)}) custom-call(bf16[64,6144]{1,0:T(8,128)(2,1)S(1)} %collective-permute-done.from_after, bf16[64,6144]{1,0:T(8,128)(2,1)S(1)} %collective-permute-done.1.from_before, f32[32,64]{1,0:T(8,128)S(1)} %collective-permute-done.3.wrapped, ...), custom_call_target="tpu_custom_call" | custom-call | tf_op jit(solution)/shard_map/pallas_call | solution.py:77
  38.6 3.7 %collective-permute-start.4 = (bf16[4,64,768]{2,1,0:T(8,128)(2,1)S(1)}, bf16[4,64,768]{2,1,0:T(8,128)(2,1)S(1)}, u32[]{:S(2)}, u32[]{:S(2)}) collective-permute-start(bf16[4,64,768]{2,1,0:T(8,128)(2,1)S(1)} %get-tuple-element.19), channel_id=1, source_target_pairs={{0,1},{1,0},{2,3},{3,2},{4,5},{5,4},{6,7},{7,6},{8,9},{9,8},{10,11... | collective-permute-start | bytes 1179656 | tf_op jit(solution)/shard_map/ppermute | solution.py:69
  42.4 1.3 %collective-permute-done.4.arrived = bf16[4,64,768]{2,1,0:T(8,128)(2,1)S(1)} collective-permute-done((bf16[4,64,768]{2,1,0:T(8,128)(2,1)S(1)}, bf16[4,64,768]{2,1,0:T(8,128)(2,1)S(1)}, u32[]{:S(2)}, u32[]{:S(2)}) %collective-permute-start.4) | collective-permute-done | bytes 393248 | tf_op jit(solution)/shard_map/ppermute | solution.py:69
  43.7 0.0 copy-start.2
  43.7 0.0 copy-start.3
  43.7 0.0 copy-start.4
  43.7 0.1 shard_map.97
  43.8 11.0 %all_to_all.15.arrived = bf16[4,64,768]{2,1,0:T(8,128)(2,1)S(1)} all-to-all(bf16[4,64,768]{2,1,0:T(8,128)(2,1)S(1)} %shard_map.97), channel_id=1, replica_groups=mesh['y'=4,'zl'=8,'zh'=2,'x'=4,'c'=2] {'x'}, dimensions={0} | all-to-all | bytes 786432 | tf_op jit(solution)/shard_map/all_to_all | solution.py:282
  54.8 0.1 shard_map.98
  54.9 3.9 %collective-permute-start.5 = (bf16[16,768]{1,0:T(8,128)(2,1)S(1)}, bf16[16,768]{1,0:T(8,128)(2,1)S(1)}, u32[]{:S(2)}, u32[]{:S(2)}) collective-permute-start(bf16[16,768]{1,0:T(8,128)(2,1)S(1)} %get-tuple-element.21), channel_id=1, source_target_pairs={{112,368},{368,112},{128,384},{384,128},{113,369},{369,113},{129,3... | collective-permute-start | bytes 73736 | tf_op jit(solution)/shard_map/ppermute | solution.py:284
  58.8 2.1 %collective-permute-done.5.swap = bf16[16,768]{1,0:T(8,128)(2,1)S(1)} collective-permute-done((bf16[16,768]{1,0:T(8,128)(2,1)S(1)}, bf16[16,768]{1,0:T(8,128)(2,1)S(1)}, u32[]{:S(2)}, u32[]{:S(2)}) %collective-permute-start.5) | collective-permute-done | bytes 24608 | tf_op jit(solution)/shard_map/ppermute | solution.py:284
  61.0 21.1 %all_to_all.16.arrived = bf16[4,2,16,384]{3,2,1,0:T(8,128)(2,1)S(1)} all-to-all(bf16[4,2,16,384]{3,2,1,0:T(8,128)(2,1)S(1)} %shard_map.99), channel_id=1, replica_groups={{0,8,496,504},{16,24,480,488},{32,40,464,472},{48,56,448,456},{64,72,43..., dimensions={0} | all-to-all | bytes 196608 | tf_op jit(solution)/shard_map/all_to_all | solution.py:286
  82.1 0.0 copy-done.2
  82.1 0.0 copy-done.3
  82.1 0.0 copy-done.4
  82.1 0.7 shard_map.100
  82.8 3.3 %all-to-all-start.2 = ((bf16[4,2,16,384]{3,2,1,0:T(8,128)(2,1)}), bf16[4,2,16,384]{3,2,1,0:T(8,128)(2,1)S(1)}, u32[]{:S(2)}, u32[]{:S(2)}) async-start(bf16[4,2,16,384]{3,2,1,0:T(8,128)(2,1)} %get-tuple-element.25), calls=%async_computation.2 | async-start | bytes 196608 | tf_op jit(solution)/shard_map/all_to_all | solution.py:293
  86.1 0.6 copy.10
  86.8 0.6 copy.11
  87.4 0.6 copy.12
  88.0 9.7 %all-to-all-done.2 = bf16[4,2,16,384]{3,2,1,0:T(8,128)(2,1)S(1)} async-done(((bf16[4,2,16,384]{3,2,1,0:T(8,128)(2,1)}), bf16[4,2,16,384]{3,2,1,0:T(8,128)(2,1)S(1)}, u32[]{:S(2)}, u32[]{:S(2)}) %all-to-all-start.2) | async-done | bytes 98336 | tf_op jit(solution)/shard_map/all_to_all | solution.py:293
  97.7 18.9 %all-gather = bf16[32,2,16,384]{3,2,1,0:T(8,128)(2,1)S(1)} all-gather(bf16[4,2,16,384]{3,2,1,0:T(8,128)(2,1)S(1)} %all-to-all-done.2), channel_id=2, replica_groups=mesh['y'=4,'zl'=8,'zh'=2,'x'=4,'c'=2] {'x','c'}, dimensions={0}, use_global_device_ids=true | all-gather | bytes 884736 | tf_op jit(solution)/shard_map/all_gather | solution.py:294
  116.6 0.8 shard_map.101
  (1 shorter events, 0.0 us)
Async XLA Ops:
  0.6 18.0 %copy-start = (bf16[1,2,2,16,6144]{4,3,2,1,0:T(8,128)(2,1)S(1)}, bf16[1,2,2,16,6144]{4,3,2,1,0:T(8,128)(2,1)}, u32[]{:S(2)}) copy-start(bf16[1,2,2,16,6144]{4,3,2,1,0:T(8,128)(2,1)} %weights.5) | copy-start | bytes 2359300
  0.6 18.0 %copy-start.1 = (bf16[1,2,64,6144]{3,2,1,0:T(8,128)(2,1)S(1)}, bf16[1,2,64,6144]{3,2,1,0:T(8,128)(2,1)}, u32[]{:S(2)}) copy-start(bf16[1,2,64,6144]{3,2,1,0:T(8,128)(2,1)} %acts.3) | copy-start | bytes 4718596
  2.3 16.9 %collective-permute-start.2 = (bf16[16,6144]{1,0:T(8,128)(2,1)S(1)}, bf16[16,6144]{1,0:T(8,128)(2,1)S(1)}, u32[]{:S(2)}, u32[]{:S(2)}) collective-permute-start(bf16[16,6144]{1,0:T(8,128)(2,1)S(1)} %get-tuple-element.17), channel_id=1, source_target_pairs={{112,136},{120,128},{128,120},{136,112},{240,264},{248,256},{256,2... | collective-permute-start | bytes 589832 | tf_op jit(solution)/shard_map/ppermute | solution.py:268
  13.3 23.9 %collective-permute-start = (bf16[64,6144]{1,0:T(8,128)(2,1)S(1)}, bf16[64,6144]{1,0:T(8,128)(2,1)S(1)}, u32[]{:S(2)}, u32[]{:S(2)}) collective-permute-start(bf16[64,6144]{1,0:T(8,128)(2,1)S(1)} %get-tuple-element.15.down), channel_id=1, source_target_pairs={{16,0},{32,16},{48,32},{64,48},{80,64},{96,80},{112,96},{144,128},... | collective-permute-start | bytes 2359304 | tf_op jit(solution)/shard_map/ppermute | solution.py:65
  14.6 22.6 %collective-permute-start.1 = (bf16[64,6144]{1,0:T(8,128)(2,1)S(1)}, bf16[64,6144]{1,0:T(8,128)(2,1)S(1)}, u32[]{:S(2)}, u32[]{:S(2)}) collective-permute-start(bf16[64,6144]{1,0:T(8,128)(2,1)S(1)} %get-tuple-element.16.up), channel_id=1, source_target_pairs={{0,16},{16,32},{32,48},{48,64},{64,80},{80,96},{96,112},{128,144},... | collective-permute-start | bytes 2359304 | tf_op jit(solution)/shard_map/ppermute | solution.py:65
  19.5 17.7 %collective-permute-start.3 = (f32[32,64]{1,0:T(8,128)S(1)}, f32[32,64]{1,0:T(8,128)S(1)}, u32[]{:S(2)}, u32[]{:S(2)}) collective-permute-start(f32[32,64]{1,0:T(8,128)S(1)} %shard_map.95), channel_id=1, source_target_pairs={{112,128},{128,112},{240,256},{256,240},{368,384},{384,368},{496,0... | collective-permute-start | bytes 24584 | tf_op jit(solution)/shard_map/ppermute | solution.py:273
  38.6 5.1 %collective-permute-start.4 = (bf16[4,64,768]{2,1,0:T(8,128)(2,1)S(1)}, bf16[4,64,768]{2,1,0:T(8,128)(2,1)S(1)}, u32[]{:S(2)}, u32[]{:S(2)}) collective-permute-start(bf16[4,64,768]{2,1,0:T(8,128)(2,1)S(1)} %get-tuple-element.19), channel_id=1, source_target_pairs={{0,1},{1,0},{2,3},{3,2},{4,5},{5,4},{6,7},{7,6},{8,9},{9,8},{10,11... | collective-permute-start | bytes 1179656 | tf_op jit(solution)/shard_map/ppermute | solution.py:69
  43.7 38.4 %copy-start.2 = (f32[1,2,16,384]{3,2,1,0:T(8,128)S(1)}, f32[1,2,16,384]{3,2,1,0:T(8,128)}, u32[]{:S(2)}) copy-start(f32[1,2,16,384]{3,2,1,0:T(8,128)} %master.1) | copy-start | bytes 147460
  43.7 38.4 %copy-start.3 = (f32[1,2,16,384]{3,2,1,0:T(8,128)S(1)}, f32[1,2,16,384]{3,2,1,0:T(8,128)}, u32[]{:S(2)}) copy-start(f32[1,2,16,384]{3,2,1,0:T(8,128)} %moment.1) | copy-start | bytes 147460
  43.7 38.4 %copy-start.4 = (f32[1,2,16,384]{3,2,1,0:T(8,128)S(1)}, f32[1,2,16,384]{3,2,1,0:T(8,128)}, u32[]{:S(2)}) copy-start(f32[1,2,16,384]{3,2,1,0:T(8,128)} %second.1) | copy-start | bytes 147460
  54.9 6.1 %collective-permute-start.5 = (bf16[16,768]{1,0:T(8,128)(2,1)S(1)}, bf16[16,768]{1,0:T(8,128)(2,1)S(1)}, u32[]{:S(2)}, u32[]{:S(2)}) collective-permute-start(bf16[16,768]{1,0:T(8,128)(2,1)S(1)} %get-tuple-element.21), channel_id=1, source_target_pairs={{112,368},{368,112},{128,384},{384,128},{113,369},{369,113},{129,3... | collective-permute-start | bytes 73736 | tf_op jit(solution)/shard_map/ppermute | solution.py:284
  82.8 14.9 %all-to-all-start.2 = ((bf16[4,2,16,384]{3,2,1,0:T(8,128)(2,1)}), bf16[4,2,16,384]{3,2,1,0:T(8,128)(2,1)S(1)}, u32[]{:S(2)}, u32[]{:S(2)}) async-start(bf16[4,2,16,384]{3,2,1,0:T(8,128)(2,1)} %get-tuple-element.25), calls=%async_computation.2 | async-start | bytes 196608 | tf_op jit(solution)/shard_map/all_to_all | solution.py:293

commit v6 on v5

--- a/solution.py
+++ b/solution.py
@@ -111,6 +111,21 @@
         copy.start()
     for copy in copies:
         copy.wait()
+
+
+def after_kernel(_, value, out):
+    del value, out
+
+
+def after(first, value, flops):
+    return pl.pallas_call(
+        after_kernel,
+        out_shape=pltpu.VMEM(value.shape, value.dtype),
+        in_specs=[VMEM, VMEM],
+        out_specs=VMEM,
+        input_output_aliases={1: 0},
+        cost_estimate=pl.CostEstimate(flops=flops, bytes_accessed=0, transcendentals=0),
+    )(here(first), here(value))
 
 
 def forward_kernel(acts, weights, pre_act):
@@ -265,8 +280,11 @@
         grads_sent, replicas, specs=[HBM, HBM],
         scratch=[pltpu.SemaphoreType.DMA((3,))], vmem=60,
     )
+    from_before = shifted(up, 1)
+    w_out = after(up, w_out, 10**10)
     w_out_moved = lax.ppermute(w_out, FAR, weights_route())
-    from_after, from_before = shifted(down, -1), shifted(up, 1)
+    down = after(w_out, down, 10**10)
+    from_after = shifted(down, -1)
     acts, weights = here(acts), here(replicas)
     (pre_act,) = call(forward_kernel, [((2, UNITS, 64), F32)], acts, weights, flops=10**10)
     (sent,) = call(wrap_kernel, [((2 * UNITS, 64), F32)], here(w_out_moved), down, up, pre_act)

time: 118 us -> 116 us (0.983)
  the two profiles are of different devices: /device:TPU:9 before, /device:TPU:25 now
where the time goes in v6:
time: 116 us; the launch traced here: 115 us
  blocking collectives  45.9 us (40%)
  starting transfers between devices  40.7 us (35%)
  waiting for transfers between devices  19.3 us (17%)
  Pallas kernels  5.41 us (5%)
  local copies, waits for them, and re-layouts  3.28 us (3%)
    all_gather x1, blocking collectives, body(): full = lax.all_gather(shared, NEAR, axis=0, tiled=False)  19.6 us
    all_to_all x1, blocking collectives, body(): lax.all_to_all(spread, FAR, 0, 0, axis_index_groups=far_groups(), tiled=T...  15.4 us
    ppermute x1, waiting for transfers between devices, body(): wrapped = lax.ppermute(sent, SECTION, wrap_route())  11.6 us
    all_to_all x1, starting transfers between devices, body(): lax.all_to_all(shared, FAR, 0, 0, axis_index_groups=far_groups(), tiled=T...  11.5 us
    all_to_all x1, blocking collectives, body(): near = lax.all_to_all(tiles, 'x', 0, 0, tiled=True)  11 us
    ppermute x1, starting transfers between devices, body(): w_out_moved = lax.ppermute(w_out, FAR, weights_route())  9 us
    ppermute x1, starting transfers between devices, body(): wrapped = lax.ppermute(sent, SECTION, wrap_route())  8.32 us
    pallas_call x9, Pallas kernels, call(): pl.pallas_call(kernel, out_shape=[pltpu.VMEM(*out) if isinstance(out, tup...  5.41 us
  transfers between devices with their start and end apart: 7, of which 5 were waited for; matrix products, arithmetic and copies ran while one was open for 2% of the time, Pallas kernels for 1%

profile of v6, /device:TPU:25, one launch (start us, length us, event | category | flops | bytes accessed | tf_op | source)
XLA Modules:
  0.0 115.4 jit_solution(11082313802848320255)
XLA Ops:
  0.6 1.5 %shard_map.93 = (bf16[16,6144]{1,0:T(8,128)(2,1)S(1)}, bf16[64,6144]{1,0:T(8,128)(2,1)S(1)}, bf16[64,6144]{1,0:T(8,128)(2,1)S(1)}) custom-call(bf16[1,2,64,6144]{3,2,1,0:T(8,128)(2,1)} %grads.1, bf16[1,2,2,16,6144]{4,3,2,1,0:T(8,128)(2,1)} %weights.5), custom_call_target="tpu_custom_call" | custom-call | tf_op jit(solution)/shard_map/pallas_call | solution.py:77
  2.2 3.6 %collective-permute-start.1 = (bf16[64,6144]{1,0:T(8,128)(2,1)S(1)}, bf16[64,6144]{1,0:T(8,128)(2,1)S(1)}, u32[]{:S(2)}, u32[]{:S(2)}) collective-permute-start(bf16[64,6144]{1,0:T(8,128)(2,1)S(1)} %get-tuple-element.15._.up), channel_id=1, source_target_pairs={{0,16},{16,32},{32,48},{48,64},{64,80},{80,96},{96,112},{128,144},... | collective-permute-start | bytes 2359304 | tf_op jit(solution)/shard_map/ppermute | solution.py:65
  5.8 9.0 %collective-permute-start.2 = (bf16[16,6144]{1,0:T(8,128)(2,1)S(1)}, bf16[16,6144]{1,0:T(8,128)(2,1)S(1)}, u32[]{:S(2)}, u32[]{:S(2)}) collective-permute-start(bf16[16,6144]{1,0:T(8,128)(2,1)S(1)} %shard_map.94._), channel_id=1, source_target_pairs={{112,136},{120,128},{128,120},{136,112},{240,264},{248,256},{256,2... | collective-permute-start | bytes 589832 | tf_op jit(solution)/shard_map/ppermute | solution.py:285
  14.8 0.0 copy-start
  14.8 1.4 %collective-permute-start = (bf16[64,6144]{1,0:T(8,128)(2,1)S(1)}, bf16[64,6144]{1,0:T(8,128)(2,1)S(1)}, u32[]{:S(2)}, u32[]{:S(2)}) collective-permute-start(bf16[64,6144]{1,0:T(8,128)(2,1)S(1)} %shard_map.95.down), channel_id=1, source_target_pairs={{16,0},{32,16},{48,32},{64,48},{80,64},{96,80},{112,96},{144,128},... | collective-permute-start | bytes 2359304 | tf_op jit(solution)/shard_map/ppermute | solution.py:65
  16.2 0.0 copy-done
  16.2 0.0 copy-start.1
  16.3 1.4 %copy-done.1 = bf16[1,2,64,6144]{3,2,1,0:T(8,128)(2,1)S(1)} copy-done((bf16[1,2,64,6144]{3,2,1,0:T(8,128)(2,1)S(1)}, bf16[1,2,64,6144]{3,2,1,0:T(8,128)(2,1)}, u32[]{:S(2)}) %copy-start.1) | copy-done | bytes 1572888
  17.7 0.5 shard_map.96.pre_act
  18.2 1.2 %collective-permute-done.2.w_out = bf16[16,6144]{1,0:T(8,128)(2,1)S(1)} collective-permute-done((bf16[16,6144]{1,0:T(8,128)(2,1)S(1)}, bf16[16,6144]{1,0:T(8,128)(2,1)S(1)}, u32[]{:S(2)}, u32[]{:S(2)}) %collective-permute-start.2) | collective-permute-done | bytes 196640 | tf_op jit(solution)/shard_map/ppermute | solution.py:285
  19.4 0.3 shard_map.97
  19.7 8.3 %collective-permute-start.3 = (f32[32,64]{1,0:T(8,128)S(1)}, f32[32,64]{1,0:T(8,128)S(1)}, u32[]{:S(2)}, u32[]{:S(2)}) collective-permute-start(f32[32,64]{1,0:T(8,128)S(1)} %shard_map.97), channel_id=1, source_target_pairs={{112,128},{128,112},{240,256},{256,240},{368,384},{384,368},{496,0... | collective-permute-start | bytes 24584 | tf_op jit(solution)/shard_map/ppermute | solution.py:291
  28.0 11.6 %collective-permute-done.3.wrapped = f32[32,64]{1,0:T(8,128)S(1)} collective-permute-done((f32[32,64]{1,0:T(8,128)S(1)}, f32[32,64]{1,0:T(8,128)S(1)}, u32[]{:S(2)}, u32[]{:S(2)}) %collective-permute-start.3) | collective-permute-done | bytes 8224 | tf_op jit(solution)/shard_map/ppermute | solution.py:291
  39.6 0.0 collective-permute-done.from_after
  39.6 0.0 collective-permute-done.1.from_before
  39.6 1.4 %shard_map.98 = (f32[4,64,768]{2,1,0:T(8,128)S(1)}, bf16[4,64,768]{2,1,0:T(8,128)(2,1)S(1)}) custom-call(bf16[64,6144]{1,0:T(8,128)(2,1)S(1)} %collective-permute-done.from_after, bf16[64,6144]{1,0:T(8,128)(2,1)S(1)} %collective-permute-done.1.from_before, f32[32,64]{1,0:T(8,128)S(1)} %collective-permute-done.3.wrapped, ...), custom_call_target="tpu_custom_call" | custom-call | tf_op jit(solution)/shard_map/pallas_call | solution.py:77
  41.0 4.1 %collective-permute-start.4 = (bf16[4,64,768]{2,1,0:T(8,128)(2,1)S(1)}, bf16[4,64,768]{2,1,0:T(8,128)(2,1)S(1)}, u32[]{:S(2)}, u32[]{:S(2)}) collective-permute-start(bf16[4,64,768]{2,1,0:T(8,128)(2,1)S(1)} %get-tuple-element.19), channel_id=1, source_target_pairs={{0,1},{1,0},{2,3},{3,2},{4,5},{5,4},{6,7},{7,6},{8,9},{9,8},{10,11... | collective-permute-start | bytes 1179656 | tf_op jit(solution)/shard_map/ppermute | solution.py:69
  45.1 1.3 %collective-permute-done.4.arrived = bf16[4,64,768]{2,1,0:T(8,128)(2,1)S(1)} collective-permute-done((bf16[4,64,768]{2,1,0:T(8,128)(2,1)S(1)}, bf16[4,64,768]{2,1,0:T(8,128)(2,1)S(1)}, u32[]{:S(2)}, u32[]{:S(2)}) %collective-permute-start.4) | collective-permute-done | bytes 393248 | tf_op jit(solution)/shard_map/ppermute | solution.py:69
  46.4 0.0 copy-start.2
  46.4 0.0 copy-start.3
  46.4 0.0 copy-start.4
  46.4 0.1 shard_map.99
  46.5 11.0 %all_to_all.15.arrived = bf16[4,64,768]{2,1,0:T(8,128)(2,1)S(1)} all-to-all(bf16[4,64,768]{2,1,0:T(8,128)(2,1)S(1)} %shard_map.99), channel_id=1, replica_groups=mesh['y'=4,'zl'=8,'zh'=2,'x'=4,'c'=2] {'x'}, dimensions={0} | all-to-all | bytes 786432 | tf_op jit(solution)/shard_map/all_to_all | solution.py:300
  57.5 0.1 shard_map.100
  57.6 2.9 %collective-permute-start.5 = (bf16[16,768]{1,0:T(8,128)(2,1)S(1)}, bf16[16,768]{1,0:T(8,128)(2,1)S(1)}, u32[]{:S(2)}, u32[]{:S(2)}) collective-permute-start(bf16[16,768]{1,0:T(8,128)(2,1)S(1)} %get-tuple-element.21), channel_id=1, source_target_pairs={{112,368},{368,112},{128,384},{384,128},{113,369},{369,113},{129,3... | collective-permute-start | bytes 73736 | tf_op jit(solution)/shard_map/ppermute | solution.py:302
  60.4 3.2 %collective-permute-done.5.swap = bf16[16,768]{1,0:T(8,128)(2,1)S(1)} collective-permute-done((bf16[16,768]{1,0:T(8,128)(2,1)S(1)}, bf16[16,768]{1,0:T(8,128)(2,1)S(1)}, u32[]{:S(2)}, u32[]{:S(2)}) %collective-permute-start.5) | collective-permute-done | bytes 24608 | tf_op jit(solution)/shard_map/ppermute | solution.py:302
  63.7 15.4 %all_to_all.16.arrived = bf16[4,2,16,384]{3,2,1,0:T(8,128)(2,1)S(1)} all-to-all(bf16[4,2,16,384]{3,2,1,0:T(8,128)(2,1)S(1)} %shard_map.101), channel_id=1, replica_groups={{0,8,496,504},{16,24,480,488},{32,40,464,472},{48,56,448,456},{64,72,43..., dimensions={0} | all-to-all | bytes 196608 | tf_op jit(solution)/shard_map/all_to_all | solution.py:304
  79.0 0.0 copy-done.2
  79.0 0.0 copy-done.3
  79.0 0.0 copy-done.4
  79.0 0.7 shard_map.102
  79.8 11.5 %all-to-all-start.2 = ((bf16[4,2,16,384]{3,2,1,0:T(8,128)(2,1)}), bf16[4,2,16,384]{3,2,1,0:T(8,128)(2,1)S(1)}, u32[]{:S(2)}, u32[]{:S(2)}) async-start(bf16[4,2,16,384]{3,2,1,0:T(8,128)(2,1)} %get-tuple-element.25), calls=%async_computation.2 | async-start | bytes 196608 | tf_op jit(solution)/shard_map/all_to_all | solution.py:311
  91.2 0.6 copy.14
  91.8 0.6 copy.15
  92.5 0.6 copy.16
  93.1 2.0 %all-to-all-done.2 = bf16[4,2,16,384]{3,2,1,0:T(8,128)(2,1)S(1)} async-done(((bf16[4,2,16,384]{3,2,1,0:T(8,128)(2,1)}), bf16[4,2,16,384]{3,2,1,0:T(8,128)(2,1)S(1)}, u32[]{:S(2)}, u32[]{:S(2)}) %all-to-all-start.2) | async-done | bytes 98336 | tf_op jit(solution)/shard_map/all_to_all | solution.py:311
  95.0 19.6 %all-gather = bf16[32,2,16,384]{3,2,1,0:T(8,128)(2,1)S(1)} all-gather(bf16[4,2,16,384]{3,2,1,0:T(8,128)(2,1)S(1)} %all-to-all-done.2), channel_id=2, replica_groups=mesh['y'=4,'zl'=8,'zh'=2,'x'=4,'c'=2] {'x','c'}, dimensions={0}, use_global_device_ids=true | all-gather | bytes 884736 | tf_op jit(solution)/shard_map/all_gather | solution.py:312
  114.6 0.8 shard_map.103
  (3 shorter events, 0.0 us)
Async XLA Ops:
  2.2 37.5 %collective-permute-start.1 = (bf16[64,6144]{1,0:T(8,128)(2,1)S(1)}, bf16[64,6144]{1,0:T(8,128)(2,1)S(1)}, u32[]{:S(2)}, u32[]{:S(2)}) collective-permute-start(bf16[64,6144]{1,0:T(8,128)(2,1)S(1)} %get-tuple-element.15._.up), channel_id=1, source_target_pairs={{0,16},{16,32},{32,48},{48,64},{64,80},{80,96},{96,112},{128,144},... | collective-permute-start | bytes 2359304 | tf_op jit(solution)/shard_map/ppermute | solution.py:65
  5.8 13.6 %collective-permute-start.2 = (bf16[16,6144]{1,0:T(8,128)(2,1)S(1)}, bf16[16,6144]{1,0:T(8,128)(2,1)S(1)}, u32[]{:S(2)}, u32[]{:S(2)}) collective-permute-start(bf16[16,6144]{1,0:T(8,128)(2,1)S(1)} %shard_map.94._), channel_id=1, source_target_pairs={{112,136},{120,128},{128,120},{136,112},{240,264},{248,256},{256,2... | collective-permute-start | bytes 589832 | tf_op jit(solution)/shard_map/ppermute | solution.py:285
  14.8 1.5 %copy-start = (bf16[1,2,2,16,6144]{4,3,2,1,0:T(8,128)(2,1)S(1)}, bf16[1,2,2,16,6144]{4,3,2,1,0:T(8,128)(2,1)}, u32[]{:S(2)}) copy-start(bf16[1,2,2,16,6144]{4,3,2,1,0:T(8,128)(2,1)} %weights.5) | copy-start | bytes 2359300
  14.8 24.8 %collective-permute-start = (bf16[64,6144]{1,0:T(8,128)(2,1)S(1)}, bf16[64,6144]{1,0:T(8,128)(2,1)S(1)}, u32[]{:S(2)}, u32[]{:S(2)}) collective-permute-start(bf16[64,6144]{1,0:T(8,128)(2,1)S(1)} %shard_map.95.down), channel_id=1, source_target_pairs={{16,0},{32,16},{48,32},{64,48},{80,64},{96,80},{112,96},{144,128},... | collective-permute-start | bytes 2359304 | tf_op jit(solution)/shard_map/ppermute | solution.py:65
  16.2 1.4 %copy-start.1 = (bf16[1,2,64,6144]{3,2,1,0:T(8,128)(2,1)S(1)}, bf16[1,2,64,6144]{3,2,1,0:T(8,128)(2,1)}, u32[]{:S(2)}) copy-start(bf16[1,2,64,6144]{3,2,1,0:T(8,128)(2,1)} %acts.3) | copy-start | bytes 4718596
  19.7 19.9 %collective-permute-start.3 = (f32[32,64]{1,0:T(8,128)S(1)}, f32[32,64]{1,0:T(8,128)S(1)}, u32[]{:S(2)}, u32[]{:S(2)}) collective-permute-start(f32[32,64]{1,0:T(8,128)S(1)} %shard_map.97), channel_id=1, source_target_pairs={{112,128},{128,112},{240,256},{256,240},{368,384},{384,368},{496,0... | collective-permute-start | bytes 24584 | tf_op jit(solution)/shard_map/ppermute | solution.py:291
  41.0 5.4 %collective-permute-start.4 = (bf16[4,64,768]{2,1,0:T(8,128)(2,1)S(1)}, bf16[4,64,768]{2,1,0:T(8,128)(2,1)S(1)}, u32[]{:S(2)}, u32[]{:S(2)}) collective-permute-start(bf16[4,64,768]{2,1,0:T(8,128)(2,1)S(1)} %get-tuple-element.19), channel_id=1, source_target_pairs={{0,1},{1,0},{2,3},{3,2},{4,5},{5,4},{6,7},{7,6},{8,9},{9,8},{10,11... | collective-permute-start | bytes 1179656 | tf_op jit(solution)/shard_map/ppermute | solution.py:69
  46.4 32.6 %copy-start.2 = (f32[1,2,16,384]{3,2,1,0:T(8,128)S(1)}, f32[1,2,16,384]{3,2,1,0:T(8,128)}, u32[]{:S(2)}) copy-start(f32[1,2,16,384]{3,2,1,0:T(8,128)} %master.1) | copy-start | bytes 147460
  46.4 32.6 %copy-start.3 = (f32[1,2,16,384]{3,2,1,0:T(8,128)S(1)}, f32[1,2,16,384]{3,2,1,0:T(8,128)}, u32[]{:S(2)}) copy-start(f32[1,2,16,384]{3,2,1,0:T(8,128)} %moment.1) | copy-start | bytes 147460
  46.4 32.6 %copy-start.4 = (f32[1,2,16,384]{3,2,1,0:T(8,128)S(1)}, f32[1,2,16,384]{3,2,1,0:T(8,128)}, u32[]{:S(2)}) copy-start(f32[1,2,16,384]{3,2,1,0:T(8,128)} %second.1) | copy-start | bytes 147460
  57.6 6.1 %collective-permute-start.5 = (bf16[16,768]{1,0:T(8,128)(2,1)S(1)}, bf16[16,768]{1,0:T(8,128)(2,1)S(1)}, u32[]{:S(2)}, u32[]{:S(2)}) collective-permute-start(bf16[16,768]{1,0:T(8,128)(2,1)S(1)} %get-tuple-element.21), channel_id=1, source_target_pairs={{112,368},{368,112},{128,384},{384,128},{113,369},{369,113},{129,3... | collective-permute-start | bytes 73736 | tf_op jit(solution)/shard_map/ppermute | solution.py:302
  79.8 15.3 %all-to-all-start.2 = ((bf16[4,2,16,384]{3,2,1,0:T(8,128)(2,1)}), bf16[4,2,16,384]{3,2,1,0:T(8,128)(2,1)S(1)}, u32[]{:S(2)}, u32[]{:S(2)}) async-start(bf16[4,2,16,384]{3,2,1,0:T(8,128)(2,1)} %get-tuple-element.25), calls=%async_computation.2 | async-start | bytes 196608 | tf_op jit(solution)/shard_map/all_to_all | solution.py:311

commit v7 on v6

--- a/solution.py
+++ b/solution.py
@@ -59,9 +59,8 @@
     return route
 
 
-def shifted(block, distance):
-    skipped = 7 if distance < 0 else 0
-    route = [((i - distance) % 32, i) for i in range(32) if i % 8 != skipped]
+def shifted(block, distance, senders):
+    route = [(w, (w + distance) % 32) for w in range(32) if w % 8 in senders]
     return lax.ppermute(block, SECTION, route)
 
 
@@ -100,12 +99,22 @@
     return lax.dot_general(a, b, (((ca,), (cb,)), ((), ())), preferred_element_type=F32)
 
 
-def take_kernel(grads, weights, w_out, down, up, sems):
+def joined(*parts):
+    return jnp.concatenate([part[...] for part in parts], axis=0)
+
+
+def columns(parts, at):
+    return joined(*[part.at[:, at : at + 384] for part in parts])
+
+
+def take_kernel(grads, weights, w_out, down, down_a, down_b, up, sems):
     side = jnp.where(lax.axis_index("zl") == 7, 0, 1)
     copies = [
         pltpu.make_async_copy(weights.at[0, side, 1], w_out, sems.at[0]),
-        pltpu.make_async_copy(grads.at[0, 0], down, sems.at[1]),
-        pltpu.make_async_copy(grads.at[0, 1], up, sems.at[2]),
+        pltpu.make_async_copy(grads.at[0, 1], up, sems.at[1]),
+        pltpu.make_async_copy(grads.at[0, 0], down, sems.at[2]),
+        pltpu.make_async_copy(grads.at[0, 0, :32], down_a, sems.at[3]),
+        pltpu.make_async_copy(grads.at[0, 0, 32:], down_b, sems.at[4]),
     ]
     for copy in copies:
         copy.start()
@@ -125,6 +134,7 @@
         out_specs=VMEM,
         input_output_aliases={1: 0},
         cost_estimate=pl.CostEstimate(flops=flops, bytes_accessed=0, transcendentals=0),
+        compiler_params=pltpu.CompilerParams(vmem_limit_bytes=2 * 2**20),
     )(here(first), here(value))
 
 
@@ -148,7 +158,8 @@
 
 
 def terms_kernel(
-    from_after, from_before, wrapped, acts, weights, pre_act, down, up, keep, send, grad, factor
+    from_after, after_a, after_b, from_before, wrapped, acts, weights, pre_act, down, up,
+    keep, send, grad, factor,
 ):
     zl = lax.axis_index("zl")
     first = lax.axis_index("c") == 0
@@ -156,39 +167,46 @@
     def product(lhs, rhs, scale, row):
         for block in range(8):
             x, zh = block % 4, block // 4
-            even = dot(lhs, rhs(block * 768), 1, 0) * scale
-            odd = dot(lhs, rhs(block * 768 + 384), 1, 0) * scale
+            even = dot(lhs, columns(rhs, block * 768), 1, 0) * scale
+            odd = dot(lhs, columns(rhs, block * 768 + 384), 1, 0) * scale
             spot = (x, pl.ds(row, UNITS), pl.ds(zh * 384, 384))
             keep[spot] = jnp.where(first, even, odd)
             send[spot] = jnp.where(first, odd, even).astype(BF16)
 
     for c in range(2):
         wrap = zl == (7 if c == 0 else 0)
-        upstream = from_after if c == 0 else from_before
-        own = up if c == 0 else down
+        if c == 0:
+            own = up
+            beside = zl == 6
+            sources = [
+                (jnp.logical_not(wrap | beside), (from_after,)),
+                (beside, (after_a, after_b)),
+            ]
+        else:
+            own = down
+            sources = [(jnp.logical_not(wrap), (from_before,))]
 
         @pl.when(wrap)
         def _():
             grad[...] = wrapped[UNITS:]
             factor[...] = wrapped[:UNITS]
 
-        @pl.when(jnp.logical_not(wrap))
-        def _():
-            grad[...] = dot(weights[0, c, 1], upstream[...], 1, 1) * INV_HIDDEN
-            factor[...] = pre_act[c]
+        for chosen, upstream in sources:
+
+            @pl.when(chosen)
+            def _():
+                grad[...] = dot(weights[0, c, 1], joined(*upstream), 1, 1) * INV_HIDDEN
+                factor[...] = pre_act[c]
 
         pre_grad = (grad[...] * gelu_slope(pre_act[c])).astype(BF16)
         activation = gelu_exact(factor[...]).astype(BF16)
         row = c * 2 * UNITS
-        product(pre_grad, lambda at: acts[0, c, :, at : at + 384], INV_WIDTH, row)
-
-        @pl.when(wrap)
-        def _():
-            product(activation, lambda at: own[:, at : at + 384], INV_HIDDEN, row + UNITS)
-
-        @pl.when(jnp.logical_not(wrap))
-        def _():
-            product(activation, lambda at: upstream[:, at : at + 384], INV_HIDDEN, row + UNITS)
+        product(pre_grad, (acts.at[0, c],), INV_WIDTH, row)
+        for chosen, upstream in [(wrap, (own,))] + sources:
+
+            @pl.when(chosen)
+            def _():
+                product(activation, upstream, INV_HIDDEN, row + UNITS)
 
 
 def merge_kernel(keep, arrived, out):
@@ -274,25 +292,34 @@
 
 
 def body(acts, grads_sent, replicas, master, moment, second):
-    w_out, down, up = call(
+    half = ((32, D), BF16)
+    w_out, down, down_a, down_b, up = call(
         take_kernel,
-        [((UNITS, D), BF16), ((64, D), BF16), ((64, D), BF16)],
+        [((UNITS, D), BF16), ((64, D), BF16), half, half, ((64, D), BF16)],
         grads_sent, replicas, specs=[HBM, HBM],
-        scratch=[pltpu.SemaphoreType.DMA((3,))], vmem=60,
-    )
-    from_before = shifted(up, 1)
-    w_out = after(up, w_out, 10**10)
+        scratch=[pltpu.SemaphoreType.DMA((5,))], vmem=58,
+    )
+    from_before = shifted(up, 1, range(7))
+    down = after(up, down, 10**10)
+    from_after = shifted(down, -1, range(1, 7))
+    w_out = after(down, w_out, 10**10)
     w_out_moved = lax.ppermute(w_out, FAR, weights_route())
-    down = after(w_out, down, 10**10)
-    from_after = shifted(down, -1)
+    down_a = after(w_out, down_a, 10**10)
+    after_a = shifted(down_a, -1, (7,))
     acts, weights = here(acts), here(replicas)
     (pre_act,) = call(forward_kernel, [((2, UNITS, 64), F32)], acts, weights, flops=10**10)
-    (sent,) = call(wrap_kernel, [((2 * UNITS, 64), F32)], here(w_out_moved), down, up, pre_act)
+    (sent,) = call(
+        wrap_kernel, [((2 * UNITS, 64), F32)], here(w_out_moved), down, up, pre_act
+    )
     wrapped = lax.ppermute(sent, SECTION, wrap_route())
+    down_b = after(sent, down_b, 10**10)
+    after_b = shifted(down_b, -1, (7,))
+    pre_act = after(down_b, pre_act, 10**10)
     keep, send = call(
         terms_kernel,
         [((4, 64, 768), F32), ((4, 64, 768), BF16)],
-        here(from_after), here(from_before), here(wrapped), acts, weights, pre_act, down, up,
+        here(from_after), here(after_a), here(after_b), here(from_before), here(wrapped),
+        acts, weights, pre_act, down, up,
         scratch=[pltpu.VMEM((UNITS, 64), F32), pltpu.VMEM((UNITS, 64), F32)],
     )
     arrived = swap_cores(send)

time: 116 us -> 116 us (level)
  waiting for transfers between devices: 19.3 us -> 11.3 us
  blocking collectives: 45.9 us -> 52.1 us
  starting transfers between devices: 40.7 us -> 42.6 us
    ppermute x1, waiting for transfers between devices: 11.6 us -> 2.61 us  [body(): wrapped = lax.ppermute(sent, SECTION, wrap_route())]
    all_to_all x1, blocking collectives: 15.4 us -> 21 us  [body(): lax.all_to_all(spread, FAR, 0, 0, axis_index_groups=far_groups(), tiled=T...]
    ppermute x2 -> x4, starting transfers between devices: 5.01 us -> 6.39 us  [shifted(): return lax.ppermute(block, SECTION, route)]
    ppermute x1, waiting for transfers between devices: 1.23 us -> 2.44 us  [body(): w_out_moved = lax.ppermute(w_out, FAR, weights_route())]
  transfers between devices with their start and end apart: 7 -> 9, of which waited for: 5 -> 5; matrix products, arithmetic and copies ran while one was open for 2% -> 2% of each run, Pallas kernels for 1% -> 1%
where the time goes in v7:
time: 116 us; the launch traced here: 115 us
  blocking collectives  52.1 us (45%)
  starting transfers between devices  42.6 us (37%)
  waiting for transfers between devices  11.3 us (10%)
  Pallas kernels  5.67 us (5%)
  local copies, waits for them, and re-layouts  2.68 us (2%)
    all_to_all x1, blocking collectives, body(): lax.all_to_all(spread, FAR, 0, 0, axis_index_groups=far_groups(), tiled=T...  21 us
    all_gather x1, blocking collectives, body(): full = lax.all_gather(shared, NEAR, axis=0, tiled=False)  20 us
    all_to_all x1, starting transfers between devices, body(): lax.all_to_all(shared, FAR, 0, 0, axis_index_groups=far_groups(), tiled=T...  11.4 us
    all_to_all x1, blocking collectives, body(): near = lax.all_to_all(tiles, 'x', 0, 0, tiled=True)  11 us
    ppermute x1, starting transfers between devices, body(): wrapped = lax.ppermute(sent, SECTION, wrap_route())  8.9 us
    ppermute x1, starting transfers between devices, body(): w_out_moved = lax.ppermute(w_out, FAR, weights_route())  8.42 us
    ppermute x4, starting transfers between devices, shifted(): return lax.ppermute(block, SECTION, route)  6.39 us
    pallas_call x9, Pallas kernels, call(): pl.pallas_call(kernel, out_shape=[pltpu.VMEM(*out) if isinstance(out, tup...  5.66 us
  transfers between devices with their start and end apart: 9, of which 5 were waited for; matrix products, arithmetic and copies ran while one was open for 2% of the time, Pallas kernels for 1%

profile of v7, /device:TPU:25, one launch (start us, length us, event | category | flops | bytes accessed | tf_op | source)
XLA Modules:
  0.0 115.1 jit_solution(17041712594346479210)
XLA Ops:
  0.6 1.8 %shard_map.93 = (bf16[16,6144]{1,0:T(8,128)(2,1)S(1)}, bf16[64,6144]{1,0:T(8,128)(2,1)S(1)}, bf16[32,6144]{1,0:T(8,128)(2,1)S(1)}, bf16[32,6144]{1,0:T(8,128)(2,1)S(1)}, bf16[64,6144]{1,0:T(8,128)(2,1)S(1)}) custom-call(bf16[1,2,64,6144]{3,2,1,0:T(8,128)(2,1)} %grads.1, bf16[1,2,2,16,6144]{4,3,2,1,0:T(8,128)(2,1)} %weights.5), custom_call_target="tpu_custom_call" | custom-call | tf_op jit(solution)/shard_map/pallas_call | solution.py:76
  2.4 3.6 %collective-permute-start.4 = (bf16[64,6144]{1,0:T(8,128)(2,1)S(1)}, bf16[64,6144]{1,0:T(8,128)(2,1)S(1)}, u32[]{:S(2)}, u32[]{:S(2)}) collective-permute-start(bf16[64,6144]{1,0:T(8,128)(2,1)S(1)} %get-tuple-element.17._.up), channel_id=1, source_target_pairs={{0,16},{16,32},{32,48},{48,64},{64,80},{80,96},{96,112},{128,144},... | collective-permute-start | bytes 2359304 | tf_op jit(solution)/shard_map/ppermute | solution.py:64
  6.0 1.3 %collective-permute-start = (bf16[64,6144]{1,0:T(8,128)(2,1)S(1)}, bf16[64,6144]{1,0:T(8,128)(2,1)S(1)}, u32[]{:S(2)}, u32[]{:S(2)}) collective-permute-start(bf16[64,6144]{1,0:T(8,128)(2,1)S(1)} %shard_map.94._.down), channel_id=1, source_target_pairs={{16,0},{32,16},{48,32},{64,48},{80,64},{96,80},{144,128},{160,144}... | collective-permute-start | bytes 2359304 | tf_op jit(solution)/shard_map/ppermute | solution.py:64
  7.3 8.4 %collective-permute-start.2 = (bf16[16,6144]{1,0:T(8,128)(2,1)S(1)}, bf16[16,6144]{1,0:T(8,128)(2,1)S(1)}, u32[]{:S(2)}, u32[]{:S(2)}) collective-permute-start(bf16[16,6144]{1,0:T(8,128)(2,1)S(1)} %shard_map.95._), channel_id=1, source_target_pairs={{112,136},{120,128},{128,120},{136,112},{240,264},{248,256},{256,2... | collective-permute-start | bytes 589832 | tf_op jit(solution)/shard_map/ppermute | solution.py:306
  15.7 0.0 copy-start
  15.7 0.0 copy-start.1
  15.8 0.8 collective-permute-start.1
  16.6 0.3 copy-done
  16.9 0.5 copy-done.1
  17.4 0.5 shard_map.97.pre_act.value
  17.9 2.4 %collective-permute-done.2.w_out = bf16[16,6144]{1,0:T(8,128)(2,1)S(1)} collective-permute-done((bf16[16,6144]{1,0:T(8,128)(2,1)S(1)}, bf16[16,6144]{1,0:T(8,128)(2,1)S(1)}, u32[]{:S(2)}, u32[]{:S(2)}) %collective-permute-start.2) | collective-permute-done | bytes 196640 | tf_op jit(solution)/shard_map/ppermute | solution.py:306
  20.3 0.3 shard_map.98._
  20.7 8.9 %collective-permute-start.5 = (f32[32,64]{1,0:T(8,128)S(1)}, f32[32,64]{1,0:T(8,128)S(1)}, u32[]{:S(2)}, u32[]{:S(2)}) collective-permute-start(f32[32,64]{1,0:T(8,128)S(1)} %shard_map.98._), channel_id=1, source_target_pairs={{112,128},{128,112},{240,256},{256,240},{368,384},{384,368},{496,0... | collective-permute-start | bytes 24584 | tf_op jit(solution)/shard_map/ppermute | solution.py:314
  29.6 0.7 collective-permute-start.3
  30.3 2.6 %collective-permute-done.5.wrapped = f32[32,64]{1,0:T(8,128)S(1)} collective-permute-done((f32[32,64]{1,0:T(8,128)S(1)}, f32[32,64]{1,0:T(8,128)S(1)}, u32[]{:S(2)}, u32[]{:S(2)}) %collective-permute-start.5) | collective-permute-done | bytes 8224 | tf_op jit(solution)/shard_map/ppermute | solution.py:314
  32.9 0.0 collective-permute-done.1.after_a
  32.9 0.0 collective-permute-done.3.after_b
  32.9 0.0 collective-permute-done.from_after
  32.9 0.0 collective-permute-done.4.from_before
  32.9 1.4 %shard_map.101 = (f32[4,64,768]{2,1,0:T(8,128)S(1)}, bf16[4,64,768]{2,1,0:T(8,128)(2,1)S(1)}) custom-call(bf16[64,6144]{1,0:T(8,128)(2,1)S(1)} %collective-permute-done.from_after, bf16[32,6144]{1,0:T(8,128)(2,1)S(1)} %collective-permute-done.1.after_a, bf16[32,6144]{1,0:T(8,128)(2,1)S(1)} %collective-permute-done.3.after_b, ...), custom_call_target="tpu_custom_call" | custom-call | tf_op jit(solution)/shard_map/pallas_call | solution.py:76
  34.3 4.3 %collective-permute-start.6 = (bf16[4,64,768]{2,1,0:T(8,128)(2,1)S(1)}, bf16[4,64,768]{2,1,0:T(8,128)(2,1)S(1)}, u32[]{:S(2)}, u32[]{:S(2)}) collective-permute-start(bf16[4,64,768]{2,1,0:T(8,128)(2,1)S(1)} %get-tuple-element.23), channel_id=1, source_target_pairs={{0,1},{1,0},{2,3},{3,2},{4,5},{5,4},{6,7},{7,6},{8,9},{9,8},{10,11... | collective-permute-start | bytes 1179656 | tf_op jit(solution)/shard_map/ppermute | solution.py:68
  38.6 1.3 %collective-permute-done.6.arrived = bf16[4,64,768]{2,1,0:T(8,128)(2,1)S(1)} collective-permute-done((bf16[4,64,768]{2,1,0:T(8,128)(2,1)S(1)}, bf16[4,64,768]{2,1,0:T(8,128)(2,1)S(1)}, u32[]{:S(2)}, u32[]{:S(2)}) %collective-permute-start.6) | collective-permute-done | bytes 393248 | tf_op jit(solution)/shard_map/ppermute | solution.py:68
  39.9 0.0 copy-start.2
  39.9 0.0 copy-start.3
  39.9 0.0 copy-start.4
  39.9 0.1 shard_map.102
  40.0 11.0 %all_to_all.15.arrived = bf16[4,64,768]{2,1,0:T(8,128)(2,1)S(1)} all-to-all(bf16[4,64,768]{2,1,0:T(8,128)(2,1)S(1)} %shard_map.102), channel_id=1, replica_groups=mesh['y'=4,'zl'=8,'zh'=2,'x'=4,'c'=2] {'x'}, dimensions={0} | all-to-all | bytes 786432 | tf_op jit(solution)/shard_map/all_to_all | solution.py:327
  51.0 0.1 shard_map.103
  51.1 3.2 %collective-permute-start.7 = (bf16[16,768]{1,0:T(8,128)(2,1)S(1)}, bf16[16,768]{1,0:T(8,128)(2,1)S(1)}, u32[]{:S(2)}, u32[]{:S(2)}) collective-permute-start(bf16[16,768]{1,0:T(8,128)(2,1)S(1)} %get-tuple-element.25), channel_id=1, source_target_pairs={{112,368},{368,112},{128,384},{384,128},{113,369},{369,113},{129,3... | collective-permute-start | bytes 73736 | tf_op jit(solution)/shard_map/ppermute | solution.py:329
  54.3 2.9 %collective-permute-done.7.swap = bf16[16,768]{1,0:T(8,128)(2,1)S(1)} collective-permute-done((bf16[16,768]{1,0:T(8,128)(2,1)S(1)}, bf16[16,768]{1,0:T(8,128)(2,1)S(1)}, u32[]{:S(2)}, u32[]{:S(2)}) %collective-permute-start.7) | collective-permute-done | bytes 24608 | tf_op jit(solution)/shard_map/ppermute | solution.py:329
  57.2 21.0 %all_to_all.16.arrived = bf16[4,2,16,384]{3,2,1,0:T(8,128)(2,1)S(1)} all-to-all(bf16[4,2,16,384]{3,2,1,0:T(8,128)(2,1)S(1)} %shard_map.104), channel_id=1, replica_groups={{0,8,496,504},{16,24,480,488},{32,40,464,472},{48,56,448,456},{64,72,43..., dimensions={0} | all-to-all | bytes 196608 | tf_op jit(solution)/shard_map/all_to_all | solution.py:331
  78.2 0.0 copy-done.2
  78.2 0.0 copy-done.3
  78.2 0.0 copy-done.4
  78.2 0.7 shard_map.105
  79.0 11.4 %all-to-all-start.2 = ((bf16[4,2,16,384]{3,2,1,0:T(8,128)(2,1)}), bf16[4,2,16,384]{3,2,1,0:T(8,128)(2,1)S(1)}, u32[]{:S(2)}, u32[]{:S(2)}) async-start(bf16[4,2,16,384]{3,2,1,0:T(8,128)(2,1)} %get-tuple-element.29), calls=%async_computation.2 | async-start | bytes 196608 | tf_op jit(solution)/shard_map/all_to_all | solution.py:338
  90.4 0.6 copy.20
  91.0 0.6 copy.21
  91.6 0.6 copy.22
  92.3 2.0 %all-to-all-done.2 = bf16[4,2,16,384]{3,2,1,0:T(8,128)(2,1)S(1)} async-done(((bf16[4,2,16,384]{3,2,1,0:T(8,128)(2,1)}), bf16[4,2,16,384]{3,2,1,0:T(8,128)(2,1)S(1)}, u32[]{:S(2)}, u32[]{:S(2)}) %all-to-all-start.2) | async-done | bytes 98336 | tf_op jit(solution)/shard_map/all_to_all | solution.py:338
  94.2 20.0 %all-gather = bf16[32,2,16,384]{3,2,1,0:T(8,128)(2,1)S(1)} all-gather(bf16[4,2,16,384]{3,2,1,0:T(8,128)(2,1)S(1)} %all-to-all-done.2), channel_id=2, replica_groups=mesh['y'=4,'zl'=8,'zh'=2,'x'=4,'c'=2] {'x','c'}, dimensions={0}, use_global_device_ids=true | all-gather | bytes 884736 | tf_op jit(solution)/shard_map/all_gather | solution.py:339
  114.2 0.8 shard_map.106
  (6 shorter events, 0.0 us)
Async XLA Ops:
  2.4 30.5 %collective-permute-start.4 = (bf16[64,6144]{1,0:T(8,128)(2,1)S(1)}, bf16[64,6144]{1,0:T(8,128)(2,1)S(1)}, u32[]{:S(2)}, u32[]{:S(2)}) collective-permute-start(bf16[64,6144]{1,0:T(8,128)(2,1)S(1)} %get-tuple-element.17._.up), channel_id=1, source_target_pairs={{0,16},{16,32},{32,48},{48,64},{64,80},{80,96},{96,112},{128,144},... | collective-permute-start | bytes 2359304 | tf_op jit(solution)/shard_map/ppermute | solution.py:64
  6.0 26.9 %collective-permute-start = (bf16[64,6144]{1,0:T(8,128)(2,1)S(1)}, bf16[64,6144]{1,0:T(8,128)(2,1)S(1)}, u32[]{:S(2)}, u32[]{:S(2)}) collective-permute-start(bf16[64,6144]{1,0:T(8,128)(2,1)S(1)} %shard_map.94._.down), channel_id=1, source_target_pairs={{16,0},{32,16},{48,32},{64,48},{80,64},{96,80},{144,128},{160,144}... | collective-permute-start | bytes 2359304 | tf_op jit(solution)/shard_map/ppermute | solution.py:64
  7.3 13.0 %collective-permute-start.2 = (bf16[16,6144]{1,0:T(8,128)(2,1)S(1)}, bf16[16,6144]{1,0:T(8,128)(2,1)S(1)}, u32[]{:S(2)}, u32[]{:S(2)}) collective-permute-start(bf16[16,6144]{1,0:T(8,128)(2,1)S(1)} %shard_map.95._), channel_id=1, source_target_pairs={{112,136},{120,128},{128,120},{136,112},{240,264},{248,256},{256,2... | collective-permute-start | bytes 589832 | tf_op jit(solution)/shard_map/ppermute | solution.py:306
  15.7 1.1 copy-start
  15.7 1.6 %copy-start.1 = (bf16[1,2,64,6144]{3,2,1,0:T(8,128)(2,1)S(1)}, bf16[1,2,64,6144]{3,2,1,0:T(8,128)(2,1)}, u32[]{:S(2)}) copy-start(bf16[1,2,64,6144]{3,2,1,0:T(8,128)(2,1)} %acts.3) | copy-start | bytes 4718596
  15.8 17.1 %collective-permute-start.1 = (bf16[32,6144]{1,0:T(8,128)(2,1)S(1)}, bf16[32,6144]{1,0:T(8,128)(2,1)S(1)}, u32[]{:S(2)}, u32[]{:S(2)}) collective-permute-start(bf16[32,6144]{1,0:T(8,128)(2,1)S(1)} %shard_map.96), channel_id=1, source_target_pairs={{112,96},{240,224},{368,352},{496,480},{113,97},{241,225},{369,353... | collective-permute-start | bytes 1179656 | tf_op jit(solution)/shard_map/ppermute | solution.py:64
  20.7 12.2 %collective-permute-start.5 = (f32[32,64]{1,0:T(8,128)S(1)}, f32[32,64]{1,0:T(8,128)S(1)}, u32[]{:S(2)}, u32[]{:S(2)}) collective-permute-start(f32[32,64]{1,0:T(8,128)S(1)} %shard_map.98._), channel_id=1, source_target_pairs={{112,128},{128,112},{240,256},{256,240},{368,384},{384,368},{496,0... | collective-permute-start | bytes 24584 | tf_op jit(solution)/shard_map/ppermute | solution.py:314
  29.6 3.3 %collective-permute-start.3 = (bf16[32,6144]{1,0:T(8,128)(2,1)S(1)}, bf16[32,6144]{1,0:T(8,128)(2,1)S(1)}, u32[]{:S(2)}, u32[]{:S(2)}) collective-permute-start(bf16[32,6144]{1,0:T(8,128)(2,1)S(1)} %shard_map.99._), channel_id=1, source_target_pairs={{112,96},{240,224},{368,352},{496,480},{113,97},{241,225},{369,353... | collective-permute-start | bytes 1179656 | tf_op jit(solution)/shard_map/ppermute | solution.py:64
  34.3 5.6 %collective-permute-start.6 = (bf16[4,64,768]{2,1,0:T(8,128)(2,1)S(1)}, bf16[4,64,768]{2,1,0:T(8,128)(2,1)S(1)}, u32[]{:S(2)}, u32[]{:S(2)}) collective-permute-start(bf16[4,64,768]{2,1,0:T(8,128)(2,1)S(1)} %get-tuple-element.23), channel_id=1, source_target_pairs={{0,1},{1,0},{2,3},{3,2},{4,5},{5,4},{6,7},{7,6},{8,9},{9,8},{10,11... | collective-permute-start | bytes 1179656 | tf_op jit(solution)/shard_map/ppermute | solution.py:68
  39.9 38.3 %copy-start.2 = (f32[1,2,16,384]{3,2,1,0:T(8,128)S(1)}, f32[1,2,16,384]{3,2,1,0:T(8,128)}, u32[]{:S(2)}) copy-start(f32[1,2,16,384]{3,2,1,0:T(8,128)} %master.1) | copy-start | bytes 147460
  39.9 38.3 %copy-start.3 = (f32[1,2,16,384]{3,2,1,0:T(8,128)S(1)}, f32[1,2,16,384]{3,2,1,0:T(8,128)}, u32[]{:S(2)}) copy-start(f32[1,2,16,384]{3,2,1,0:T(8,128)} %moment.1) | copy-start | bytes 147460
  39.9 38.3 %copy-start.4 = (f32[1,2,16,384]{3,2,1,0:T(8,128)S(1)}, f32[1,2,16,384]{3,2,1,0:T(8,128)}, u32[]{:S(2)}) copy-start(f32[1,2,16,384]{3,2,1,0:T(8,128)} %second.1) | copy-start | bytes 147460
  51.1 6.1 %collective-permute-start.7 = (bf16[16,768]{1,0:T(8,128)(2,1)S(1)}, bf16[16,768]{1,0:T(8,128)(2,1)S(1)}, u32[]{:S(2)}, u32[]{:S(2)}) collective-permute-start(bf16[16,768]{1,0:T(8,128)(2,1)S(1)} %get-tuple-element.25), channel_id=1, source_target_pairs={{112,368},{368,112},{128,384},{384,128},{113,369},{369,113},{129,3... | collective-permute-start | bytes 73736 | tf_op jit(solution)/shard_map/ppermute | solution.py:329
  79.0 15.3 %all-to-all-start.2 = ((bf16[4,2,16,384]{3,2,1,0:T(8,128)(2,1)}), bf16[4,2,16,384]{3,2,1,0:T(8,128)(2,1)S(1)}, u32[]{:S(2)}, u32[]{:S(2)}) async-start(bf16[4,2,16,384]{3,2,1,0:T(8,128)(2,1)} %get-tuple-element.29), calls=%async_computation.2 | async-start | bytes 196608 | tf_op jit(solution)/shard_map/all_to_all | solution.py:338

commit v8 on v7

--- a/solution.py
+++ b/solution.py
@@ -113,8 +113,8 @@
         pltpu.make_async_copy(weights.at[0, side, 1], w_out, sems.at[0]),
         pltpu.make_async_copy(grads.at[0, 1], up, sems.at[1]),
         pltpu.make_async_copy(grads.at[0, 0], down, sems.at[2]),
-        pltpu.make_async_copy(grads.at[0, 0, :32], down_a, sems.at[3]),
-        pltpu.make_async_copy(grads.at[0, 0, 32:], down_b, sems.at[4]),
+        pltpu.make_async_copy(grads.at[0, 0, :48], down_a, sems.at[3]),
+        pltpu.make_async_copy(grads.at[0, 0, 48:], down_b, sems.at[4]),
     ]
     for copy in copies:
         copy.start()
@@ -292,10 +292,9 @@
 
 
 def body(acts, grads_sent, replicas, master, moment, second):
-    half = ((32, D), BF16)
     w_out, down, down_a, down_b, up = call(
         take_kernel,
-        [((UNITS, D), BF16), ((64, D), BF16), half, half, ((64, D), BF16)],
+        [((UNITS, D), BF16), ((64, D), BF16), ((48, D), BF16), ((16, D), BF16), ((64, D), BF16)],
         grads_sent, replicas, specs=[HBM, HBM],
         scratch=[pltpu.SemaphoreType.DMA((5,))], vmem=58,
     )

time: 116 us -> 115 us (level)
  the two profiles are of different devices: /device:TPU:25 before, /device:TPU:9 now
where the time goes in v8:
time: 115 us
  blocking collectives  46.8 us (41%)
  starting transfers between devices  36.5 us (32%)
  waiting for transfers between devices  22.3 us (19%)
  Pallas kernels  5.65 us (5%)
  local copies, waits for them, and re-layouts  2.67 us (2%)
    all_gather x1, blocking collectives, body(): full = lax.all_gather(shared, NEAR, axis=0, tiled=False)  18.8 us
    all_to_all x1, blocking collectives, body(): lax.all_to_all(spread, FAR, 0, 0, axis_index_groups=far_groups(), tiled=T...  17 us
    all_to_all x1, blocking collectives, body(): near = lax.all_to_all(tiles, 'x', 0, 0, tiled=True)  11 us
    all_to_all x1, waiting for transfers between devices, body(): lax.all_to_all(shared, FAR, 0, 0, axis_index_groups=far_groups(), tiled=T...  9.7 us
    ppermute x1, starting transfers between devices, body(): wrapped = lax.ppermute(sent, SECTION, wrap_route())  9.19 us
    ppermute x1, starting transfers between devices, body(): w_out_moved = lax.ppermute(w_out, FAR, weights_route())  8.13 us
    ppermute x1, waiting for transfers between devices, body(): wrapped = lax.ppermute(sent, SECTION, wrap_route())  6.69 us
    ppermute x4, starting transfers between devices, shifted(): return lax.ppermute(block, SECTION, route)  6.39 us
  transfers between devices with their start and end apart: 9, of which 5 were waited for; matrix products, arithmetic and copies ran while one was open for 2% of the time, Pallas kernels for 1%

profile of v8, /device:TPU:9, one launch (start us, length us, event | category | flops | bytes accessed | tf_op | source)
XLA Modules:
  0.0 114.7 jit_solution(17838933440665096114)
XLA Ops:
  0.6 1.7 %shard_map.93 = (bf16[16,6144]{1,0:T(8,128)(2,1)S(1)}, bf16[64,6144]{1,0:T(8,128)(2,1)S(1)}, bf16[48,6144]{1,0:T(8,128)(2,1)S(1)}, bf16[16,6144]{1,0:T(8,128)(2,1)S(1)}, bf16[64,6144]{1,0:T(8,128)(2,1)S(1)}) custom-call(bf16[1,2,64,6144]{3,2,1,0:T(8,128)(2,1)} %grads.1, bf16[1,2,2,16,6144]{4,3,2,1,0:T(8,128)(2,1)} %weights.5), custom_call_target="tpu_custom_call" | custom-call | tf_op jit(solution)/shard_map/pallas_call | solution.py:76
  2.4 3.6 %collective-permute-start.4 = (bf16[64,6144]{1,0:T(8,128)(2,1)S(1)}, bf16[64,6144]{1,0:T(8,128)(2,1)S(1)}, u32[]{:S(2)}, u32[]{:S(2)}) collective-permute-start(bf16[64,6144]{1,0:T(8,128)(2,1)S(1)} %get-tuple-element.17._.up), channel_id=1, source_target_pairs={{0,16},{16,32},{32,48},{48,64},{64,80},{80,96},{96,112},{128,144},... | collective-permute-start | bytes 2359304 | tf_op jit(solution)/shard_map/ppermute | solution.py:64
  6.0 1.3 %collective-permute-start = (bf16[64,6144]{1,0:T(8,128)(2,1)S(1)}, bf16[64,6144]{1,0:T(8,128)(2,1)S(1)}, u32[]{:S(2)}, u32[]{:S(2)}) collective-permute-start(bf16[64,6144]{1,0:T(8,128)(2,1)S(1)} %shard_map.94._.down), channel_id=1, source_target_pairs={{16,0},{32,16},{48,32},{64,48},{80,64},{96,80},{144,128},{160,144}... | collective-permute-start | bytes 2359304 | tf_op jit(solution)/shard_map/ppermute | solution.py:64
  7.3 8.1 %collective-permute-start.2 = (bf16[16,6144]{1,0:T(8,128)(2,1)S(1)}, bf16[16,6144]{1,0:T(8,128)(2,1)S(1)}, u32[]{:S(2)}, u32[]{:S(2)}) collective-permute-start(bf16[16,6144]{1,0:T(8,128)(2,1)S(1)} %shard_map.95._), channel_id=1, source_target_pairs={{112,136},{120,128},{128,120},{136,112},{240,264},{248,256},{256,2... | collective-permute-start | bytes 589832 | tf_op jit(solution)/shard_map/ppermute | solution.py:305
  15.4 0.0 copy-start
  15.4 0.0 copy-start.1
  15.5 0.8 collective-permute-start.1
  16.3 0.3 copy-done
  16.6 0.5 copy-done.1
  17.1 0.5 shard_map.97.pre_act.value
  17.6 2.4 %collective-permute-done.2.w_out = bf16[16,6144]{1,0:T(8,128)(2,1)S(1)} collective-permute-done((bf16[16,6144]{1,0:T(8,128)(2,1)S(1)}, bf16[16,6144]{1,0:T(8,128)(2,1)S(1)}, u32[]{:S(2)}, u32[]{:S(2)}) %collective-permute-start.2) | collective-permute-done | bytes 196640 | tf_op jit(solution)/shard_map/ppermute | solution.py:305
  20.0 0.3 shard_map.98._
  20.3 9.2 %collective-permute-start.5 = (f32[32,64]{1,0:T(8,128)S(1)}, f32[32,64]{1,0:T(8,128)S(1)}, u32[]{:S(2)}, u32[]{:S(2)}) collective-permute-start(f32[32,64]{1,0:T(8,128)S(1)} %shard_map.98._), channel_id=1, source_target_pairs={{112,128},{128,112},{240,256},{256,240},{368,384},{384,368},{496,0... | collective-permute-start | bytes 24584 | tf_op jit(solution)/shard_map/ppermute | solution.py:313
  29.6 0.7 collective-permute-start.3
  30.3 6.7 %collective-permute-done.5.wrapped = f32[32,64]{1,0:T(8,128)S(1)} collective-permute-done((f32[32,64]{1,0:T(8,128)S(1)}, f32[32,64]{1,0:T(8,128)S(1)}, u32[]{:S(2)}, u32[]{:S(2)}) %collective-permute-start.5) | collective-permute-done | bytes 8224 | tf_op jit(solution)/shard_map/ppermute | solution.py:313
  36.9 0.0 collective-permute-done.3.after_b
  36.9 0.0 collective-permute-done.1.after_a
  37.0 0.0 collective-permute-done.from_after
  37.0 0.0 collective-permute-done.4.from_before
  37.0 1.4 %shard_map.101 = (f32[4,64,768]{2,1,0:T(8,128)S(1)}, bf16[4,64,768]{2,1,0:T(8,128)(2,1)S(1)}) custom-call(bf16[64,6144]{1,0:T(8,128)(2,1)S(1)} %collective-permute-done.from_after, bf16[48,6144]{1,0:T(8,128)(2,1)S(1)} %collective-permute-done.1.after_a, bf16[16,6144]{1,0:T(8,128)(2,1)S(1)} %collective-permute-done.3.after_b, ...), custom_call_target="tpu_custom_call" | custom-call | tf_op jit(solution)/shard_map/pallas_call | solution.py:76
  38.4 5.5 %collective-permute-start.6 = (bf16[4,64,768]{2,1,0:T(8,128)(2,1)S(1)}, bf16[4,64,768]{2,1,0:T(8,128)(2,1)S(1)}, u32[]{:S(2)}, u32[]{:S(2)}) collective-permute-start(bf16[4,64,768]{2,1,0:T(8,128)(2,1)S(1)} %get-tuple-element.23), channel_id=1, source_target_pairs={{0,1},{1,0},{2,3},{3,2},{4,5},{5,4},{6,7},{7,6},{8,9},{9,8},{10,11... | collective-permute-start | bytes 1179656 | tf_op jit(solution)/shard_map/ppermute | solution.py:68
  43.9 1.3 %collective-permute-done.6.arrived = bf16[4,64,768]{2,1,0:T(8,128)(2,1)S(1)} collective-permute-done((bf16[4,64,768]{2,1,0:T(8,128)(2,1)S(1)}, bf16[4,64,768]{2,1,0:T(8,128)(2,1)S(1)}, u32[]{:S(2)}, u32[]{:S(2)}) %collective-permute-start.6) | collective-permute-done | bytes 393248 | tf_op jit(solution)/shard_map/ppermute | solution.py:68
  45.2 0.0 copy-start.2
  45.2 0.0 copy-start.3
  45.2 0.0 copy-start.4
  45.2 0.1 shard_map.102
  45.3 11.0 %all_to_all.15.arrived = bf16[4,64,768]{2,1,0:T(8,128)(2,1)S(1)} all-to-all(bf16[4,64,768]{2,1,0:T(8,128)(2,1)S(1)} %shard_map.102), channel_id=1, replica_groups=mesh['y'=4,'zl'=8,'zh'=2,'x'=4,'c'=2] {'x'}, dimensions={0} | all-to-all | bytes 786432 | tf_op jit(solution)/shard_map/all_to_all | solution.py:326
  56.3 0.1 shard_map.103
  56.4 3.9 %collective-permute-start.7 = (bf16[16,768]{1,0:T(8,128)(2,1)S(1)}, bf16[16,768]{1,0:T(8,128)(2,1)S(1)}, u32[]{:S(2)}, u32[]{:S(2)}) collective-permute-start(bf16[16,768]{1,0:T(8,128)(2,1)S(1)} %get-tuple-element.25), channel_id=1, source_target_pairs={{112,368},{368,112},{128,384},{384,128},{113,369},{369,113},{129,3... | collective-permute-start | bytes 73736 | tf_op jit(solution)/shard_map/ppermute | solution.py:328
  60.3 2.1 %collective-permute-done.7.swap = bf16[16,768]{1,0:T(8,128)(2,1)S(1)} collective-permute-done((bf16[16,768]{1,0:T(8,128)(2,1)S(1)}, bf16[16,768]{1,0:T(8,128)(2,1)S(1)}, u32[]{:S(2)}, u32[]{:S(2)}) %collective-permute-start.7) | collective-permute-done | bytes 24608 | tf_op jit(solution)/shard_map/ppermute | solution.py:328
  62.5 17.0 %all_to_all.16.arrived = bf16[4,2,16,384]{3,2,1,0:T(8,128)(2,1)S(1)} all-to-all(bf16[4,2,16,384]{3,2,1,0:T(8,128)(2,1)S(1)} %shard_map.104), channel_id=1, replica_groups={{0,8,496,504},{16,24,480,488},{32,40,464,472},{48,56,448,456},{64,72,43..., dimensions={0} | all-to-all | bytes 196608 | tf_op jit(solution)/shard_map/all_to_all | solution.py:330
  79.5 0.0 copy-done.2
  79.5 0.0 copy-done.3
  79.5 0.0 copy-done.4
  79.5 0.7 shard_map.105
  80.2 3.3 %all-to-all-start.2 = ((bf16[4,2,16,384]{3,2,1,0:T(8,128)(2,1)}), bf16[4,2,16,384]{3,2,1,0:T(8,128)(2,1)S(1)}, u32[]{:S(2)}, u32[]{:S(2)}) async-start(bf16[4,2,16,384]{3,2,1,0:T(8,128)(2,1)} %get-tuple-element.29), calls=%async_computation.2 | async-start | bytes 196608 | tf_op jit(solution)/shard_map/all_to_all | solution.py:337
  83.5 0.6 copy.20
  84.1 0.6 copy.21
  84.7 0.6 copy.22
  85.4 9.7 %all-to-all-done.2 = bf16[4,2,16,384]{3,2,1,0:T(8,128)(2,1)S(1)} async-done(((bf16[4,2,16,384]{3,2,1,0:T(8,128)(2,1)}), bf16[4,2,16,384]{3,2,1,0:T(8,128)(2,1)S(1)}, u32[]{:S(2)}, u32[]{:S(2)}) %all-to-all-start.2) | async-done | bytes 98336 | tf_op jit(solution)/shard_map/all_to_all | solution.py:337
  95.1 18.8 %all-gather = bf16[32,2,16,384]{3,2,1,0:T(8,128)(2,1)S(1)} all-gather(bf16[4,2,16,384]{3,2,1,0:T(8,128)(2,1)S(1)} %all-to-all-done.2), channel_id=2, replica_groups=mesh['y'=4,'zl'=8,'zh'=2,'x'=4,'c'=2] {'x','c'}, dimensions={0}, use_global_device_ids=true | all-gather | bytes 884736 | tf_op jit(solution)/shard_map/all_gather | solution.py:338
  113.9 0.8 shard_map.106
  (6 shorter events, 0.0 us)
Async XLA Ops:
  2.4 34.6 %collective-permute-start.4 = (bf16[64,6144]{1,0:T(8,128)(2,1)S(1)}, bf16[64,6144]{1,0:T(8,128)(2,1)S(1)}, u32[]{:S(2)}, u32[]{:S(2)}) collective-permute-start(bf16[64,6144]{1,0:T(8,128)(2,1)S(1)} %get-tuple-element.17._.up), channel_id=1, source_target_pairs={{0,16},{16,32},{32,48},{48,64},{64,80},{80,96},{96,112},{128,144},... | collective-permute-start | bytes 2359304 | tf_op jit(solution)/shard_map/ppermute | solution.py:64
  6.0 31.0 %collective-permute-start = (bf16[64,6144]{1,0:T(8,128)(2,1)S(1)}, bf16[64,6144]{1,0:T(8,128)(2,1)S(1)}, u32[]{:S(2)}, u32[]{:S(2)}) collective-permute-start(bf16[64,6144]{1,0:T(8,128)(2,1)S(1)} %shard_map.94._.down), channel_id=1, source_target_pairs={{16,0},{32,16},{48,32},{64,48},{80,64},{96,80},{144,128},{160,144}... | collective-permute-start | bytes 2359304 | tf_op jit(solution)/shard_map/ppermute | solution.py:64
  7.3 12.7 %collective-permute-start.2 = (bf16[16,6144]{1,0:T(8,128)(2,1)S(1)}, bf16[16,6144]{1,0:T(8,128)(2,1)S(1)}, u32[]{:S(2)}, u32[]{:S(2)}) collective-permute-start(bf16[16,6144]{1,0:T(8,128)(2,1)S(1)} %shard_map.95._), channel_id=1, source_target_pairs={{112,136},{120,128},{128,120},{136,112},{240,264},{248,256},{256,2... | collective-permute-start | bytes 589832 | tf_op jit(solution)/shard_map/ppermute | solution.py:305
  15.4 1.1 copy-start
  15.4 1.6 %copy-start.1 = (bf16[1,2,64,6144]{3,2,1,0:T(8,128)(2,1)S(1)}, bf16[1,2,64,6144]{3,2,1,0:T(8,128)(2,1)}, u32[]{:S(2)}) copy-start(bf16[1,2,64,6144]{3,2,1,0:T(8,128)(2,1)} %acts.3) | copy-start | bytes 4718596
  15.5 21.5 %collective-permute-start.1 = (bf16[48,6144]{1,0:T(8,128)(2,1)S(1)}, bf16[48,6144]{1,0:T(8,128)(2,1)S(1)}, u32[]{:S(2)}, u32[]{:S(2)}) collective-permute-start(bf16[48,6144]{1,0:T(8,128)(2,1)S(1)} %shard_map.96), channel_id=1, source_target_pairs={{112,96},{240,224},{368,352},{496,480},{113,97},{241,225},{369,353... | collective-permute-start | bytes 1769480 | tf_op jit(solution)/shard_map/ppermute | solution.py:64
  20.3 16.6 %collective-permute-start.5 = (f32[32,64]{1,0:T(8,128)S(1)}, f32[32,64]{1,0:T(8,128)S(1)}, u32[]{:S(2)}, u32[]{:S(2)}) collective-permute-start(f32[32,64]{1,0:T(8,128)S(1)} %shard_map.98._), channel_id=1, source_target_pairs={{112,128},{128,112},{240,256},{256,240},{368,384},{384,368},{496,0... | collective-permute-start | bytes 24584 | tf_op jit(solution)/shard_map/ppermute | solution.py:313
  29.6 7.4 %collective-permute-start.3 = (bf16[16,6144]{1,0:T(8,128)(2,1)S(1)}, bf16[16,6144]{1,0:T(8,128)(2,1)S(1)}, u32[]{:S(2)}, u32[]{:S(2)}) collective-permute-start(bf16[16,6144]{1,0:T(8,128)(2,1)S(1)} %shard_map.99._), channel_id=1, source_target_pairs={{112,96},{240,224},{368,352},{496,480},{113,97},{241,225},{369,353... | collective-permute-start | bytes 589832 | tf_op jit(solution)/shard_map/ppermute | solution.py:64
  38.4 6.9 %collective-permute-start.6 = (bf16[4,64,768]{2,1,0:T(8,128)(2,1)S(1)}, bf16[4,64,768]{2,1,0:T(8,128)(2,1)S(1)}, u32[]{:S(2)}, u32[]{:S(2)}) collective-permute-start(bf16[4,64,768]{2,1,0:T(8,128)(2,1)S(1)} %get-tuple-element.23), channel_id=1, source_target_pairs={{0,1},{1,0},{2,3},{3,2},{4,5},{5,4},{6,7},{7,6},{8,9},{9,8},{10,11... | collective-permute-start | bytes 1179656 | tf_op jit(solution)/shard_map/ppermute | solution.py:68
  45.2 34.2 %copy-start.2 = (f32[1,2,16,384]{3,2,1,0:T(8,128)S(1)}, f32[1,2,16,384]{3,2,1,0:T(8,128)}, u32[]{:S(2)}) copy-start(f32[1,2,16,384]{3,2,1,0:T(8,128)} %master.1) | copy-start | bytes 147460
  45.2 34.2 %copy-start.3 = (f32[1,2,16,384]{3,2,1,0:T(8,128)S(1)}, f32[1,2,16,384]{3,2,1,0:T(8,128)}, u32[]{:S(2)}) copy-start(f32[1,2,16,384]{3,2,1,0:T(8,128)} %moment.1) | copy-start | bytes 147460
  45.2 34.2 %copy-start.4 = (f32[1,2,16,384]{3,2,1,0:T(8,128)S(1)}, f32[1,2,16,384]{3,2,1,0:T(8,128)}, u32[]{:S(2)}) copy-start(f32[1,2,16,384]{3,2,1,0:T(8,128)} %second.1) | copy-start | bytes 147460
  56.4 6.1 %collective-permute-start.7 = (bf16[16,768]{1,0:T(8,128)(2,1)S(1)}, bf16[16,768]{1,0:T(8,128)(2,1)S(1)}, u32[]{:S(2)}, u32[]{:S(2)}) collective-permute-start(bf16[16,768]{1,0:T(8,128)(2,1)S(1)} %get-tuple-element.25), channel_id=1, source_target_pairs={{112,368},{368,112},{128,384},{384,128},{113,369},{369,113},{129,3... | collective-permute-start | bytes 73736 | tf_op jit(solution)/shard_map/ppermute | solution.py:328
  80.2 14.9 %all-to-all-start.2 = ((bf16[4,2,16,384]{3,2,1,0:T(8,128)(2,1)}), bf16[4,2,16,384]{3,2,1,0:T(8,128)(2,1)S(1)}, u32[]{:S(2)}, u32[]{:S(2)}) async-start(bf16[4,2,16,384]{3,2,1,0:T(8,128)(2,1)} %get-tuple-element.29), calls=%async_computation.2 | async-start | bytes 196608 | tf_op jit(solution)/shard_map/all_to_all | solution.py:337

commit v9 on v8

--- a/solution.py
+++ b/solution.py
@@ -299,12 +299,12 @@
         scratch=[pltpu.SemaphoreType.DMA((5,))], vmem=58,
     )
     from_before = shifted(up, 1, range(7))
-    down = after(up, down, 10**10)
-    from_after = shifted(down, -1, range(1, 7))
-    w_out = after(down, w_out, 10**10)
+    w_out = after(up, w_out, 10**10)
     w_out_moved = lax.ppermute(w_out, FAR, weights_route())
     down_a = after(w_out, down_a, 10**10)
     after_a = shifted(down_a, -1, (7,))
+    down = after(down_a, down, 10**10)
+    from_after = shifted(down, -1, range(1, 7))
     acts, weights = here(acts), here(replicas)
     (pre_act,) = call(forward_kernel, [((2, UNITS, 64), F32)], acts, weights, flops=10**10)
     (sent,) = call(

time: 115 us -> 114 us (level)
  transfers between devices with their start and end apart: 9 -> 9, of which waited for: 5 -> 6; matrix products, arithmetic and copies ran while one was open for 2% -> 2% of each run, Pallas kernels for 1% -> 1%
where the time goes in v9:
time: 114 us; the launch traced here: 113 us
  blocking collectives  46.4 us (41%)
  starting transfers between devices  36.9 us (32%)
  waiting for transfers between devices  21.6 us (19%)
  Pallas kernels  5.64 us (5%)
  local copies, waits for them, and re-layouts  2.06 us (2%)
    all_gather x1, blocking collectives, body(): full = lax.all_gather(shared, NEAR, axis=0, tiled=False)  18.3 us
    all_to_all x1, blocking collectives, body(): lax.all_to_all(spread, FAR, 0, 0, axis_index_groups=far_groups(), tiled=T...  17.1 us
    all_to_all x1, blocking collectives, body(): near = lax.all_to_all(tiles, 'x', 0, 0, tiled=True)  11 us
    all_to_all x1, waiting for transfers between devices, body(): lax.all_to_all(shared, FAR, 0, 0, axis_index_groups=far_groups(), tiled=T...  9.74 us
    ppermute x1, starting transfers between devices, body(): w_out_moved = lax.ppermute(w_out, FAR, weights_route())  8.71 us
    ppermute x1, starting transfers between devices, body(): wrapped = lax.ppermute(sent, SECTION, wrap_route())  8.61 us
    ppermute x1, waiting for transfers between devices, body(): wrapped = lax.ppermute(sent, SECTION, wrap_route())  6.54 us
    ppermute x4, starting transfers between devices, shifted(): return lax.ppermute(block, SECTION, route)  6.39 us
  transfers between devices with their start and end apart: 9, of which 6 were waited for; matrix products, arithmetic and copies ran while one was open for 2% of the time, Pallas kernels for 1%

profile of v9, /device:TPU:9, one launch (start us, length us, event | category | flops | bytes accessed | tf_op | source)
XLA Modules:
  0.0 113.4 jit_solution(9032826832203177057)
XLA Ops:
  0.6 1.7 %shard_map.93 = (bf16[16,6144]{1,0:T(8,128)(2,1)S(1)}, bf16[64,6144]{1,0:T(8,128)(2,1)S(1)}, bf16[48,6144]{1,0:T(8,128)(2,1)S(1)}, bf16[16,6144]{1,0:T(8,128)(2,1)S(1)}, bf16[64,6144]{1,0:T(8,128)(2,1)S(1)}) custom-call(bf16[1,2,64,6144]{3,2,1,0:T(8,128)(2,1)} %grads.1, bf16[1,2,2,16,6144]{4,3,2,1,0:T(8,128)(2,1)} %weights.5), custom_call_target="tpu_custom_call" | custom-call | tf_op jit(solution)/shard_map/pallas_call | solution.py:76
  2.4 3.6 %collective-permute-start.4 = (bf16[64,6144]{1,0:T(8,128)(2,1)S(1)}, bf16[64,6144]{1,0:T(8,128)(2,1)S(1)}, u32[]{:S(2)}, u32[]{:S(2)}) collective-permute-start(bf16[64,6144]{1,0:T(8,128)(2,1)S(1)} %get-tuple-element.17._.up), channel_id=1, source_target_pairs={{0,16},{16,32},{32,48},{48,64},{64,80},{80,96},{96,112},{128,144},... | collective-permute-start | bytes 2359304 | tf_op jit(solution)/shard_map/ppermute | solution.py:64
  6.0 8.7 %collective-permute-start.2 = (bf16[16,6144]{1,0:T(8,128)(2,1)S(1)}, bf16[16,6144]{1,0:T(8,128)(2,1)S(1)}, u32[]{:S(2)}, u32[]{:S(2)}) collective-permute-start(bf16[16,6144]{1,0:T(8,128)(2,1)S(1)} %shard_map.94._), channel_id=1, source_target_pairs={{112,136},{120,128},{128,120},{136,112},{240,264},{248,256},{256,2... | collective-permute-start | bytes 589832 | tf_op jit(solution)/shard_map/ppermute | solution.py:303
  14.7 0.7 collective-permute-start.1
  15.4 0.0 copy-start
  15.4 0.0 copy-start.1
  15.5 1.4 %collective-permute-start = (bf16[64,6144]{1,0:T(8,128)(2,1)S(1)}, bf16[64,6144]{1,0:T(8,128)(2,1)S(1)}, u32[]{:S(2)}, u32[]{:S(2)}) collective-permute-start(bf16[64,6144]{1,0:T(8,128)(2,1)S(1)} %shard_map.96.down), channel_id=1, source_target_pairs={{16,0},{32,16},{48,32},{64,48},{80,64},{96,80},{144,128},{160,144}... | collective-permute-start | bytes 2359304 | tf_op jit(solution)/shard_map/ppermute | solution.py:64
  16.9 0.0 copy-done
  16.9 0.2 copy-done.1
  17.1 0.5 shard_map.97.pre_act.value
  17.6 1.7 %collective-permute-done.2.w_out = bf16[16,6144]{1,0:T(8,128)(2,1)S(1)} collective-permute-done((bf16[16,6144]{1,0:T(8,128)(2,1)S(1)}, bf16[16,6144]{1,0:T(8,128)(2,1)S(1)}, u32[]{:S(2)}, u32[]{:S(2)}) %collective-permute-start.2) | collective-permute-done | bytes 196640 | tf_op jit(solution)/shard_map/ppermute | solution.py:303
  19.3 0.3 shard_map.98._
  19.6 8.6 %collective-permute-start.5 = (f32[32,64]{1,0:T(8,128)S(1)}, f32[32,64]{1,0:T(8,128)S(1)}, u32[]{:S(2)}, u32[]{:S(2)}) collective-permute-start(f32[32,64]{1,0:T(8,128)S(1)} %shard_map.98._), channel_id=1, source_target_pairs={{112,128},{128,112},{240,256},{256,240},{368,384},{384,368},{496,0... | collective-permute-start | bytes 24584 | tf_op jit(solution)/shard_map/ppermute | solution.py:313
  28.3 0.7 collective-permute-start.3
  28.9 6.5 %collective-permute-done.5.wrapped = f32[32,64]{1,0:T(8,128)S(1)} collective-permute-done((f32[32,64]{1,0:T(8,128)S(1)}, f32[32,64]{1,0:T(8,128)S(1)}, u32[]{:S(2)}, u32[]{:S(2)}) %collective-permute-start.5) | collective-permute-done | bytes 8224 | tf_op jit(solution)/shard_map/ppermute | solution.py:313
  35.5 0.0 collective-permute-done.3.after_b
  35.5 0.0 collective-permute-done.1.after_a
  35.5 0.1 collective-permute-done.from_after
  35.6 0.0 collective-permute-done.4.from_before
  35.6 1.4 %shard_map.101 = (f32[4,64,768]{2,1,0:T(8,128)S(1)}, bf16[4,64,768]{2,1,0:T(8,128)(2,1)S(1)}) custom-call(bf16[64,6144]{1,0:T(8,128)(2,1)S(1)} %collective-permute-done.from_after, bf16[48,6144]{1,0:T(8,128)(2,1)S(1)} %collective-permute-done.1.after_a, bf16[16,6144]{1,0:T(8,128)(2,1)S(1)} %collective-permute-done.3.after_b, ...), custom_call_target="tpu_custom_call" | custom-call | tf_op jit(solution)/shard_map/pallas_call | solution.py:76
  37.0 5.5 %collective-permute-start.6 = (bf16[4,64,768]{2,1,0:T(8,128)(2,1)S(1)}, bf16[4,64,768]{2,1,0:T(8,128)(2,1)S(1)}, u32[]{:S(2)}, u32[]{:S(2)}) collective-permute-start(bf16[4,64,768]{2,1,0:T(8,128)(2,1)S(1)} %get-tuple-element.23), channel_id=1, source_target_pairs={{0,1},{1,0},{2,3},{3,2},{4,5},{5,4},{6,7},{7,6},{8,9},{9,8},{10,11... | collective-permute-start | bytes 1179656 | tf_op jit(solution)/shard_map/ppermute | solution.py:68
  42.4 1.3 %collective-permute-done.6.arrived = bf16[4,64,768]{2,1,0:T(8,128)(2,1)S(1)} collective-permute-done((bf16[4,64,768]{2,1,0:T(8,128)(2,1)S(1)}, bf16[4,64,768]{2,1,0:T(8,128)(2,1)S(1)}, u32[]{:S(2)}, u32[]{:S(2)}) %collective-permute-start.6) | collective-permute-done | bytes 393248 | tf_op jit(solution)/shard_map/ppermute | solution.py:68
  43.8 0.0 copy-start.2
  43.8 0.0 copy-start.3
  43.8 0.0 copy-start.4
  43.8 0.1 shard_map.102
  43.9 11.0 %all_to_all.15.arrived = bf16[4,64,768]{2,1,0:T(8,128)(2,1)S(1)} all-to-all(bf16[4,64,768]{2,1,0:T(8,128)(2,1)S(1)} %shard_map.102), channel_id=1, replica_groups=mesh['y'=4,'zl'=8,'zh'=2,'x'=4,'c'=2] {'x'}, dimensions={0} | all-to-all | bytes 786432 | tf_op jit(solution)/shard_map/all_to_all | solution.py:326
  54.9 0.1 shard_map.103
  54.9 3.9 %collective-permute-start.7 = (bf16[16,768]{1,0:T(8,128)(2,1)S(1)}, bf16[16,768]{1,0:T(8,128)(2,1)S(1)}, u32[]{:S(2)}, u32[]{:S(2)}) collective-permute-start(bf16[16,768]{1,0:T(8,128)(2,1)S(1)} %get-tuple-element.25), channel_id=1, source_target_pairs={{112,368},{368,112},{128,384},{384,128},{113,369},{369,113},{129,3... | collective-permute-start | bytes 73736 | tf_op jit(solution)/shard_map/ppermute | solution.py:328
  58.9 2.1 %collective-permute-done.7.swap = bf16[16,768]{1,0:T(8,128)(2,1)S(1)} collective-permute-done((bf16[16,768]{1,0:T(8,128)(2,1)S(1)}, bf16[16,768]{1,0:T(8,128)(2,1)S(1)}, u32[]{:S(2)}, u32[]{:S(2)}) %collective-permute-start.7) | collective-permute-done | bytes 24608 | tf_op jit(solution)/shard_map/ppermute | solution.py:328
  61.0 17.1 %all_to_all.16.arrived = bf16[4,2,16,384]{3,2,1,0:T(8,128)(2,1)S(1)} all-to-all(bf16[4,2,16,384]{3,2,1,0:T(8,128)(2,1)S(1)} %shard_map.104), channel_id=1, replica_groups={{0,8,496,504},{16,24,480,488},{32,40,464,472},{48,56,448,456},{64,72,43..., dimensions={0} | all-to-all | bytes 196608 | tf_op jit(solution)/shard_map/all_to_all | solution.py:330
  78.2 0.0 copy-done.2
  78.2 0.0 copy-done.3
  78.2 0.0 copy-done.4
  78.2 0.7 shard_map.105
  78.9 3.9 %all-to-all-start.2 = ((bf16[4,2,16,384]{3,2,1,0:T(8,128)(2,1)}), bf16[4,2,16,384]{3,2,1,0:T(8,128)(2,1)S(1)}, u32[]{:S(2)}, u32[]{:S(2)}) async-start(bf16[4,2,16,384]{3,2,1,0:T(8,128)(2,1)} %get-tuple-element.29), calls=%async_computation.2 | async-start | bytes 196608 | tf_op jit(solution)/shard_map/all_to_all | solution.py:337
  82.7 0.6 copy.20
  83.4 0.6 copy.21
  84.0 0.6 copy.22
  84.6 9.7 %all-to-all-done.2 = bf16[4,2,16,384]{3,2,1,0:T(8,128)(2,1)S(1)} async-done(((bf16[4,2,16,384]{3,2,1,0:T(8,128)(2,1)}), bf16[4,2,16,384]{3,2,1,0:T(8,128)(2,1)S(1)}, u32[]{:S(2)}, u32[]{:S(2)}) %all-to-all-start.2) | async-done | bytes 98336 | tf_op jit(solution)/shard_map/all_to_all | solution.py:337
  94.3 18.3 %all-gather = bf16[32,2,16,384]{3,2,1,0:T(8,128)(2,1)S(1)} all-gather(bf16[4,2,16,384]{3,2,1,0:T(8,128)(2,1)S(1)} %all-to-all-done.2), channel_id=2, replica_groups=mesh['y'=4,'zl'=8,'zh'=2,'x'=4,'c'=2] {'x','c'}, dimensions={0}, use_global_device_ids=true | all-gather | bytes 884736 | tf_op jit(solution)/shard_map/all_gather | solution.py:338
  112.6 0.8 shard_map.106
  (6 shorter events, 0.0 us)
Async XLA Ops:
  2.4 33.2 %collective-permute-start.4 = (bf16[64,6144]{1,0:T(8,128)(2,1)S(1)}, bf16[64,6144]{1,0:T(8,128)(2,1)S(1)}, u32[]{:S(2)}, u32[]{:S(2)}) collective-permute-start(bf16[64,6144]{1,0:T(8,128)(2,1)S(1)} %get-tuple-element.17._.up), channel_id=1, source_target_pairs={{0,16},{16,32},{32,48},{48,64},{64,80},{80,96},{96,112},{128,144},... | collective-permute-start | bytes 2359304 | tf_op jit(solution)/shard_map/ppermute | solution.py:64
  6.0 13.3 %collective-permute-start.2 = (bf16[16,6144]{1,0:T(8,128)(2,1)S(1)}, bf16[16,6144]{1,0:T(8,128)(2,1)S(1)}, u32[]{:S(2)}, u32[]{:S(2)}) collective-permute-start(bf16[16,6144]{1,0:T(8,128)(2,1)S(1)} %shard_map.94._), channel_id=1, source_target_pairs={{112,136},{120,128},{128,120},{136,112},{240,264},{248,256},{256,2... | collective-permute-start | bytes 589832 | tf_op jit(solution)/shard_map/ppermute | solution.py:303
  14.7 20.8 %collective-permute-start.1 = (bf16[48,6144]{1,0:T(8,128)(2,1)S(1)}, bf16[48,6144]{1,0:T(8,128)(2,1)S(1)}, u32[]{:S(2)}, u32[]{:S(2)}) collective-permute-start(bf16[48,6144]{1,0:T(8,128)(2,1)S(1)} %shard_map.95._), channel_id=1, source_target_pairs={{112,96},{240,224},{368,352},{496,480},{113,97},{241,225},{369,353... | collective-permute-start | bytes 1769480 | tf_op jit(solution)/shard_map/ppermute | solution.py:64
  15.4 1.5 %copy-start = (bf16[1,2,2,16,6144]{4,3,2,1,0:T(8,128)(2,1)S(1)}, bf16[1,2,2,16,6144]{4,3,2,1,0:T(8,128)(2,1)}, u32[]{:S(2)}) copy-start(bf16[1,2,2,16,6144]{4,3,2,1,0:T(8,128)(2,1)} %weights.5) | copy-start | bytes 2359300
  15.4 1.6 %copy-start.1 = (bf16[1,2,64,6144]{3,2,1,0:T(8,128)(2,1)S(1)}, bf16[1,2,64,6144]{3,2,1,0:T(8,128)(2,1)}, u32[]{:S(2)}) copy-start(bf16[1,2,64,6144]{3,2,1,0:T(8,128)(2,1)} %acts.3) | copy-start | bytes 4718596
  15.5 20.1 %collective-permute-start = (bf16[64,6144]{1,0:T(8,128)(2,1)S(1)}, bf16[64,6144]{1,0:T(8,128)(2,1)S(1)}, u32[]{:S(2)}, u32[]{:S(2)}) collective-permute-start(bf16[64,6144]{1,0:T(8,128)(2,1)S(1)} %shard_map.96.down), channel_id=1, source_target_pairs={{16,0},{32,16},{48,32},{64,48},{80,64},{96,80},{144,128},{160,144}... | collective-permute-start | bytes 2359304 | tf_op jit(solution)/shard_map/ppermute | solution.py:64
  19.6 15.9 %collective-permute-start.5 = (f32[32,64]{1,0:T(8,128)S(1)}, f32[32,64]{1,0:T(8,128)S(1)}, u32[]{:S(2)}, u32[]{:S(2)}) collective-permute-start(f32[32,64]{1,0:T(8,128)S(1)} %shard_map.98._), channel_id=1, source_target_pairs={{112,128},{128,112},{240,256},{256,240},{368,384},{384,368},{496,0... | collective-permute-start | bytes 24584 | tf_op jit(solution)/shard_map/ppermute | solution.py:313
  28.3 7.2 %collective-permute-start.3 = (bf16[16,6144]{1,0:T(8,128)(2,1)S(1)}, bf16[16,6144]{1,0:T(8,128)(2,1)S(1)}, u32[]{:S(2)}, u32[]{:S(2)}) collective-permute-start(bf16[16,6144]{1,0:T(8,128)(2,1)S(1)} %shard_map.99._), channel_id=1, source_target_pairs={{112,96},{240,224},{368,352},{496,480},{113,97},{241,225},{369,353... | collective-permute-start | bytes 589832 | tf_op jit(solution)/shard_map/ppermute | solution.py:64
  37.0 6.8 %collective-permute-start.6 = (bf16[4,64,768]{2,1,0:T(8,128)(2,1)S(1)}, bf16[4,64,768]{2,1,0:T(8,128)(2,1)S(1)}, u32[]{:S(2)}, u32[]{:S(2)}) collective-permute-start(bf16[4,64,768]{2,1,0:T(8,128)(2,1)S(1)} %get-tuple-element.23), channel_id=1, source_target_pairs={{0,1},{1,0},{2,3},{3,2},{4,5},{5,4},{6,7},{7,6},{8,9},{9,8},{10,11... | collective-permute-start | bytes 1179656 | tf_op jit(solution)/shard_map/ppermute | solution.py:68
  43.8 34.4 %copy-start.2 = (f32[1,2,16,384]{3,2,1,0:T(8,128)S(1)}, f32[1,2,16,384]{3,2,1,0:T(8,128)}, u32[]{:S(2)}) copy-start(f32[1,2,16,384]{3,2,1,0:T(8,128)} %master.1) | copy-start | bytes 147460
  43.8 34.4 %copy-start.3 = (f32[1,2,16,384]{3,2,1,0:T(8,128)S(1)}, f32[1,2,16,384]{3,2,1,0:T(8,128)}, u32[]{:S(2)}) copy-start(f32[1,2,16,384]{3,2,1,0:T(8,128)} %moment.1) | copy-start | bytes 147460
  43.8 34.4 %copy-start.4 = (f32[1,2,16,384]{3,2,1,0:T(8,128)S(1)}, f32[1,2,16,384]{3,2,1,0:T(8,128)}, u32[]{:S(2)}) copy-start(f32[1,2,16,384]{3,2,1,0:T(8,128)} %second.1) | copy-start | bytes 147460
  54.9 6.1 %collective-permute-start.7 = (bf16[16,768]{1,0:T(8,128)(2,1)S(1)}, bf16[16,768]{1,0:T(8,128)(2,1)S(1)}, u32[]{:S(2)}, u32[]{:S(2)}) collective-permute-start(bf16[16,768]{1,0:T(8,128)(2,1)S(1)} %get-tuple-element.25), channel_id=1, source_target_pairs={{112,368},{368,112},{128,384},{384,128},{113,369},{369,113},{129,3... | collective-permute-start | bytes 73736 | tf_op jit(solution)/shard_map/ppermute | solution.py:328
  78.9 15.5 %all-to-all-start.2 = ((bf16[4,2,16,384]{3,2,1,0:T(8,128)(2,1)}), bf16[4,2,16,384]{3,2,1,0:T(8,128)(2,1)S(1)}, u32[]{:S(2)}, u32[]{:S(2)}) async-start(bf16[4,2,16,384]{3,2,1,0:T(8,128)(2,1)} %get-tuple-element.29), calls=%async_computation.2 | async-start | bytes 196608 | tf_op jit(solution)/shard_map/all_to_all | solution.py:337

commit v10 on v9

--- a/solution.py
+++ b/solution.py
@@ -22,7 +22,6 @@
 
 SECTION = ("y", "zl")
 DP = ("zh", "x", "c")
-NEAR = ("x", "c")
 FAR = ("y", "zl", "zh")
 
 ANY = pl.BlockSpec(memory_space=pl.ANY)
@@ -64,8 +63,8 @@
     return lax.ppermute(block, SECTION, route)
 
 
-def swap_cores(block):
-    return lax.ppermute(block, "c", [(0, 1), (1, 0)])
+def both_cores(block):
+    return lax.all_gather(block, "c", axis=0, tiled=False)
 
 
 def here(array):
@@ -210,7 +209,8 @@
 
 
 def merge_kernel(keep, arrived, out):
-    out[...] = (keep[...] + arrived[...].astype(F32)).astype(BF16)
+    other = arrived[1 - lax.axis_index("c")]
+    out[...] = (keep[...] + other.astype(F32)).astype(BF16)
 
 
 def near_kernel(arrived, total, swap):
@@ -282,7 +282,7 @@
                 for p in range(2):
                     copies.append(
                         pltpu.make_async_copy(
-                            full.at[near, 2 * p + zh, sec], out.at[0, c, p, :, pl.ds(at, 384)], sem
+                            full.at[near % 2, near // 2, 2 * p + zh, sec], out.at[0, c, p, :, pl.ds(at, 384)], sem
                         )
                     )
     for copy in copies:
@@ -321,7 +321,7 @@
         acts, weights, pre_act, down, up,
         scratch=[pltpu.VMEM((UNITS, 64), F32), pltpu.VMEM((UNITS, 64), F32)],
     )
-    arrived = swap_cores(send)
+    arrived = both_cores(send)
     (tiles,) = call(merge_kernel, [((4, 64, 768), BF16)], keep, here(arrived))
     near = lax.all_to_all(tiles, "x", 0, 0, tiled=True)
     total, swap = call(near_kernel, [((64, 768), BF16), ((UNITS, 768), BF16)], here(near))
@@ -335,7 +335,8 @@
         here(far), here(master), here(moment), here(second),
     )
     shared = lax.all_to_all(shared, FAR, 0, 0, axis_index_groups=far_groups(), tiled=True)
-    full = lax.all_gather(shared, NEAR, axis=0, tiled=False)
+    copies = jnp.broadcast_to(shared[None], (4, *shared.shape))
+    full = both_cores(lax.all_to_all(copies, "x", 0, 0, tiled=True))
     (new_replicas,) = call(
         finish_kernel,
         [jax.ShapeDtypeStruct((1, 2, 2, UNITS, D), BF16)],

time: 114 us -> 112 us (0.982)
  blocking collectives: 46.4 us -> 56.8 us
  waiting for transfers between devices: 21.6 us -> 14.9 us
  starting transfers between devices: 36.9 us -> 31.1 us
    all_to_all x0 -> x1, blocking collectives: none -> 15.3 us  [body(): lax.all_to_all(shared, FAR, 0, 0, axis_index_groups=far_groups(), tiled=T...]
    ppermute x1 -> x0, starting transfers between devices: 5.45 us -> none  [swap_cores(): return lax.ppermute(block, 'c', [(0, 1), (1, 0)])]
    all_to_all x1, waiting for transfers between devices: 9.74 us -> 4.33 us  [body(): full = both_cores(lax.all_to_all(copies, 'x', 0, 0, tiled=True))]
    all_gather x1 -> x2, blocking collectives: 18.3 us -> 13.4 us  [both_cores(): return lax.all_gather(block, 'c', axis=0, tiled=False)]
    ppermute x1 -> x0, waiting for transfers between devices: 1.33 us -> none  [swap_cores(): return lax.ppermute(block, 'c', [(0, 1), (1, 0)])]
  transfers between devices with their start and end apart: 9 -> 8, of which waited for: 6 -> 5; matrix products, arithmetic and copies ran while one was open for 2% -> 2% of each run, Pallas kernels for 1% -> 1%
where the time goes in v10:
time: 112 us; the launch traced here: 111 us
  blocking collectives  56.8 us (51%)
  starting transfers between devices  31.1 us (28%)
  waiting for transfers between devices  14.9 us (13%)
  Pallas kernels  5 us (4%)
  local copies, waits for them, and re-layouts  2.85 us (3%)
    all_to_all x1, blocking collectives, body(): lax.all_to_all(spread, FAR, 0, 0, axis_index_groups=far_groups(), tiled=T...  17.1 us
    all_to_all x1, blocking collectives, body(): lax.all_to_all(shared, FAR, 0, 0, axis_index_groups=far_groups(), tiled=T...  15.3 us
    all_gather x2, blocking collectives, both_cores(): return lax.all_gather(block, 'c', axis=0, tiled=False)  13.4 us
    all_to_all x1, blocking collectives, body(): near = lax.all_to_all(tiles, 'x', 0, 0, tiled=True)  11 us
    ppermute x1, starting transfers between devices, body(): w_out_moved = lax.ppermute(w_out, FAR, weights_route())  8.71 us
    ppermute x1, starting transfers between devices, body(): wrapped = lax.ppermute(sent, SECTION, wrap_route())  8.61 us
    ppermute x1, waiting for transfers between devices, body(): wrapped = lax.ppermute(sent, SECTION, wrap_route())  6.54 us
    ppermute x4, starting transfers between devices, shifted(): return lax.ppermute(block, SECTION, route)  6.39 us
  transfers between devices with their start and end apart: 8, of which 5 were waited for; matrix products, arithmetic and copies ran while one was open for 2% of the time, Pallas kernels for 1%

profile of v10, /device:TPU:9, one launch (start us, length us, event | category | flops | bytes accessed | tf_op | source)
XLA Modules:
  0.0 111.4 jit_solution(6183713310085305321)
XLA Ops:
  0.6 1.7 %shard_map.93 = (bf16[16,6144]{1,0:T(8,128)(2,1)S(1)}, bf16[64,6144]{1,0:T(8,128)(2,1)S(1)}, bf16[48,6144]{1,0:T(8,128)(2,1)S(1)}, bf16[16,6144]{1,0:T(8,128)(2,1)S(1)}, bf16[64,6144]{1,0:T(8,128)(2,1)S(1)}) custom-call(bf16[1,2,64,6144]{3,2,1,0:T(8,128)(2,1)} %grads.1, bf16[1,2,2,16,6144]{4,3,2,1,0:T(8,128)(2,1)} %weights.5), custom_call_target="tpu_custom_call" | custom-call | tf_op jit(solution)/shard_map/pallas_call | solution.py:75
  2.4 3.6 %collective-permute-start.4 = (bf16[64,6144]{1,0:T(8,128)(2,1)S(1)}, bf16[64,6144]{1,0:T(8,128)(2,1)S(1)}, u32[]{:S(2)}, u32[]{:S(2)}) collective-permute-start(bf16[64,6144]{1,0:T(8,128)(2,1)S(1)} %get-tuple-element.17._.up), channel_id=1, source_target_pairs={{0,16},{16,32},{32,48},{48,64},{64,80},{80,96},{96,112},{128,144},... | collective-permute-start | bytes 2359304 | tf_op jit(solution)/shard_map/ppermute | solution.py:63
  6.0 8.7 %collective-permute-start.2 = (bf16[16,6144]{1,0:T(8,128)(2,1)S(1)}, bf16[16,6144]{1,0:T(8,128)(2,1)S(1)}, u32[]{:S(2)}, u32[]{:S(2)}) collective-permute-start(bf16[16,6144]{1,0:T(8,128)(2,1)S(1)} %shard_map.94._), channel_id=1, source_target_pairs={{112,136},{120,128},{128,120},{136,112},{240,264},{248,256},{256,2... | collective-permute-start | bytes 589832 | tf_op jit(solution)/shard_map/ppermute | solution.py:303
  14.7 0.7 collective-permute-start.1
  15.4 0.0 copy-start
  15.4 0.0 copy-start.1
  15.5 1.4 %collective-permute-start = (bf16[64,6144]{1,0:T(8,128)(2,1)S(1)}, bf16[64,6144]{1,0:T(8,128)(2,1)S(1)}, u32[]{:S(2)}, u32[]{:S(2)}) collective-permute-start(bf16[64,6144]{1,0:T(8,128)(2,1)S(1)} %shard_map.96.down), channel_id=1, source_target_pairs={{16,0},{32,16},{48,32},{64,48},{80,64},{96,80},{144,128},{160,144}... | collective-permute-start | bytes 2359304 | tf_op jit(solution)/shard_map/ppermute | solution.py:63
  16.9 0.0 copy-done
  16.9 0.2 copy-done.1
  17.1 0.5 shard_map.97.pre_act.value
  17.6 1.7 %collective-permute-done.2.w_out = bf16[16,6144]{1,0:T(8,128)(2,1)S(1)} collective-permute-done((bf16[16,6144]{1,0:T(8,128)(2,1)S(1)}, bf16[16,6144]{1,0:T(8,128)(2,1)S(1)}, u32[]{:S(2)}, u32[]{:S(2)}) %collective-permute-start.2) | collective-permute-done | bytes 196640 | tf_op jit(solution)/shard_map/ppermute | solution.py:303
  19.3 0.3 shard_map.98._
  19.6 8.6 %collective-permute-start.5 = (f32[32,64]{1,0:T(8,128)S(1)}, f32[32,64]{1,0:T(8,128)S(1)}, u32[]{:S(2)}, u32[]{:S(2)}) collective-permute-start(f32[32,64]{1,0:T(8,128)S(1)} %shard_map.98._), channel_id=1, source_target_pairs={{112,128},{128,112},{240,256},{256,240},{368,384},{384,368},{496,0... | collective-permute-start | bytes 24584 | tf_op jit(solution)/shard_map/ppermute | solution.py:313
  28.3 0.7 collective-permute-start.3
  28.9 6.5 %collective-permute-done.5.wrapped = f32[32,64]{1,0:T(8,128)S(1)} collective-permute-done((f32[32,64]{1,0:T(8,128)S(1)}, f32[32,64]{1,0:T(8,128)S(1)}, u32[]{:S(2)}, u32[]{:S(2)}) %collective-permute-start.5) | collective-permute-done | bytes 8224 | tf_op jit(solution)/shard_map/ppermute | solution.py:313
  35.5 0.0 collective-permute-done.3.after_b
  35.5 0.0 collective-permute-done.1.after_a
  35.5 0.1 collective-permute-done.from_after
  35.6 0.0 collective-permute-done.4.from_before
  35.6 1.4 %shard_map.101 = (f32[4,64,768]{2,1,0:T(8,128)S(1)}, bf16[4,64,768]{2,1,0:T(8,128)(2,1)S(1)}) custom-call(bf16[64,6144]{1,0:T(8,128)(2,1)S(1)} %collective-permute-done.from_after, bf16[48,6144]{1,0:T(8,128)(2,1)S(1)} %collective-permute-done.1.after_a, bf16[16,6144]{1,0:T(8,128)(2,1)S(1)} %collective-permute-done.3.after_b, ...), custom_call_target="tpu_custom_call" | custom-call | tf_op jit(solution)/shard_map/pallas_call | solution.py:75
  37.0 5.5 %all-gather = bf16[8,64,768]{2,1,0:T(8,128)(2,1)S(1)} all-gather(bf16[4,64,768]{2,1,0:T(8,128)(2,1)S(1)} %get-tuple-element.23), channel_id=2, replica_groups=mesh['y'=4,'zl'=8,'zh'=2,'x'=4,'c'=2] {'c'}, dimensions={0}, use_global_device_ids=true | all-gather | bytes 1179648 | tf_op jit(solution)/shard_map/all_gather | solution.py:67
  42.5 0.0 copy-start.2
  42.5 0.0 copy-start.3
  42.5 0.0 copy-start.4
  42.5 0.1 shard_map.102
  42.6 11.0 %all_to_all.20.arrived = bf16[4,64,768]{2,1,0:T(8,128)(2,1)S(1)} all-to-all(bf16[4,64,768]{2,1,0:T(8,128)(2,1)S(1)} %shard_map.102), channel_id=1, replica_groups=mesh['y'=4,'zl'=8,'zh'=2,'x'=4,'c'=2] {'x'}, dimensions={0} | all-to-all | bytes 786432 | tf_op jit(solution)/shard_map/all_to_all | solution.py:326
  53.6 0.1 shard_map.103
  53.7 3.9 %collective-permute-start.6 = (bf16[16,768]{1,0:T(8,128)(2,1)S(1)}, bf16[16,768]{1,0:T(8,128)(2,1)S(1)}, u32[]{:S(2)}, u32[]{:S(2)}) collective-permute-start(bf16[16,768]{1,0:T(8,128)(2,1)S(1)} %get-tuple-element.25), channel_id=1, source_target_pairs={{112,368},{368,112},{128,384},{384,128},{113,369},{369,113},{129,3... | collective-permute-start | bytes 73736 | tf_op jit(solution)/shard_map/ppermute | solution.py:328
  57.6 2.1 %collective-permute-done.6.swap = bf16[16,768]{1,0:T(8,128)(2,1)S(1)} collective-permute-done((bf16[16,768]{1,0:T(8,128)(2,1)S(1)}, bf16[16,768]{1,0:T(8,128)(2,1)S(1)}, u32[]{:S(2)}, u32[]{:S(2)}) %collective-permute-start.6) | collective-permute-done | bytes 24608 | tf_op jit(solution)/shard_map/ppermute | solution.py:328
  59.8 17.1 %all_to_all.21.arrived = bf16[4,2,16,384]{3,2,1,0:T(8,128)(2,1)S(1)} all-to-all(bf16[4,2,16,384]{3,2,1,0:T(8,128)(2,1)S(1)} %shard_map.104), channel_id=1, replica_groups={{0,8,496,504},{16,24,480,488},{32,40,464,472},{48,56,448,456},{64,72,43..., dimensions={0} | all-to-all | bytes 196608 | tf_op jit(solution)/shard_map/all_to_all | solution.py:330
  76.9 0.0 copy-done.2
  76.9 0.0 copy-done.3
  76.9 0.0 copy-done.4
  76.9 0.1 shard_map.105
  77.0 15.3 %all_to_all.22 = bf16[4,2,16,384]{3,2,1,0:T(8,128)(2,1)S(1)} all-to-all(bf16[4,2,16,384]{3,2,1,0:T(8,128)(2,1)S(1)} %get-tuple-element.29), channel_id=1, replica_groups={{0,8,496,504},{16,24,480,488},{32,40,464,472},{48,56,448,456},{64,72,43..., dimensions={0} | all-to-all | bytes 196608 | tf_op jit(solution)/shard_map/all_to_all | solution.py:337
  92.3 0.8 broadcast_in_dim.2
  93.1 3.5 %all-to-all-start.3 = ((bf16[4,4,2,16,384]{4,3,2,1,0:T(8,128)(2,1)}), bf16[4,4,2,16,384]{4,3,2,1,0:T(8,128)(2,1)S(1)}, u32[]{:S(2)}, u32[]{:S(2)}) async-start(bf16[4,4,2,16,384]{4,3,2,1,0:T(8,128)(2,1)} %broadcast_in_dim.2), calls=%async_computation.3 | async-start | bytes 786432 | tf_op jit(solution)/shard_map/all_to_all | solution.py:339
  96.5 0.6 copy.20
  97.1 0.6 copy.21
  97.8 0.6 copy.22
  98.4 4.3 %all-to-all-done.3 = bf16[4,4,2,16,384]{4,3,2,1,0:T(8,128)(2,1)S(1)} async-done(((bf16[4,4,2,16,384]{4,3,2,1,0:T(8,128)(2,1)}), bf16[4,4,2,16,384]{4,3,2,1,0:T(8,128)(2,1)S(1)}, u32[]{:S(2)}, u32[]{:S(2)}) %all-to-all-start.3) | async-done | bytes 393248 | tf_op jit(solution)/shard_map/all_to_all | solution.py:339
  102.7 7.8 %all-gather.1 = bf16[8,4,2,16,384]{4,3,2,1,0:T(8,128)(2,1)S(1)} all-gather(bf16[4,4,2,16,384]{4,3,2,1,0:T(8,128)(2,1)S(1)} %all-to-all-done.3), channel_id=3, replica_groups=mesh['y'=4,'zl'=8,'zh'=2,'x'=4,'c'=2] {'c'}, dimensions={0}, use_global_device_ids=true | all-gather | bytes 1179648 | tf_op jit(solution)/shard_map/all_gather | solution.py:67
  110.5 0.8 shard_map.106
  (6 shorter events, 0.0 us)
Async XLA Ops:
  2.4 33.2 %collective-permute-start.4 = (bf16[64,6144]{1,0:T(8,128)(2,1)S(1)}, bf16[64,6144]{1,0:T(8,128)(2,1)S(1)}, u32[]{:S(2)}, u32[]{:S(2)}) collective-permute-start(bf16[64,6144]{1,0:T(8,128)(2,1)S(1)} %get-tuple-element.17._.up), channel_id=1, source_target_pairs={{0,16},{16,32},{32,48},{48,64},{64,80},{80,96},{96,112},{128,144},... | collective-permute-start | bytes 2359304 | tf_op jit(solution)/shard_map/ppermute | solution.py:63
  6.0 13.3 %collective-permute-start.2 = (bf16[16,6144]{1,0:T(8,128)(2,1)S(1)}, bf16[16,6144]{1,0:T(8,128)(2,1)S(1)}, u32[]{:S(2)}, u32[]{:S(2)}) collective-permute-start(bf16[16,6144]{1,0:T(8,128)(2,1)S(1)} %shard_map.94._), channel_id=1, source_target_pairs={{112,136},{120,128},{128,120},{136,112},{240,264},{248,256},{256,2... | collective-permute-start | bytes 589832 | tf_op jit(solution)/shard_map/ppermute | solution.py:303
  14.7 20.8 %collective-permute-start.1 = (bf16[48,6144]{1,0:T(8,128)(2,1)S(1)}, bf16[48,6144]{1,0:T(8,128)(2,1)S(1)}, u32[]{:S(2)}, u32[]{:S(2)}) collective-permute-start(bf16[48,6144]{1,0:T(8,128)(2,1)S(1)} %shard_map.95._), channel_id=1, source_target_pairs={{112,96},{240,224},{368,352},{496,480},{113,97},{241,225},{369,353... | collective-permute-start | bytes 1769480 | tf_op jit(solution)/shard_map/ppermute | solution.py:63
  15.4 1.5 %copy-start = (bf16[1,2,2,16,6144]{4,3,2,1,0:T(8,128)(2,1)S(1)}, bf16[1,2,2,16,6144]{4,3,2,1,0:T(8,128)(2,1)}, u32[]{:S(2)}) copy-start(bf16[1,2,2,16,6144]{4,3,2,1,0:T(8,128)(2,1)} %weights.5) | copy-start | bytes 2359300
  15.4 1.6 %copy-start.1 = (bf16[1,2,64,6144]{3,2,1,0:T(8,128)(2,1)S(1)}, bf16[1,2,64,6144]{3,2,1,0:T(8,128)(2,1)}, u32[]{:S(2)}) copy-start(bf16[1,2,64,6144]{3,2,1,0:T(8,128)(2,1)} %acts.3) | copy-start | bytes 4718596
  15.5 20.1 %collective-permute-start = (bf16[64,6144]{1,0:T(8,128)(2,1)S(1)}, bf16[64,6144]{1,0:T(8,128)(2,1)S(1)}, u32[]{:S(2)}, u32[]{:S(2)}) collective-permute-start(bf16[64,6144]{1,0:T(8,128)(2,1)S(1)} %shard_map.96.down), channel_id=1, source_target_pairs={{16,0},{32,16},{48,32},{64,48},{80,64},{96,80},{144,128},{160,144}... | collective-permute-start | bytes 2359304 | tf_op jit(solution)/shard_map/ppermute | solution.py:63
  19.6 15.9 %collective-permute-start.5 = (f32[32,64]{1,0:T(8,128)S(1)}, f32[32,64]{1,0:T(8,128)S(1)}, u32[]{:S(2)}, u32[]{:S(2)}) collective-permute-start(f32[32,64]{1,0:T(8,128)S(1)} %shard_map.98._), channel_id=1, source_target_pairs={{112,128},{128,112},{240,256},{256,240},{368,384},{384,368},{496,0... | collective-permute-start | bytes 24584 | tf_op jit(solution)/shard_map/ppermute | solution.py:313
  28.3 7.2 %collective-permute-start.3 = (bf16[16,6144]{1,0:T(8,128)(2,1)S(1)}, bf16[16,6144]{1,0:T(8,128)(2,1)S(1)}, u32[]{:S(2)}, u32[]{:S(2)}) collective-permute-start(bf16[16,6144]{1,0:T(8,128)(2,1)S(1)} %shard_map.99._), channel_id=1, source_target_pairs={{112,96},{240,224},{368,352},{496,480},{113,97},{241,225},{369,353... | collective-permute-start | bytes 589832 | tf_op jit(solution)/shard_map/ppermute | solution.py:63
  42.5 34.4 %copy-start.2 = (f32[1,2,16,384]{3,2,1,0:T(8,128)S(1)}, f32[1,2,16,384]{3,2,1,0:T(8,128)}, u32[]{:S(2)}) copy-start(f32[1,2,16,384]{3,2,1,0:T(8,128)} %master.1) | copy-start | bytes 147460
  42.5 34.4 %copy-start.3 = (f32[1,2,16,384]{3,2,1,0:T(8,128)S(1)}, f32[1,2,16,384]{3,2,1,0:T(8,128)}, u32[]{:S(2)}) copy-start(f32[1,2,16,384]{3,2,1,0:T(8,128)} %moment.1) | copy-start | bytes 147460
  42.5 34.4 %copy-start.4 = (f32[1,2,16,384]{3,2,1,0:T(8,128)S(1)}, f32[1,2,16,384]{3,2,1,0:T(8,128)}, u32[]{:S(2)}) copy-start(f32[1,2,16,384]{3,2,1,0:T(8,128)} %second.1) | copy-start | bytes 147460
  53.7 6.1 %collective-permute-start.6 = (bf16[16,768]{1,0:T(8,128)(2,1)S(1)}, bf16[16,768]{1,0:T(8,128)(2,1)S(1)}, u32[]{:S(2)}, u32[]{:S(2)}) collective-permute-start(bf16[16,768]{1,0:T(8,128)(2,1)S(1)} %get-tuple-element.25), channel_id=1, source_target_pairs={{112,368},{368,112},{128,384},{384,128},{113,369},{369,113},{129,3... | collective-permute-start | bytes 73736 | tf_op jit(solution)/shard_map/ppermute | solution.py:328
  93.1 9.7 %all-to-all-start.3 = ((bf16[4,4,2,16,384]{4,3,2,1,0:T(8,128)(2,1)}), bf16[4,4,2,16,384]{4,3,2,1,0:T(8,128)(2,1)S(1)}, u32[]{:S(2)}, u32[]{:S(2)}) async-start(bf16[4,4,2,16,384]{4,3,2,1,0:T(8,128)(2,1)} %broadcast_in_dim.2), calls=%async_computation.3 | async-start | bytes 786432 | tf_op jit(solution)/shard_map/all_to_all | solution.py:339

commit v11 on v10

--- a/solution.py
+++ b/solution.py
@@ -98,27 +98,22 @@
     return lax.dot_general(a, b, (((ca,), (cb,)), ((), ())), preferred_element_type=F32)
 
 
-def joined(*parts):
-    return jnp.concatenate([part[...] for part in parts], axis=0)
-
-
-def columns(parts, at):
-    return joined(*[part.at[:, at : at + 384] for part in parts])
-
-
-def take_kernel(grads, weights, w_out, down, down_a, down_b, up, sems):
-    side = jnp.where(lax.axis_index("zl") == 7, 0, 1)
-    copies = [
-        pltpu.make_async_copy(weights.at[0, side, 1], w_out, sems.at[0]),
-        pltpu.make_async_copy(grads.at[0, 1], up, sems.at[1]),
-        pltpu.make_async_copy(grads.at[0, 0], down, sems.at[2]),
-        pltpu.make_async_copy(grads.at[0, 0, :48], down_a, sems.at[3]),
-        pltpu.make_async_copy(grads.at[0, 0, 48:], down_b, sems.at[4]),
-    ]
+def copy_all(pairs, sems):
+    copies = [pltpu.make_async_copy(*pair, sems.at[i]) for i, pair in enumerate(pairs)]
     for copy in copies:
         copy.start()
     for copy in copies:
         copy.wait()
+
+
+def take_kernel(grads, weights, w_out, down, up, sems):
+    side = jnp.where(lax.axis_index("zl") == 7, 0, 1)
+    pairs = [(weights.at[0, side, 1], w_out), (grads.at[0, 1], up), (grads.at[0, 0], down)]
+    copy_all(pairs, sems)
+
+
+def take_again_kernel(grads, _, down, up, sems):
+    copy_all([(grads.at[0, 1], up), (grads.at[0, 0], down)], sems)
 
 
 def after_kernel(_, value, out):
@@ -157,7 +152,7 @@
 
 
 def terms_kernel(
-    from_after, after_a, after_b, from_before, wrapped, acts, weights, pre_act, down, up,
+    from_after, from_left, from_before, from_right, wrapped, acts, weights, pre_act, down, up,
     keep, send, grad, factor,
 ):
     zl = lax.axis_index("zl")
@@ -166,24 +161,21 @@
     def product(lhs, rhs, scale, row):
         for block in range(8):
             x, zh = block % 4, block // 4
-            even = dot(lhs, columns(rhs, block * 768), 1, 0) * scale
-            odd = dot(lhs, columns(rhs, block * 768 + 384), 1, 0) * scale
+            at = block * 768
+            even = dot(lhs, rhs[:, at : at + 384], 1, 0) * scale
+            odd = dot(lhs, rhs[:, at + 384 : at + 768], 1, 0) * scale
             spot = (x, pl.ds(row, UNITS), pl.ds(zh * 384, 384))
             keep[spot] = jnp.where(first, even, odd)
             send[spot] = jnp.where(first, odd, even).astype(BF16)
 
     for c in range(2):
         wrap = zl == (7 if c == 0 else 0)
-        if c == 0:
-            own = up
-            beside = zl == 6
-            sources = [
-                (jnp.logical_not(wrap | beside), (from_after,)),
-                (beside, (after_a, after_b)),
-            ]
-        else:
-            own = down
-            sources = [(jnp.logical_not(wrap), (from_before,))]
+        beside = zl == (6 if c == 0 else 1)
+        sources = [
+            (jnp.logical_not(wrap | beside), from_after if c == 0 else from_before),
+            (beside, from_left if c == 0 else from_right),
+        ]
+        own = up if c == 0 else down
 
         @pl.when(wrap)
         def _():
@@ -194,14 +186,14 @@
 
             @pl.when(chosen)
             def _():
-                grad[...] = dot(weights[0, c, 1], joined(*upstream), 1, 1) * INV_HIDDEN
+                grad[...] = dot(weights[0, c, 1], upstream[...], 1, 1) * INV_HIDDEN
                 factor[...] = pre_act[c]
 
         pre_grad = (grad[...] * gelu_slope(pre_act[c])).astype(BF16)
         activation = gelu_exact(factor[...]).astype(BF16)
         row = c * 2 * UNITS
-        product(pre_grad, (acts.at[0, c],), INV_WIDTH, row)
-        for chosen, upstream in [(wrap, (own,))] + sources:
+        product(pre_grad, acts.at[0, c], INV_WIDTH, row)
+        for chosen, upstream in [(wrap, own)] + sources:
 
             @pl.when(chosen)
             def _():
@@ -292,32 +284,36 @@
 
 
 def body(acts, grads_sent, replicas, master, moment, second):
-    w_out, down, down_a, down_b, up = call(
+    block = ((64, D), BF16)
+    w_out, down, up = call(
         take_kernel,
-        [((UNITS, D), BF16), ((64, D), BF16), ((48, D), BF16), ((16, D), BF16), ((64, D), BF16)],
+        [((UNITS, D), BF16), block, block],
         grads_sent, replicas, specs=[HBM, HBM],
-        scratch=[pltpu.SemaphoreType.DMA((5,))], vmem=58,
-    )
-    from_before = shifted(up, 1, range(7))
-    w_out = after(up, w_out, 10**10)
+        scratch=[pltpu.SemaphoreType.DMA((3,))], vmem=60,
+    )
+    from_right = shifted(up, 1, (0,))
+    down = after(up, down, 10**10)
+    from_left = shifted(down, -1, (7,))
+    w_out = after(down, w_out, 10**10)
     w_out_moved = lax.ppermute(w_out, FAR, weights_route())
-    down_a = after(w_out, down_a, 10**10)
-    after_a = shifted(down_a, -1, (7,))
-    down = after(down_a, down, 10**10)
-    from_after = shifted(down, -1, range(1, 7))
+    down_rest, up_rest = call(
+        take_again_kernel,
+        [block, block],
+        grads_sent, here(w_out), specs=[HBM, VMEM],
+        scratch=[pltpu.SemaphoreType.DMA((2,))], vmem=56, flops=10**10,
+    )
+    from_before = shifted(up_rest, 1, range(1, 7))
+    from_after = shifted(down_rest, -1, range(1, 7))
     acts, weights = here(acts), here(replicas)
     (pre_act,) = call(forward_kernel, [((2, UNITS, 64), F32)], acts, weights, flops=10**10)
     (sent,) = call(
         wrap_kernel, [((2 * UNITS, 64), F32)], here(w_out_moved), down, up, pre_act
     )
     wrapped = lax.ppermute(sent, SECTION, wrap_route())
-    down_b = after(sent, down_b, 10**10)
-    after_b = shifted(down_b, -1, (7,))
-    pre_act = after(down_b, pre_act, 10**10)
     keep, send = call(
         terms_kernel,
         [((4, 64, 768), F32), ((4, 64, 768), BF16)],
-        here(from_after), here(after_a), here(after_b), here(from_before), here(wrapped),
+        here(from_after), here(from_left), here(from_before), here(from_right), here(wrapped),
         acts, weights, pre_act, down, up,
         scratch=[pltpu.VMEM((UNITS, 64), F32), pltpu.VMEM((UNITS, 64), F32)],
     )

time: 112 us -> 116 us (1.036)
  blocking collectives: 56.8 us -> 58.2 us
  Pallas kernels: 5 us -> 6.17 us
    ppermute x4, waiting for transfers between devices: 0.12 us -> 4.64 us  [shifted(): return lax.ppermute(block, SECTION, route)]
    all_to_all x1, blocking collectives: 17.1 us -> 19.8 us  [body(): lax.all_to_all(spread, FAR, 0, 0, axis_index_groups=far_groups(), tiled=T...]
    ppermute x1, waiting for transfers between devices: 6.54 us -> 4.65 us  [body(): wrapped = lax.ppermute(sent, SECTION, wrap_route())]
    ppermute x1, starting transfers between devices: 8.71 us -> 10.2 us  [body(): w_out_moved = lax.ppermute(w_out, FAR, weights_route())]
    ppermute x1, waiting for transfers between devices: 1.73 us -> 0.35 us  [body(): w_out_moved = lax.ppermute(w_out, FAR, weights_route())]
    pallas_call x9 -> x10, Pallas kernels: 4.99 us -> 6.17 us  [call(): pl.pallas_call(kernel, out_shape=[pltpu.VMEM(*out) if isinstance(out, tup...]
  transfers between devices with their start and end apart: 8 -> 8, of which waited for: 5 -> 5; matrix products, arithmetic and copies ran while one was open for 2% -> 2% of each run, Pallas kernels for 1% -> 2%
where the time goes in v11:
time: 116 us; the launch traced here: 115 us
  blocking collectives  58.2 us (50%)
  starting transfers between devices  31.8 us (27%)
  waiting for transfers between devices  15.8 us (14%)
  Pallas kernels  6.17 us (5%)
  local copies, waits for them, and re-layouts  2.67 us (2%)
    all_to_all x1, blocking collectives, body(): lax.all_to_all(spread, FAR, 0, 0, axis_index_groups=far_groups(), tiled=T...  19.8 us
    all_to_all x1, blocking collectives, body(): lax.all_to_all(shared, FAR, 0, 0, axis_index_groups=far_groups(), tiled=T...  14.1 us
    all_gather x2, blocking collectives, both_cores(): return lax.all_gather(block, 'c', axis=0, tiled=False)  13.2 us
    all_to_all x1, blocking collectives, body(): near = lax.all_to_all(tiles, 'x', 0, 0, tiled=True)  11 us
    ppermute x1, starting transfers between devices, body(): w_out_moved = lax.ppermute(w_out, FAR, weights_route())  10.2 us
    ppermute x1, starting transfers between devices, body(): wrapped = lax.ppermute(sent, SECTION, wrap_route())  7.54 us
    ppermute x4, starting transfers between devices, shifted(): return lax.ppermute(block, SECTION, route)  6.31 us
    pallas_call x10, Pallas kernels, call(): pl.pallas_call(kernel, out_shape=[pltpu.VMEM(*out) if isinstance(out, tup...  6.17 us
  transfers between devices with their start and end apart: 8, of which 5 were waited for; matrix products, arithmetic and copies ran while one was open for 2% of the time, Pallas kernels for 2%

profile of v11, /device:TPU:9, one launch (start us, length us, event | category | flops | bytes accessed | tf_op | source)
XLA Modules:
  0.0 115.4 jit_solution(437293586100671016)
XLA Ops:
  0.6 1.5 %shard_map.93 = (bf16[16,6144]{1,0:T(8,128)(2,1)S(1)}, bf16[64,6144]{1,0:T(8,128)(2,1)S(1)}, bf16[64,6144]{1,0:T(8,128)(2,1)S(1)}) custom-call(bf16[1,2,64,6144]{3,2,1,0:T(8,128)(2,1)} %grads.3, bf16[1,2,2,16,6144]{4,3,2,1,0:T(8,128)(2,1)} %weights.5), custom_call_target="tpu_custom_call" | custom-call | tf_op jit(solution)/shard_map/pallas_call | solution.py:75
  2.2 3.6 %collective-permute-start.3 = (bf16[64,6144]{1,0:T(8,128)(2,1)S(1)}, bf16[64,6144]{1,0:T(8,128)(2,1)S(1)}, u32[]{:S(2)}, u32[]{:S(2)}) collective-permute-start(bf16[64,6144]{1,0:T(8,128)(2,1)S(1)} %get-tuple-element.17._.up), channel_id=1, source_target_pairs={{0,16},{128,144},{256,272},{384,400},{1,17},{129,145},{257,273},{3... | collective-permute-start | bytes 2359304 | tf_op jit(solution)/shard_map/ppermute | solution.py:63
  5.8 0.7 collective-permute-start.1
  6.5 0.0 copy-start
  6.5 0.0 copy-start.1
  6.5 10.2 %collective-permute-start.4 = (bf16[16,6144]{1,0:T(8,128)(2,1)S(1)}, bf16[16,6144]{1,0:T(8,128)(2,1)S(1)}, u32[]{:S(2)}, u32[]{:S(2)}) collective-permute-start(bf16[16,6144]{1,0:T(8,128)(2,1)S(1)} %shard_map.95._), channel_id=1, source_target_pairs={{112,136},{120,128},{128,120},{136,112},{240,264},{248,256},{256,2... | collective-permute-start | bytes 589832 | tf_op jit(solution)/shard_map/ppermute | solution.py:298
  16.8 1.4 %shard_map.96 = (bf16[64,6144]{1,0:T(8,128)(2,1)S(1)}, bf16[64,6144]{1,0:T(8,128)(2,1)S(1)}) custom-call(bf16[1,2,64,6144]{3,2,1,0:T(8,128)(2,1)} %grads.3, bf16[16,6144]{1,0:T(8,128)(2,1)S(1)} %shard_map.95._), custom_call_target="tpu_custom_call" | custom-call | flops 10000000000 | tf_op jit(solution)/shard_map/pallas_call | solution.py:75
  18.2 1.3 %collective-permute-start = (bf16[64,6144]{1,0:T(8,128)(2,1)S(1)}, bf16[64,6144]{1,0:T(8,128)(2,1)S(1)}, u32[]{:S(2)}, u32[]{:S(2)}) collective-permute-start(bf16[64,6144]{1,0:T(8,128)(2,1)S(1)} %get-tuple-element.20), channel_id=1, source_target_pairs={{16,0},{32,16},{48,32},{64,48},{80,64},{96,80},{144,128},{160,144}... | collective-permute-start | bytes 2359304 | tf_op jit(solution)/shard_map/ppermute | solution.py:63
  19.5 0.7 collective-permute-start.2
  20.2 0.0 copy-done
  20.2 0.0 copy-done.1
  20.2 0.5 shard_map.97.pre_act
  20.7 0.3 collective-permute-done.4.w_out
  21.1 0.3 shard_map.98
  21.4 7.5 %collective-permute-start.5 = (f32[32,64]{1,0:T(8,128)S(1)}, f32[32,64]{1,0:T(8,128)S(1)}, u32[]{:S(2)}, u32[]{:S(2)}) collective-permute-start(f32[32,64]{1,0:T(8,128)S(1)} %shard_map.98), channel_id=1, source_target_pairs={{112,128},{128,112},{240,256},{256,240},{368,384},{384,368},{496,0... | collective-permute-start | bytes 24584 | tf_op jit(solution)/shard_map/ppermute | solution.py:312
  28.9 4.7 %collective-permute-done.5.wrapped = f32[32,64]{1,0:T(8,128)S(1)} collective-permute-done((f32[32,64]{1,0:T(8,128)S(1)}, f32[32,64]{1,0:T(8,128)S(1)}, u32[]{:S(2)}, u32[]{:S(2)}) %collective-permute-start.5) | collective-permute-done | bytes 8224 | tf_op jit(solution)/shard_map/ppermute | solution.py:312
  33.6 0.0 collective-permute-done.1.from_left
  33.6 0.0 collective-permute-done.3.from_right
  33.6 4.6 %collective-permute-done.from_after = bf16[64,6144]{1,0:T(8,128)(2,1)S(1)} collective-permute-done((bf16[64,6144]{1,0:T(8,128)(2,1)S(1)}, bf16[64,6144]{1,0:T(8,128)(2,1)S(1)}, u32[]{:S(2)}, u32[]{:S(2)}) %collective-permute-start) | collective-permute-done | bytes 786464 | tf_op jit(solution)/shard_map/ppermute | solution.py:63
  38.2 0.0 collective-permute-done.2.from_before
  38.2 1.4 %shard_map.99 = (f32[4,64,768]{2,1,0:T(8,128)S(1)}, bf16[4,64,768]{2,1,0:T(8,128)(2,1)S(1)}) custom-call(bf16[64,6144]{1,0:T(8,128)(2,1)S(1)} %collective-permute-done.from_after, bf16[64,6144]{1,0:T(8,128)(2,1)S(1)} %collective-permute-done.1.from_left, bf16[64,6144]{1,0:T(8,128)(2,1)S(1)} %collective-permute-done.2.from_before, ...), custom_call_target="tpu_custom_call" | custom-call | tf_op jit(solution)/shard_map/pallas_call | solution.py:75
  39.6 4.2 %all-gather = bf16[8,64,768]{2,1,0:T(8,128)(2,1)S(1)} all-gather(bf16[4,64,768]{2,1,0:T(8,128)(2,1)S(1)} %get-tuple-element.23), channel_id=2, replica_groups=mesh['y'=4,'zl'=8,'zh'=2,'x'=4,'c'=2] {'c'}, dimensions={0}, use_global_device_ids=true | all-gather | bytes 1179648 | tf_op jit(solution)/shard_map/all_gather | solution.py:67
  43.7 0.0 copy-start.2
  43.7 0.0 copy-start.3
  43.8 0.0 copy-start.4
  43.8 0.1 shard_map.100
  43.8 11.0 %all_to_all.20.arrived = bf16[4,64,768]{2,1,0:T(8,128)(2,1)S(1)} all-to-all(bf16[4,64,768]{2,1,0:T(8,128)(2,1)S(1)} %shard_map.100), channel_id=1, replica_groups=mesh['y'=4,'zl'=8,'zh'=2,'x'=4,'c'=2] {'x'}, dimensions={0} | all-to-all | bytes 786432 | tf_op jit(solution)/shard_map/all_to_all | solution.py:322
  54.9 0.1 shard_map.101
  54.9 4.2 %collective-permute-start.6 = (bf16[16,768]{1,0:T(8,128)(2,1)S(1)}, bf16[16,768]{1,0:T(8,128)(2,1)S(1)}, u32[]{:S(2)}, u32[]{:S(2)}) collective-permute-start(bf16[16,768]{1,0:T(8,128)(2,1)S(1)} %get-tuple-element.25), channel_id=1, source_target_pairs={{112,368},{368,112},{128,384},{384,128},{113,369},{369,113},{129,3... | collective-permute-start | bytes 73736 | tf_op jit(solution)/shard_map/ppermute | solution.py:324
  59.1 1.8 %collective-permute-done.6.swap = bf16[16,768]{1,0:T(8,128)(2,1)S(1)} collective-permute-done((bf16[16,768]{1,0:T(8,128)(2,1)S(1)}, bf16[16,768]{1,0:T(8,128)(2,1)S(1)}, u32[]{:S(2)}, u32[]{:S(2)}) %collective-permute-start.6) | collective-permute-done | bytes 24608 | tf_op jit(solution)/shard_map/ppermute | solution.py:324
  61.0 19.8 %all_to_all.21.arrived = bf16[4,2,16,384]{3,2,1,0:T(8,128)(2,1)S(1)} all-to-all(bf16[4,2,16,384]{3,2,1,0:T(8,128)(2,1)S(1)} %shard_map.102), channel_id=1, replica_groups={{0,8,496,504},{16,24,480,488},{32,40,464,472},{48,56,448,456},{64,72,43..., dimensions={0} | all-to-all | bytes 196608 | tf_op jit(solution)/shard_map/all_to_all | solution.py:326
  80.9 0.0 copy-done.2
  80.9 0.0 copy-done.3
  80.9 0.0 copy-done.4
  80.9 0.1 shard_map.103
  80.9 14.1 %all_to_all.22 = bf16[4,2,16,384]{3,2,1,0:T(8,128)(2,1)S(1)} all-to-all(bf16[4,2,16,384]{3,2,1,0:T(8,128)(2,1)S(1)} %get-tuple-element.29), channel_id=1, replica_groups={{0,8,496,504},{16,24,480,488},{32,40,464,472},{48,56,448,456},{64,72,43..., dimensions={0} | all-to-all | bytes 196608 | tf_op jit(solution)/shard_map/all_to_all | solution.py:333
  95.1 0.8 broadcast_in_dim.2
  95.9 3.5 %all-to-all-start.3 = ((bf16[4,4,2,16,384]{4,3,2,1,0:T(8,128)(2,1)}), bf16[4,4,2,16,384]{4,3,2,1,0:T(8,128)(2,1)S(1)}, u32[]{:S(2)}, u32[]{:S(2)}) async-start(bf16[4,4,2,16,384]{4,3,2,1,0:T(8,128)(2,1)} %broadcast_in_dim.2), calls=%async_computation.3 | async-start | bytes 786432 | tf_op jit(solution)/shard_map/all_to_all | solution.py:335
  99.3 0.6 copy.14
  100.0 0.6 copy.15
  100.6 0.6 copy.16
  101.2 4.3 %all-to-all-done.3 = bf16[4,4,2,16,384]{4,3,2,1,0:T(8,128)(2,1)S(1)} async-done(((bf16[4,4,2,16,384]{4,3,2,1,0:T(8,128)(2,1)}), bf16[4,4,2,16,384]{4,3,2,1,0:T(8,128)(2,1)S(1)}, u32[]{:S(2)}, u32[]{:S(2)}) %all-to-all-start.3) | async-done | bytes 393248 | tf_op jit(solution)/shard_map/all_to_all | solution.py:335
  105.5 9.0 %all-gather.1 = bf16[8,4,2,16,384]{4,3,2,1,0:T(8,128)(2,1)S(1)} all-gather(bf16[4,4,2,16,384]{4,3,2,1,0:T(8,128)(2,1)S(1)} %all-to-all-done.3), channel_id=3, replica_groups=mesh['y'=4,'zl'=8,'zh'=2,'x'=4,'c'=2] {'c'}, dimensions={0}, use_global_device_ids=true | all-gather | bytes 1179648 | tf_op jit(solution)/shard_map/all_gather | solution.py:67
  114.6 0.8 shard_map.104
  (3 shorter events, 0.0 us)
Async XLA Ops:
  2.2 31.4 %collective-permute-start.3 = (bf16[64,6144]{1,0:T(8,128)(2,1)S(1)}, bf16[64,6144]{1,0:T(8,128)(2,1)S(1)}, u32[]{:S(2)}, u32[]{:S(2)}) collective-permute-start(bf16[64,6144]{1,0:T(8,128)(2,1)S(1)} %get-tuple-element.17._.up), channel_id=1, source_target_pairs={{0,16},{128,144},{256,272},{384,400},{1,17},{129,145},{257,273},{3... | collective-permute-start | bytes 2359304 | tf_op jit(solution)/shard_map/ppermute | solution.py:63
  5.8 27.8 %collective-permute-start.1 = (bf16[64,6144]{1,0:T(8,128)(2,1)S(1)}, bf16[64,6144]{1,0:T(8,128)(2,1)S(1)}, u32[]{:S(2)}, u32[]{:S(2)}) collective-permute-start(bf16[64,6144]{1,0:T(8,128)(2,1)S(1)} %shard_map.94._.down), channel_id=1, source_target_pairs={{112,96},{240,224},{368,352},{496,480},{113,97},{241,225},{369,353... | collective-permute-start | bytes 2359304 | tf_op jit(solution)/shard_map/ppermute | solution.py:63
  6.5 13.7 %copy-start = (bf16[1,2,2,16,6144]{4,3,2,1,0:T(8,128)(2,1)S(1)}, bf16[1,2,2,16,6144]{4,3,2,1,0:T(8,128)(2,1)}, u32[]{:S(2)}) copy-start(bf16[1,2,2,16,6144]{4,3,2,1,0:T(8,128)(2,1)} %weights.5) | copy-start | bytes 2359300
  6.5 13.7 %copy-start.1 = (bf16[1,2,64,6144]{3,2,1,0:T(8,128)(2,1)S(1)}, bf16[1,2,64,6144]{3,2,1,0:T(8,128)(2,1)}, u32[]{:S(2)}) copy-start(bf16[1,2,64,6144]{3,2,1,0:T(8,128)(2,1)} %acts.3) | copy-start | bytes 4718596
  6.5 14.5 %collective-permute-start.4 = (bf16[16,6144]{1,0:T(8,128)(2,1)S(1)}, bf16[16,6144]{1,0:T(8,128)(2,1)S(1)}, u32[]{:S(2)}, u32[]{:S(2)}) collective-permute-start(bf16[16,6144]{1,0:T(8,128)(2,1)S(1)} %shard_map.95._), channel_id=1, source_target_pairs={{112,136},{120,128},{128,120},{136,112},{240,264},{248,256},{256,2... | collective-permute-start | bytes 589832 | tf_op jit(solution)/shard_map/ppermute | solution.py:298
  18.2 20.0 %collective-permute-start = (bf16[64,6144]{1,0:T(8,128)(2,1)S(1)}, bf16[64,6144]{1,0:T(8,128)(2,1)S(1)}, u32[]{:S(2)}, u32[]{:S(2)}) collective-permute-start(bf16[64,6144]{1,0:T(8,128)(2,1)S(1)} %get-tuple-element.20), channel_id=1, source_target_pairs={{16,0},{32,16},{48,32},{64,48},{80,64},{96,80},{144,128},{160,144}... | collective-permute-start | bytes 2359304 | tf_op jit(solution)/shard_map/ppermute | solution.py:63
  19.5 18.7 %collective-permute-start.2 = (bf16[64,6144]{1,0:T(8,128)(2,1)S(1)}, bf16[64,6144]{1,0:T(8,128)(2,1)S(1)}, u32[]{:S(2)}, u32[]{:S(2)}) collective-permute-start(bf16[64,6144]{1,0:T(8,128)(2,1)S(1)} %get-tuple-element.21), channel_id=1, source_target_pairs={{16,32},{32,48},{48,64},{64,80},{80,96},{96,112},{144,160},{160,17... | collective-permute-start | bytes 2359304 | tf_op jit(solution)/shard_map/ppermute | solution.py:63
  21.4 12.2 %collective-permute-start.5 = (f32[32,64]{1,0:T(8,128)S(1)}, f32[32,64]{1,0:T(8,128)S(1)}, u32[]{:S(2)}, u32[]{:S(2)}) collective-permute-start(f32[32,64]{1,0:T(8,128)S(1)} %shard_map.98), channel_id=1, source_target_pairs={{112,128},{128,112},{240,256},{256,240},{368,384},{384,368},{496,0... | collective-permute-start | bytes 24584 | tf_op jit(solution)/shard_map/ppermute | solution.py:312
  43.7 37.1 %copy-start.2 = (f32[1,2,16,384]{3,2,1,0:T(8,128)S(1)}, f32[1,2,16,384]{3,2,1,0:T(8,128)}, u32[]{:S(2)}) copy-start(f32[1,2,16,384]{3,2,1,0:T(8,128)} %master.1) | copy-start | bytes 147460
  43.7 37.1 %copy-start.3 = (f32[1,2,16,384]{3,2,1,0:T(8,128)S(1)}, f32[1,2,16,384]{3,2,1,0:T(8,128)}, u32[]{:S(2)}) copy-start(f32[1,2,16,384]{3,2,1,0:T(8,128)} %moment.1) | copy-start | bytes 147460
  43.8 37.1 %copy-start.4 = (f32[1,2,16,384]{3,2,1,0:T(8,128)S(1)}, f32[1,2,16,384]{3,2,1,0:T(8,128)}, u32[]{:S(2)}) copy-start(f32[1,2,16,384]{3,2,1,0:T(8,128)} %second.1) | copy-start | bytes 147460
  54.9 6.1 %collective-permute-start.6 = (bf16[16,768]{1,0:T(8,128)(2,1)S(1)}, bf16[16,768]{1,0:T(8,128)(2,1)S(1)}, u32[]{:S(2)}, u32[]{:S(2)}) collective-permute-start(bf16[16,768]{1,0:T(8,128)(2,1)S(1)} %get-tuple-element.25), channel_id=1, source_target_pairs={{112,368},{368,112},{128,384},{384,128},{113,369},{369,113},{129,3... | collective-permute-start | bytes 73736 | tf_op jit(solution)/shard_map/ppermute | solution.py:324
  95.9 9.7 %all-to-all-start.3 = ((bf16[4,4,2,16,384]{4,3,2,1,0:T(8,128)(2,1)}), bf16[4,4,2,16,384]{4,3,2,1,0:T(8,128)(2,1)S(1)}, u32[]{:S(2)}, u32[]{:S(2)}) async-start(bf16[4,4,2,16,384]{4,3,2,1,0:T(8,128)(2,1)} %broadcast_in_dim.2), calls=%async_computation.3 | async-start | bytes 786432 | tf_op jit(solution)/shard_map/all_to_all | solution.py:335

commit v12 on v10

--- a/solution.py
+++ b/solution.py
@@ -282,7 +282,7 @@
                 for p in range(2):
                     copies.append(
                         pltpu.make_async_copy(
-                            full.at[near % 2, near // 2, 2 * p + zh, sec], out.at[0, c, p, :, pl.ds(at, 384)], sem
+                            full.at[near, 2 * p + zh, sec], out.at[0, c, p, :, pl.ds(at, 384)], sem
                         )
                     )
     for copy in copies:
@@ -335,8 +335,7 @@
         here(far), here(master), here(moment), here(second),
     )
     shared = lax.all_to_all(shared, FAR, 0, 0, axis_index_groups=far_groups(), tiled=True)
-    copies = jnp.broadcast_to(shared[None], (4, *shared.shape))
-    full = both_cores(lax.all_to_all(copies, "x", 0, 0, tiled=True))
+    full = lax.all_gather(shared, ("x", "c"), axis=0, tiled=False)
     (new_replicas,) = call(
         finish_kernel,
         [jax.ShapeDtypeStruct((1, 2, 2, UNITS, D), BF16)],

time: 112 us -> 113 us (level)
  waiting for transfers between devices: 14.9 us -> 20.3 us
  blocking collectives: 56.8 us -> 52 us
    all_gather x0 -> x1, blocking collectives: none -> 18.3 us  [body(): full = lax.all_gather(shared, ('x', 'c'), axis=0, tiled=False)]
    all_to_all x1 -> x0, blocking collectives: 15.3 us -> none  [body(): lax.all_to_all(shared, FAR, 0, 0, axis_index_groups=far_groups(), tiled=T...]
    all_gather x2 -> x1, blocking collectives: 13.4 us -> 5.54 us  [both_cores(): return lax.all_gather(block, 'c', axis=0, tiled=False)]
    all_to_all x1, waiting for transfers between devices: 4.33 us -> 9.74 us  [body(): lax.all_to_all(shared, FAR, 0, 0, axis_index_groups=far_groups(), tiled=T...]
where the time goes in v12:
time: 113 us; the launch traced here: 112 us
  blocking collectives  52 us (46%)
  starting transfers between devices  31.5 us (28%)
  waiting for transfers between devices  20.3 us (18%)
  Pallas kernels  5.64 us (5%)
  local copies, waits for them, and re-layouts  2.06 us (2%)
    all_gather x1, blocking collectives, body(): full = lax.all_gather(shared, ('x', 'c'), axis=0, tiled=False)  18.3 us
    all_to_all x1, blocking collectives, body(): lax.all_to_all(spread, FAR, 0, 0, axis_index_groups=far_groups(), tiled=T...  17.1 us
    all_to_all x1, blocking collectives, body(): near = lax.all_to_all(tiles, 'x', 0, 0, tiled=True)  11 us
    all_to_all x1, waiting for transfers between devices, body(): lax.all_to_all(shared, FAR, 0, 0, axis_index_groups=far_groups(), tiled=T...  9.74 us
    ppermute x1, starting transfers between devices, body(): w_out_moved = lax.ppermute(w_out, FAR, weights_route())  8.71 us
    ppermute x1, starting transfers between devices, body(): wrapped = lax.ppermute(sent, SECTION, wrap_route())  8.61 us
    ppermute x1, waiting for transfers between devices, body(): wrapped = lax.ppermute(sent, SECTION, wrap_route())  6.54 us
    ppermute x4, starting transfers between devices, shifted(): return lax.ppermute(block, SECTION, route)  6.39 us
  transfers between devices with their start and end apart: 8, of which 5 were waited for; matrix products, arithmetic and copies ran while one was open for 2% of the time, Pallas kernels for 1%

profile of v12, /device:TPU:9, one launch (start us, length us, event | category | flops | bytes accessed | tf_op | source)
XLA Modules:
  0.0 112.2 jit_solution(11000732289258076913)
XLA Ops:
  0.6 1.7 %shard_map.93 = (bf16[16,6144]{1,0:T(8,128)(2,1)S(1)}, bf16[64,6144]{1,0:T(8,128)(2,1)S(1)}, bf16[48,6144]{1,0:T(8,128)(2,1)S(1)}, bf16[16,6144]{1,0:T(8,128)(2,1)S(1)}, bf16[64,6144]{1,0:T(8,128)(2,1)S(1)}) custom-call(bf16[1,2,64,6144]{3,2,1,0:T(8,128)(2,1)} %grads.1, bf16[1,2,2,16,6144]{4,3,2,1,0:T(8,128)(2,1)} %weights.5), custom_call_target="tpu_custom_call" | custom-call | tf_op jit(solution)/shard_map/pallas_call | solution.py:75
  2.4 3.6 %collective-permute-start.4 = (bf16[64,6144]{1,0:T(8,128)(2,1)S(1)}, bf16[64,6144]{1,0:T(8,128)(2,1)S(1)}, u32[]{:S(2)}, u32[]{:S(2)}) collective-permute-start(bf16[64,6144]{1,0:T(8,128)(2,1)S(1)} %get-tuple-element.17._.up), channel_id=1, source_target_pairs={{0,16},{16,32},{32,48},{48,64},{64,80},{80,96},{96,112},{128,144},... | collective-permute-start | bytes 2359304 | tf_op jit(solution)/shard_map/ppermute | solution.py:63
  6.0 8.7 %collective-permute-start.2 = (bf16[16,6144]{1,0:T(8,128)(2,1)S(1)}, bf16[16,6144]{1,0:T(8,128)(2,1)S(1)}, u32[]{:S(2)}, u32[]{:S(2)}) collective-permute-start(bf16[16,6144]{1,0:T(8,128)(2,1)S(1)} %shard_map.94._), channel_id=1, source_target_pairs={{112,136},{120,128},{128,120},{136,112},{240,264},{248,256},{256,2... | collective-permute-start | bytes 589832 | tf_op jit(solution)/shard_map/ppermute | solution.py:303
  14.7 0.7 collective-permute-start.1
  15.4 0.0 copy-start
  15.4 0.0 copy-start.1
  15.5 1.4 %collective-permute-start = (bf16[64,6144]{1,0:T(8,128)(2,1)S(1)}, bf16[64,6144]{1,0:T(8,128)(2,1)S(1)}, u32[]{:S(2)}, u32[]{:S(2)}) collective-permute-start(bf16[64,6144]{1,0:T(8,128)(2,1)S(1)} %shard_map.96.down), channel_id=1, source_target_pairs={{16,0},{32,16},{48,32},{64,48},{80,64},{96,80},{144,128},{160,144}... | collective-permute-start | bytes 2359304 | tf_op jit(solution)/shard_map/ppermute | solution.py:63
  16.9 0.0 copy-done
  16.9 0.2 copy-done.1
  17.1 0.5 shard_map.97.pre_act.value
  17.6 1.7 %collective-permute-done.2.w_out = bf16[16,6144]{1,0:T(8,128)(2,1)S(1)} collective-permute-done((bf16[16,6144]{1,0:T(8,128)(2,1)S(1)}, bf16[16,6144]{1,0:T(8,128)(2,1)S(1)}, u32[]{:S(2)}, u32[]{:S(2)}) %collective-permute-start.2) | collective-permute-done | bytes 196640 | tf_op jit(solution)/shard_map/ppermute | solution.py:303
  19.3 0.3 shard_map.98._
  19.6 8.6 %collective-permute-start.5 = (f32[32,64]{1,0:T(8,128)S(1)}, f32[32,64]{1,0:T(8,128)S(1)}, u32[]{:S(2)}, u32[]{:S(2)}) collective-permute-start(f32[32,64]{1,0:T(8,128)S(1)} %shard_map.98._), channel_id=1, source_target_pairs={{112,128},{128,112},{240,256},{256,240},{368,384},{384,368},{496,0... | collective-permute-start | bytes 24584 | tf_op jit(solution)/shard_map/ppermute | solution.py:313
  28.3 0.7 collective-permute-start.3
  28.9 6.5 %collective-permute-done.5.wrapped = f32[32,64]{1,0:T(8,128)S(1)} collective-permute-done((f32[32,64]{1,0:T(8,128)S(1)}, f32[32,64]{1,0:T(8,128)S(1)}, u32[]{:S(2)}, u32[]{:S(2)}) %collective-permute-start.5) | collective-permute-done | bytes 8224 | tf_op jit(solution)/shard_map/ppermute | solution.py:313
  35.5 0.0 collective-permute-done.3.after_b
  35.5 0.0 collective-permute-done.1.after_a
  35.5 0.1 collective-permute-done.from_after
  35.6 0.0 collective-permute-done.4.from_before
  35.6 1.4 %shard_map.101 = (f32[4,64,768]{2,1,0:T(8,128)S(1)}, bf16[4,64,768]{2,1,0:T(8,128)(2,1)S(1)}) custom-call(bf16[64,6144]{1,0:T(8,128)(2,1)S(1)} %collective-permute-done.from_after, bf16[48,6144]{1,0:T(8,128)(2,1)S(1)} %collective-permute-done.1.after_a, bf16[16,6144]{1,0:T(8,128)(2,1)S(1)} %collective-permute-done.3.after_b, ...), custom_call_target="tpu_custom_call" | custom-call | tf_op jit(solution)/shard_map/pallas_call | solution.py:75
  37.0 5.5 %all-gather = bf16[8,64,768]{2,1,0:T(8,128)(2,1)S(1)} all-gather(bf16[4,64,768]{2,1,0:T(8,128)(2,1)S(1)} %get-tuple-element.23), channel_id=2, replica_groups=mesh['y'=4,'zl'=8,'zh'=2,'x'=4,'c'=2] {'c'}, dimensions={0}, use_global_device_ids=true | all-gather | bytes 1179648 | tf_op jit(solution)/shard_map/all_gather | solution.py:67
  42.5 0.0 copy-start.2
  42.5 0.0 copy-start.3
  42.5 0.0 copy-start.4
  42.5 0.1 shard_map.102
  42.6 11.0 %all_to_all.15.arrived = bf16[4,64,768]{2,1,0:T(8,128)(2,1)S(1)} all-to-all(bf16[4,64,768]{2,1,0:T(8,128)(2,1)S(1)} %shard_map.102), channel_id=1, replica_groups=mesh['y'=4,'zl'=8,'zh'=2,'x'=4,'c'=2] {'x'}, dimensions={0} | all-to-all | bytes 786432 | tf_op jit(solution)/shard_map/all_to_all | solution.py:326
  53.6 0.1 shard_map.103
  53.7 3.9 %collective-permute-start.6 = (bf16[16,768]{1,0:T(8,128)(2,1)S(1)}, bf16[16,768]{1,0:T(8,128)(2,1)S(1)}, u32[]{:S(2)}, u32[]{:S(2)}) collective-permute-start(bf16[16,768]{1,0:T(8,128)(2,1)S(1)} %get-tuple-element.25), channel_id=1, source_target_pairs={{112,368},{368,112},{128,384},{384,128},{113,369},{369,113},{129,3... | collective-permute-start | bytes 73736 | tf_op jit(solution)/shard_map/ppermute | solution.py:328
  57.6 2.1 %collective-permute-done.6.swap = bf16[16,768]{1,0:T(8,128)(2,1)S(1)} collective-permute-done((bf16[16,768]{1,0:T(8,128)(2,1)S(1)}, bf16[16,768]{1,0:T(8,128)(2,1)S(1)}, u32[]{:S(2)}, u32[]{:S(2)}) %collective-permute-start.6) | collective-permute-done | bytes 24608 | tf_op jit(solution)/shard_map/ppermute | solution.py:328
  59.8 17.1 %all_to_all.16.arrived = bf16[4,2,16,384]{3,2,1,0:T(8,128)(2,1)S(1)} all-to-all(bf16[4,2,16,384]{3,2,1,0:T(8,128)(2,1)S(1)} %shard_map.104), channel_id=1, replica_groups={{0,8,496,504},{16,24,480,488},{32,40,464,472},{48,56,448,456},{64,72,43..., dimensions={0} | all-to-all | bytes 196608 | tf_op jit(solution)/shard_map/all_to_all | solution.py:330
  76.9 0.0 copy-done.2
  76.9 0.0 copy-done.3
  76.9 0.0 copy-done.4
  76.9 0.7 shard_map.105
  77.7 3.9 %all-to-all-start.2 = ((bf16[4,2,16,384]{3,2,1,0:T(8,128)(2,1)}), bf16[4,2,16,384]{3,2,1,0:T(8,128)(2,1)S(1)}, u32[]{:S(2)}, u32[]{:S(2)}) async-start(bf16[4,2,16,384]{3,2,1,0:T(8,128)(2,1)} %get-tuple-element.29), calls=%async_computation.2 | async-start | bytes 196608 | tf_op jit(solution)/shard_map/all_to_all | solution.py:337
  81.5 0.6 copy.20
  82.1 0.6 copy.21
  82.7 0.6 copy.22
  83.4 9.7 %all-to-all-done.2 = bf16[4,2,16,384]{3,2,1,0:T(8,128)(2,1)S(1)} async-done(((bf16[4,2,16,384]{3,2,1,0:T(8,128)(2,1)}), bf16[4,2,16,384]{3,2,1,0:T(8,128)(2,1)S(1)}, u32[]{:S(2)}, u32[]{:S(2)}) %all-to-all-start.2) | async-done | bytes 98336 | tf_op jit(solution)/shard_map/all_to_all | solution.py:337
  93.1 18.3 %all-gather.1 = bf16[32,2,16,384]{3,2,1,0:T(8,128)(2,1)S(1)} all-gather(bf16[4,2,16,384]{3,2,1,0:T(8,128)(2,1)S(1)} %all-to-all-done.2), channel_id=3, replica_groups=mesh['y'=4,'zl'=8,'zh'=2,'x'=4,'c'=2] {'x','c'}, dimensions={0}, use_global_device_ids=true | all-gather | bytes 884736 | tf_op jit(solution)/shard_map/all_gather | solution.py:338
  111.4 0.8 shard_map.106
  (6 shorter events, 0.0 us)
Async XLA Ops:
  2.4 33.2 %collective-permute-start.4 = (bf16[64,6144]{1,0:T(8,128)(2,1)S(1)}, bf16[64,6144]{1,0:T(8,128)(2,1)S(1)}, u32[]{:S(2)}, u32[]{:S(2)}) collective-permute-start(bf16[64,6144]{1,0:T(8,128)(2,1)S(1)} %get-tuple-element.17._.up), channel_id=1, source_target_pairs={{0,16},{16,32},{32,48},{48,64},{64,80},{80,96},{96,112},{128,144},... | collective-permute-start | bytes 2359304 | tf_op jit(solution)/shard_map/ppermute | solution.py:63
  6.0 13.3 %collective-permute-start.2 = (bf16[16,6144]{1,0:T(8,128)(2,1)S(1)}, bf16[16,6144]{1,0:T(8,128)(2,1)S(1)}, u32[]{:S(2)}, u32[]{:S(2)}) collective-permute-start(bf16[16,6144]{1,0:T(8,128)(2,1)S(1)} %shard_map.94._), channel_id=1, source_target_pairs={{112,136},{120,128},{128,120},{136,112},{240,264},{248,256},{256,2... | collective-permute-start | bytes 589832 | tf_op jit(solution)/shard_map/ppermute | solution.py:303
  14.7 20.8 %collective-permute-start.1 = (bf16[48,6144]{1,0:T(8,128)(2,1)S(1)}, bf16[48,6144]{1,0:T(8,128)(2,1)S(1)}, u32[]{:S(2)}, u32[]{:S(2)}) collective-permute-start(bf16[48,6144]{1,0:T(8,128)(2,1)S(1)} %shard_map.95._), channel_id=1, source_target_pairs={{112,96},{240,224},{368,352},{496,480},{113,97},{241,225},{369,353... | collective-permute-start | bytes 1769480 | tf_op jit(solution)/shard_map/ppermute | solution.py:63
  15.4 1.5 %copy-start = (bf16[1,2,2,16,6144]{4,3,2,1,0:T(8,128)(2,1)S(1)}, bf16[1,2,2,16,6144]{4,3,2,1,0:T(8,128)(2,1)}, u32[]{:S(2)}) copy-start(bf16[1,2,2,16,6144]{4,3,2,1,0:T(8,128)(2,1)} %weights.5) | copy-start | bytes 2359300
  15.4 1.6 %copy-start.1 = (bf16[1,2,64,6144]{3,2,1,0:T(8,128)(2,1)S(1)}, bf16[1,2,64,6144]{3,2,1,0:T(8,128)(2,1)}, u32[]{:S(2)}) copy-start(bf16[1,2,64,6144]{3,2,1,0:T(8,128)(2,1)} %acts.3) | copy-start | bytes 4718596
  15.5 20.1 %collective-permute-start = (bf16[64,6144]{1,0:T(8,128)(2,1)S(1)}, bf16[64,6144]{1,0:T(8,128)(2,1)S(1)}, u32[]{:S(2)}, u32[]{:S(2)}) collective-permute-start(bf16[64,6144]{1,0:T(8,128)(2,1)S(1)} %shard_map.96.down), channel_id=1, source_target_pairs={{16,0},{32,16},{48,32},{64,48},{80,64},{96,80},{144,128},{160,144}... | collective-permute-start | bytes 2359304 | tf_op jit(solution)/shard_map/ppermute | solution.py:63
  19.6 15.9 %collective-permute-start.5 = (f32[32,64]{1,0:T(8,128)S(1)}, f32[32,64]{1,0:T(8,128)S(1)}, u32[]{:S(2)}, u32[]{:S(2)}) collective-permute-start(f32[32,64]{1,0:T(8,128)S(1)} %shard_map.98._), channel_id=1, source_target_pairs={{112,128},{128,112},{240,256},{256,240},{368,384},{384,368},{496,0... | collective-permute-start | bytes 24584 | tf_op jit(solution)/shard_map/ppermute | solution.py:313
  28.3 7.2 %collective-permute-start.3 = (bf16[16,6144]{1,0:T(8,128)(2,1)S(1)}, bf16[16,6144]{1,0:T(8,128)(2,1)S(1)}, u32[]{:S(2)}, u32[]{:S(2)}) collective-permute-start(bf16[16,6144]{1,0:T(8,128)(2,1)S(1)} %shard_map.99._), channel_id=1, source_target_pairs={{112,96},{240,224},{368,352},{496,480},{113,97},{241,225},{369,353... | collective-permute-start | bytes 589832 | tf_op jit(solution)/shard_map/ppermute | solution.py:63
  42.5 34.4 %copy-start.2 = (f32[1,2,16,384]{3,2,1,0:T(8,128)S(1)}, f32[1,2,16,384]{3,2,1,0:T(8,128)}, u32[]{:S(2)}) copy-start(f32[1,2,16,384]{3,2,1,0:T(8,128)} %master.1) | copy-start | bytes 147460
  42.5 34.4 %copy-start.3 = (f32[1,2,16,384]{3,2,1,0:T(8,128)S(1)}, f32[1,2,16,384]{3,2,1,0:T(8,128)}, u32[]{:S(2)}) copy-start(f32[1,2,16,384]{3,2,1,0:T(8,128)} %moment.1) | copy-start | bytes 147460
  42.5 34.4 %copy-start.4 = (f32[1,2,16,384]{3,2,1,0:T(8,128)S(1)}, f32[1,2,16,384]{3,2,1,0:T(8,128)}, u32[]{:S(2)}) copy-start(f32[1,2,16,384]{3,2,1,0:T(8,128)} %second.1) | copy-start | bytes 147460
  53.7 6.1 %collective-permute-start.6 = (bf16[16,768]{1,0:T(8,128)(2,1)S(1)}, bf16[16,768]{1,0:T(8,128)(2,1)S(1)}, u32[]{:S(2)}, u32[]{:S(2)}) collective-permute-start(bf16[16,768]{1,0:T(8,128)(2,1)S(1)} %get-tuple-element.25), channel_id=1, source_target_pairs={{112,368},{368,112},{128,384},{384,128},{113,369},{369,113},{129,3... | collective-permute-start | bytes 73736 | tf_op jit(solution)/shard_map/ppermute | solution.py:328
  77.7 15.5 %all-to-all-start.2 = ((bf16[4,2,16,384]{3,2,1,0:T(8,128)(2,1)}), bf16[4,2,16,384]{3,2,1,0:T(8,128)(2,1)S(1)}, u32[]{:S(2)}, u32[]{:S(2)}) async-start(bf16[4,2,16,384]{3,2,1,0:T(8,128)(2,1)} %get-tuple-element.29), calls=%async_computation.2 | async-start | bytes 196608 | tf_op jit(solution)/shard_map/all_to_all | solution.py:337

commit v13 on v10

--- a/solution.py
+++ b/solution.py
@@ -104,6 +104,14 @@
 
 def columns(parts, at):
     return joined(*[part.at[:, at : at + 384] for part in parts])
+
+
+def copy_all(pairs, sems):
+    copies = [pltpu.make_async_copy(*pair, sems.at[i]) for i, pair in enumerate(pairs)]
+    for copy in copies:
+        copy.start()
+    for copy in copies:
+        copy.wait()
 
 
 def take_kernel(grads, weights, w_out, down, down_a, down_b, up, sems):
@@ -271,6 +279,10 @@
             shared[i, sec] = part
 
 
+def repeat_kernel(block, out, sems):
+    copy_all([(block, out.at[i]) for i in range(4)], sems)
+
+
 def finish_kernel(full, out, sem):
     upper = jnp.where(lax.axis_index("y") >= 2, 1, 0)
     copies = []
@@ -335,7 +347,11 @@
         here(far), here(master), here(moment), here(second),
     )
     shared = lax.all_to_all(shared, FAR, 0, 0, axis_index_groups=far_groups(), tiled=True)
-    copies = jnp.broadcast_to(shared[None], (4, *shared.shape))
+    (copies,) = call(
+        repeat_kernel,
+        [jax.ShapeDtypeStruct((4, *shared.shape), BF16)],
+        here(shared), scratch=[pltpu.SemaphoreType.DMA((4,))],
+    )
     full = both_cores(lax.all_to_all(copies, "x", 0, 0, tiled=True))
     (new_replicas,) = call(
         finish_kernel,

time: 112 us -> 112 us (level)
    pallas_call x9 -> x10, Pallas kernels: 4.99 us -> 5.76 us  [call(): pl.pallas_call(kernel, out_shape=[pltpu.VMEM(*out) if isinstance(out, tup...]
where the time goes in v13:
time: 112 us; the launch traced here: 111 us
  blocking collectives  56.8 us (51%)
  starting transfers between devices  31.1 us (28%)
  waiting for transfers between devices  14.9 us (13%)
  Pallas kernels  5.77 us (5%)
  local copies, waits for them, and re-layouts  2.07 us (2%)
    all_to_all x1, blocking collectives, body(): lax.all_to_all(spread, FAR, 0, 0, axis_index_groups=far_groups(), tiled=T...  17.1 us
    all_to_all x1, blocking collectives, body(): lax.all_to_all(shared, FAR, 0, 0, axis_index_groups=far_groups(), tiled=T...  15.3 us
    all_gather x2, blocking collectives, both_cores(): return lax.all_gather(block, 'c', axis=0, tiled=False)  13.4 us
    all_to_all x1, blocking collectives, body(): near = lax.all_to_all(tiles, 'x', 0, 0, tiled=True)  11 us
    ppermute x1, starting transfers between devices, body(): w_out_moved = lax.ppermute(w_out, FAR, weights_route())  8.71 us
    ppermute x1, starting transfers between devices, body(): wrapped = lax.ppermute(sent, SECTION, wrap_route())  8.61 us
    ppermute x1, waiting for transfers between devices, body(): wrapped = lax.ppermute(sent, SECTION, wrap_route())  6.54 us
    ppermute x4, starting transfers between devices, shifted(): return lax.ppermute(block, SECTION, route)  6.39 us
  transfers between devices with their start and end apart: 8, of which 5 were waited for; matrix products, arithmetic and copies ran while one was open for 2% of the time, Pallas kernels for 1%

profile of v13, /device:TPU:9, one launch (start us, length us, event | category | flops | bytes accessed | tf_op | source)
XLA Modules:
  0.0 111.4 jit_solution(1045459891278133102)
XLA Ops:
  0.6 1.7 %shard_map.93 = (bf16[16,6144]{1,0:T(8,128)(2,1)S(1)}, bf16[64,6144]{1,0:T(8,128)(2,1)S(1)}, bf16[48,6144]{1,0:T(8,128)(2,1)S(1)}, bf16[16,6144]{1,0:T(8,128)(2,1)S(1)}, bf16[64,6144]{1,0:T(8,128)(2,1)S(1)}) custom-call(bf16[1,2,64,6144]{3,2,1,0:T(8,128)(2,1)} %grads.1, bf16[1,2,2,16,6144]{4,3,2,1,0:T(8,128)(2,1)} %weights.5), custom_call_target="tpu_custom_call" | custom-call | tf_op jit(solution)/shard_map/pallas_call | solution.py:75
  2.4 3.6 %collective-permute-start.4 = (bf16[64,6144]{1,0:T(8,128)(2,1)S(1)}, bf16[64,6144]{1,0:T(8,128)(2,1)S(1)}, u32[]{:S(2)}, u32[]{:S(2)}) collective-permute-start(bf16[64,6144]{1,0:T(8,128)(2,1)S(1)} %get-tuple-element.17._.up), channel_id=1, source_target_pairs={{0,16},{16,32},{32,48},{48,64},{64,80},{80,96},{96,112},{128,144},... | collective-permute-start | bytes 2359304 | tf_op jit(solution)/shard_map/ppermute | solution.py:63
  6.0 8.7 %collective-permute-start.2 = (bf16[16,6144]{1,0:T(8,128)(2,1)S(1)}, bf16[16,6144]{1,0:T(8,128)(2,1)S(1)}, u32[]{:S(2)}, u32[]{:S(2)}) collective-permute-start(bf16[16,6144]{1,0:T(8,128)(2,1)S(1)} %shard_map.94._), channel_id=1, source_target_pairs={{112,136},{120,128},{128,120},{136,112},{240,264},{248,256},{256,2... | collective-permute-start | bytes 589832 | tf_op jit(solution)/shard_map/ppermute | solution.py:315
  14.7 0.7 collective-permute-start.1
  15.4 0.0 copy-start
  15.4 0.0 copy-start.1
  15.5 1.4 %collective-permute-start = (bf16[64,6144]{1,0:T(8,128)(2,1)S(1)}, bf16[64,6144]{1,0:T(8,128)(2,1)S(1)}, u32[]{:S(2)}, u32[]{:S(2)}) collective-permute-start(bf16[64,6144]{1,0:T(8,128)(2,1)S(1)} %shard_map.96.down), channel_id=1, source_target_pairs={{16,0},{32,16},{48,32},{64,48},{80,64},{96,80},{144,128},{160,144}... | collective-permute-start | bytes 2359304 | tf_op jit(solution)/shard_map/ppermute | solution.py:63
  16.9 0.0 copy-done
  16.9 0.2 copy-done.1
  17.1 0.5 shard_map.97.pre_act.value
  17.6 1.7 %collective-permute-done.2.w_out = bf16[16,6144]{1,0:T(8,128)(2,1)S(1)} collective-permute-done((bf16[16,6144]{1,0:T(8,128)(2,1)S(1)}, bf16[16,6144]{1,0:T(8,128)(2,1)S(1)}, u32[]{:S(2)}, u32[]{:S(2)}) %collective-permute-start.2) | collective-permute-done | bytes 196640 | tf_op jit(solution)/shard_map/ppermute | solution.py:315
  19.3 0.3 shard_map.98._
  19.6 8.6 %collective-permute-start.5 = (f32[32,64]{1,0:T(8,128)S(1)}, f32[32,64]{1,0:T(8,128)S(1)}, u32[]{:S(2)}, u32[]{:S(2)}) collective-permute-start(f32[32,64]{1,0:T(8,128)S(1)} %shard_map.98._), channel_id=1, source_target_pairs={{112,128},{128,112},{240,256},{256,240},{368,384},{384,368},{496,0... | collective-permute-start | bytes 24584 | tf_op jit(solution)/shard_map/ppermute | solution.py:325
  28.3 0.7 collective-permute-start.3
  28.9 6.5 %collective-permute-done.5.wrapped = f32[32,64]{1,0:T(8,128)S(1)} collective-permute-done((f32[32,64]{1,0:T(8,128)S(1)}, f32[32,64]{1,0:T(8,128)S(1)}, u32[]{:S(2)}, u32[]{:S(2)}) %collective-permute-start.5) | collective-permute-done | bytes 8224 | tf_op jit(solution)/shard_map/ppermute | solution.py:325
  35.5 0.0 collective-permute-done.3.after_b
  35.5 0.0 collective-permute-done.1.after_a
  35.5 0.1 collective-permute-done.from_after
  35.6 0.0 collective-permute-done.4.from_before
  35.6 1.4 %shard_map.101 = (f32[4,64,768]{2,1,0:T(8,128)S(1)}, bf16[4,64,768]{2,1,0:T(8,128)(2,1)S(1)}) custom-call(bf16[64,6144]{1,0:T(8,128)(2,1)S(1)} %collective-permute-done.from_after, bf16[48,6144]{1,0:T(8,128)(2,1)S(1)} %collective-permute-done.1.after_a, bf16[16,6144]{1,0:T(8,128)(2,1)S(1)} %collective-permute-done.3.after_b, ...), custom_call_target="tpu_custom_call" | custom-call | tf_op jit(solution)/shard_map/pallas_call | solution.py:75
  37.0 5.5 %all-gather = bf16[8,64,768]{2,1,0:T(8,128)(2,1)S(1)} all-gather(bf16[4,64,768]{2,1,0:T(8,128)(2,1)S(1)} %get-tuple-element.23), channel_id=2, replica_groups=mesh['y'=4,'zl'=8,'zh'=2,'x'=4,'c'=2] {'c'}, dimensions={0}, use_global_device_ids=true | all-gather | bytes 1179648 | tf_op jit(solution)/shard_map/all_gather | solution.py:67
  42.5 0.0 copy-start.2
  42.5 0.0 copy-start.3
  42.5 0.0 copy-start.4
  42.5 0.1 shard_map.102
  42.6 11.0 %all_to_all.20.arrived = bf16[4,64,768]{2,1,0:T(8,128)(2,1)S(1)} all-to-all(bf16[4,64,768]{2,1,0:T(8,128)(2,1)S(1)} %shard_map.102), channel_id=1, replica_groups=mesh['y'=4,'zl'=8,'zh'=2,'x'=4,'c'=2] {'x'}, dimensions={0} | all-to-all | bytes 786432 | tf_op jit(solution)/shard_map/all_to_all | solution.py:338
  53.6 0.1 shard_map.103
  53.7 3.9 %collective-permute-start.6 = (bf16[16,768]{1,0:T(8,128)(2,1)S(1)}, bf16[16,768]{1,0:T(8,128)(2,1)S(1)}, u32[]{:S(2)}, u32[]{:S(2)}) collective-permute-start(bf16[16,768]{1,0:T(8,128)(2,1)S(1)} %get-tuple-element.25), channel_id=1, source_target_pairs={{112,368},{368,112},{128,384},{384,128},{113,369},{369,113},{129,3... | collective-permute-start | bytes 73736 | tf_op jit(solution)/shard_map/ppermute | solution.py:340
  57.6 2.1 %collective-permute-done.6.swap = bf16[16,768]{1,0:T(8,128)(2,1)S(1)} collective-permute-done((bf16[16,768]{1,0:T(8,128)(2,1)S(1)}, bf16[16,768]{1,0:T(8,128)(2,1)S(1)}, u32[]{:S(2)}, u32[]{:S(2)}) %collective-permute-start.6) | collective-permute-done | bytes 24608 | tf_op jit(solution)/shard_map/ppermute | solution.py:340
  59.8 17.1 %all_to_all.21.arrived = bf16[4,2,16,384]{3,2,1,0:T(8,128)(2,1)S(1)} all-to-all(bf16[4,2,16,384]{3,2,1,0:T(8,128)(2,1)S(1)} %shard_map.104), channel_id=1, replica_groups={{0,8,496,504},{16,24,480,488},{32,40,464,472},{48,56,448,456},{64,72,43..., dimensions={0} | all-to-all | bytes 196608 | tf_op jit(solution)/shard_map/all_to_all | solution.py:342
  76.9 0.0 copy-done.2
  76.9 0.0 copy-done.3
  76.9 0.0 copy-done.4
  76.9 0.1 shard_map.105
  77.0 15.3 %all_to_all.22.block = bf16[4,2,16,384]{3,2,1,0:T(8,128)(2,1)S(1)} all-to-all(bf16[4,2,16,384]{3,2,1,0:T(8,128)(2,1)S(1)} %get-tuple-element.29), channel_id=1, replica_groups={{0,8,496,504},{16,24,480,488},{32,40,464,472},{48,56,448,456},{64,72,43..., dimensions={0} | all-to-all | bytes 196608 | tf_op jit(solution)/shard_map/all_to_all | solution.py:349
  92.3 0.8 shard_map.106
  93.0 3.5 %all-to-all-start.3 = ((bf16[4,4,2,16,384]{4,3,2,1,0:T(8,128)(2,1)}), bf16[4,4,2,16,384]{4,3,2,1,0:T(8,128)(2,1)S(1)}, u32[]{:S(2)}, u32[]{:S(2)}) async-start(bf16[4,4,2,16,384]{4,3,2,1,0:T(8,128)(2,1)} %shard_map.106), calls=%async_computation.3 | async-start | bytes 786432 | tf_op jit(solution)/shard_map/all_to_all | solution.py:355
  96.5 0.6 copy.20
  97.2 0.6 copy.21
  97.8 0.6 copy.22
  98.4 4.3 %all-to-all-done.3 = bf16[4,4,2,16,384]{4,3,2,1,0:T(8,128)(2,1)S(1)} async-done(((bf16[4,4,2,16,384]{4,3,2,1,0:T(8,128)(2,1)}), bf16[4,4,2,16,384]{4,3,2,1,0:T(8,128)(2,1)S(1)}, u32[]{:S(2)}, u32[]{:S(2)}) %all-to-all-start.3) | async-done | bytes 393248 | tf_op jit(solution)/shard_map/all_to_all | solution.py:355
  102.7 7.8 %all-gather.1 = bf16[8,4,2,16,384]{4,3,2,1,0:T(8,128)(2,1)S(1)} all-gather(bf16[4,4,2,16,384]{4,3,2,1,0:T(8,128)(2,1)S(1)} %all-to-all-done.3), channel_id=3, replica_groups=mesh['y'=4,'zl'=8,'zh'=2,'x'=4,'c'=2] {'c'}, dimensions={0}, use_global_device_ids=true | all-gather | bytes 1179648 | tf_op jit(solution)/shard_map/all_gather | solution.py:67
  110.5 0.8 shard_map.107
  (6 shorter events, 0.0 us)
Async XLA Ops:
  2.4 33.2 %collective-permute-start.4 = (bf16[64,6144]{1,0:T(8,128)(2,1)S(1)}, bf16[64,6144]{1,0:T(8,128)(2,1)S(1)}, u32[]{:S(2)}, u32[]{:S(2)}) collective-permute-start(bf16[64,6144]{1,0:T(8,128)(2,1)S(1)} %get-tuple-element.17._.up), channel_id=1, source_target_pairs={{0,16},{16,32},{32,48},{48,64},{64,80},{80,96},{96,112},{128,144},... | collective-permute-start | bytes 2359304 | tf_op jit(solution)/shard_map/ppermute | solution.py:63
  6.0 13.3 %collective-permute-start.2 = (bf16[16,6144]{1,0:T(8,128)(2,1)S(1)}, bf16[16,6144]{1,0:T(8,128)(2,1)S(1)}, u32[]{:S(2)}, u32[]{:S(2)}) collective-permute-start(bf16[16,6144]{1,0:T(8,128)(2,1)S(1)} %shard_map.94._), channel_id=1, source_target_pairs={{112,136},{120,128},{128,120},{136,112},{240,264},{248,256},{256,2... | collective-permute-start | bytes 589832 | tf_op jit(solution)/shard_map/ppermute | solution.py:315
  14.7 20.8 %collective-permute-start.1 = (bf16[48,6144]{1,0:T(8,128)(2,1)S(1)}, bf16[48,6144]{1,0:T(8,128)(2,1)S(1)}, u32[]{:S(2)}, u32[]{:S(2)}) collective-permute-start(bf16[48,6144]{1,0:T(8,128)(2,1)S(1)} %shard_map.95._), channel_id=1, source_target_pairs={{112,96},{240,224},{368,352},{496,480},{113,97},{241,225},{369,353... | collective-permute-start | bytes 1769480 | tf_op jit(solution)/shard_map/ppermute | solution.py:63
  15.4 1.5 %copy-start = (bf16[1,2,2,16,6144]{4,3,2,1,0:T(8,128)(2,1)S(1)}, bf16[1,2,2,16,6144]{4,3,2,1,0:T(8,128)(2,1)}, u32[]{:S(2)}) copy-start(bf16[1,2,2,16,6144]{4,3,2,1,0:T(8,128)(2,1)} %weights.5) | copy-start | bytes 2359300
  15.4 1.6 %copy-start.1 = (bf16[1,2,64,6144]{3,2,1,0:T(8,128)(2,1)S(1)}, bf16[1,2,64,6144]{3,2,1,0:T(8,128)(2,1)}, u32[]{:S(2)}) copy-start(bf16[1,2,64,6144]{3,2,1,0:T(8,128)(2,1)} %acts.3) | copy-start | bytes 4718596
  15.5 20.1 %collective-permute-start = (bf16[64,6144]{1,0:T(8,128)(2,1)S(1)}, bf16[64,6144]{1,0:T(8,128)(2,1)S(1)}, u32[]{:S(2)}, u32[]{:S(2)}) collective-permute-start(bf16[64,6144]{1,0:T(8,128)(2,1)S(1)} %shard_map.96.down), channel_id=1, source_target_pairs={{16,0},{32,16},{48,32},{64,48},{80,64},{96,80},{144,128},{160,144}... | collective-permute-start | bytes 2359304 | tf_op jit(solution)/shard_map/ppermute | solution.py:63
  19.6 15.9 %collective-permute-start.5 = (f32[32,64]{1,0:T(8,128)S(1)}, f32[32,64]{1,0:T(8,128)S(1)}, u32[]{:S(2)}, u32[]{:S(2)}) collective-permute-start(f32[32,64]{1,0:T(8,128)S(1)} %shard_map.98._), channel_id=1, source_target_pairs={{112,128},{128,112},{240,256},{256,240},{368,384},{384,368},{496,0... | collective-permute-start | bytes 24584 | tf_op jit(solution)/shard_map/ppermute | solution.py:325
  28.3 7.2 %collective-permute-start.3 = (bf16[16,6144]{1,0:T(8,128)(2,1)S(1)}, bf16[16,6144]{1,0:T(8,128)(2,1)S(1)}, u32[]{:S(2)}, u32[]{:S(2)}) collective-permute-start(bf16[16,6144]{1,0:T(8,128)(2,1)S(1)} %shard_map.99._), channel_id=1, source_target_pairs={{112,96},{240,224},{368,352},{496,480},{113,97},{241,225},{369,353... | collective-permute-start | bytes 589832 | tf_op jit(solution)/shard_map/ppermute | solution.py:63
  42.5 34.4 %copy-start.2 = (f32[1,2,16,384]{3,2,1,0:T(8,128)S(1)}, f32[1,2,16,384]{3,2,1,0:T(8,128)}, u32[]{:S(2)}) copy-start(f32[1,2,16,384]{3,2,1,0:T(8,128)} %master.1) | copy-start | bytes 147460
  42.5 34.4 %copy-start.3 = (f32[1,2,16,384]{3,2,1,0:T(8,128)S(1)}, f32[1,2,16,384]{3,2,1,0:T(8,128)}, u32[]{:S(2)}) copy-start(f32[1,2,16,384]{3,2,1,0:T(8,128)} %moment.1) | copy-start | bytes 147460
  42.5 34.4 %copy-start.4 = (f32[1,2,16,384]{3,2,1,0:T(8,128)S(1)}, f32[1,2,16,384]{3,2,1,0:T(8,128)}, u32[]{:S(2)}) copy-start(f32[1,2,16,384]{3,2,1,0:T(8,128)} %second.1) | copy-start | bytes 147460
  53.7 6.1 %collective-permute-start.6 = (bf16[16,768]{1,0:T(8,128)(2,1)S(1)}, bf16[16,768]{1,0:T(8,128)(2,1)S(1)}, u32[]{:S(2)}, u32[]{:S(2)}) collective-permute-start(bf16[16,768]{1,0:T(8,128)(2,1)S(1)} %get-tuple-element.25), channel_id=1, source_target_pairs={{112,368},{368,112},{128,384},{384,128},{113,369},{369,113},{129,3... | collective-permute-start | bytes 73736 | tf_op jit(solution)/shard_map/ppermute | solution.py:340
  93.0 9.7 %all-to-all-start.3 = ((bf16[4,4,2,16,384]{4,3,2,1,0:T(8,128)(2,1)}), bf16[4,4,2,16,384]{4,3,2,1,0:T(8,128)(2,1)S(1)}, u32[]{:S(2)}, u32[]{:S(2)}) async-start(bf16[4,4,2,16,384]{4,3,2,1,0:T(8,128)(2,1)} %shard_map.106), calls=%async_computation.3 | async-start | bytes 786432 | tf_op jit(solution)/shard_map/all_to_all | solution.py:355
